TPU v7x, 256 devices: a whole 4x4x8 slice. The times are simulated.
256 devices in a mesh: grid: 4 (over y), gx: 8 (over x, core), gy: 8 (over z).
Axes of the slice: x: 4, y: 4, z: 8, core: 2. Of those that a mesh axis runs over, the one named last changes fastest.
Arguments:
- deck_fields: float32 [3, 32, 512, 384], P(None, None, ('grid', 'gx', 'gy')), may hold values from -6 to 6
- back_fields: float32 [3, 32, 512, 1024], P(None, None, ('grid', 'gx'), 'gy'), may hold values from -6 to 6
- metrics: float32 [4, 512, 384], P(None, ('grid', 'gx', 'gy'))
- donors: int32 [256, 512, 1], P(('grid', 'gx', 'gy')), may hold values from 0 to 63; in each aligned block of 512 rows (0 to 511, 512 to 1023, ..., all dimensions but the last counted through in order) at most 16 rows name the same one
- stencil: int32 [256, 512, 4], P(('grid', 'gx', 'gy')), may hold values from 0 to 382, as said below
- fringe_cells: int32 [256, 508], P(('grid', 'gx', 'gy')), may hold values from 0 to 2047, as said below
Outputs:
- deck_final: float32 [3, 32, 512, 384], P(None, None, ('grid', 'gx', 'gy'))
- back_final: float32 [3, 32, 512, 1024], P(None, None, ('grid', 'gx'), 'gy')
Inputs may be any that keep to these rules, and one draw needn't show every extreme that they name: `donors`: at most 16 rows of one tile name the same donor, and some tile's rows reach that in every draw. `stencil`: the first 4 rows of each tile have base row below 15 and base column below 127, the others base row below 1 and base column below 383; fractions 0 to 16. `fringe_cells`: distinct within a tile; the block's last cell is always among them.
All inputs are finite; a program needn't handle non-finite values.
Results may differ from a plain program's by a relative error of at most 0.0001.
Values sent between devices are 32-bit elements; how exact they have to be, the bound alone decides.
No kernel may reach another device: no remote copies, remote signals or barrier semaphores. Data moves between devices by JAX's collectives and lax.ppermute only.
A program may use at most 64 MiB of HBM per device.

v0:
```python
import functools

import jax
import jax.numpy as jnp
from jax import lax
from jax.experimental import pallas as pl
from jax.experimental.pallas import tpu as pltpu
from jax.sharding import PartitionSpec as P

SPAN = 32
PLANES = 96
MEMBERS = 64
CAP = 16
SLOTS = MEMBERS * CAP
ROWS = 16
COLS = 128
DROWS = 2
DCOLS = 384
FRINGE = 512
NEAR = 4
TIME_STEP = 0.05
SMAGORINSKY = 0.02
F32 = jnp.float32
BF16 = jnp.bfloat16
NT = (((1,), (1,)), ((), ()))
NN = (((1,), (0,)), ((), ()))
VMEM_LIMIT = 24 * 1024 * 1024
PACKED = CAP * PLANES
R_ROW, R_COL, R_FX, R_FY, R_GRID = range(5)


def position():
    column = lax.axis_index("gy")
    line = lax.axis_index("grid") * lax.axis_size("gx") + lax.axis_index("gx")
    tile = line * lax.axis_size("gy") + column
    return column, line, tile


def dot(a, b, dims):
    return lax.dot_general(a, b, dims, preferred_element_type=F32)


def iota(shape, dim):
    return lax.broadcasted_iota(jnp.int32, shape, dim)


def call(kernel, outs, ins, scratch=(), hbm_at=(), name=None):
    def spec(i):
        return pl.BlockSpec(memory_space=pltpu.HBM if i in hbm_at else pltpu.VMEM)

    return pl.pallas_call(
        kernel,
        out_shape=tuple(jax.ShapeDtypeStruct(s, d) for s, d in outs),
        in_specs=[spec(i) for i in range(len(ins))],
        out_specs=tuple(pl.BlockSpec(memory_space=pltpu.VMEM) for _ in outs),
        scratch_shapes=list(scratch),
        compiler_params=pltpu.CompilerParams(vmem_limit_bytes=VMEM_LIMIT),
        name=name,
    )(*ins)


def route_kernel(
    donors_hbm, stencil_hbm, cells_hbm, request_ref, fill_ref, rim_ref, near_ref, keep_ref,
    donors_ref, stencil_ref, cells_ref, local_ref, sems,
):
    pairs = [(donors_hbm, donors_ref), (stencil_hbm, stencil_ref), (cells_hbm, cells_ref)]
    copies = [pltpu.make_async_copy(a, b, sems.at[i]) for i, (a, b) in enumerate(pairs)]
    for c in copies:
        c.start()
    for c in copies:
        c.wait()
    donors = donors_ref[...]
    member = (iota((MEMBERS, FRINGE), 0) == donors).astype(F32)
    before = (iota((FRINGE, FRINGE), 0) < iota((FRINGE, FRINGE), 1)).astype(BF16)
    member_b = member.astype(BF16)
    earlier = dot(member_b, before, NN)
    rank = jnp.sum(member * earlier, axis=0, keepdims=True).astype(jnp.int32)
    at_rank = (iota((CAP, FRINGE), 0) == rank).astype(F32)

    def place(values):
        stacked = jnp.concatenate([at_rank * v.astype(F32) for v in values], axis=0)
        return dot(member_b, stacked.astype(BF16), NT)

    row = stencil_ref[0:1, :]
    col = stencil_ref[1:2, :]
    lane = iota((1, FRINGE), 1)
    grid = jnp.where(lane < NEAR, 1, 2)
    half = col >> 1
    sent = place([row, half, col - 2 * half, stencil_ref[2:3, :], stencil_ref[3:4, :], grid])
    request_ref[:, 0, :] = jnp.zeros((MEMBERS, 128), F32)
    request_ref[:, 0, 0:16] = sent[:, 0:16]
    request_ref[:, 0, 16:32] = 2.0 * sent[:, 16:32] + sent[:, 32:48]
    request_ref[:, 0, 32:80] = sent[:, 48:96]
    cells = jnp.concatenate([jnp.zeros((1, NEAR), jnp.int32), cells_ref[...]], axis=1)
    far = lane >= NEAR
    local_ref[...] = place(
        [
            jnp.where(far, (cells >> 7) + 1, 0),
            jnp.where(far, cells & 127, 0),
            jnp.where(far, 0, lane + 1),
        ]
    )
    landing(local_ref, fill_ref, rim_ref, near_ref, keep_ref)


def landing(local_ref, fill_ref, rim_ref, near_ref, keep_ref):
    lane = iota((MEMBERS, COLS), 1)
    places = local_ref[...].astype(jnp.int32)
    listed = [jnp.zeros((8, COLS), F32) for _ in range(ROWS + 1)]

    def over_eight(x):
        return jnp.sum(x.reshape(MEMBERS // 8, 8, COLS), axis=0)

    for s in range(CAP):
        at = slice(s * MEMBERS, (s + 1) * MEMBERS)
        row = jnp.broadcast_to(places[:, s : s + 1] - 1, (MEMBERS, COLS))
        col = jnp.broadcast_to(places[:, CAP + s : CAP + s + 1], (MEMBERS, COLS))
        hit = jnp.where(lane == col, 1.0, 0.0)
        for r in range(ROWS):
            here = jnp.where(row == r, hit, 0.0)
            fill_ref[at, r * COLS : (r + 1) * COLS] = here.astype(BF16)
            listed[r] = listed[r] + over_eight(here)
            if r == 0:
                rim_ref[at, 0:COLS] = here.astype(BF16)
            if r == ROWS - 1:
                rim_ref[at, COLS : 2 * COLS] = here.astype(BF16)
        side = jnp.where(col == 0, row, jnp.where(col == COLS - 1, row + ROWS, -1))
        here = jnp.where((lane == side) & (row >= 0), 1.0, 0.0)
        rim_ref[at, 2 * COLS : 3 * COLS] = here.astype(BF16)
        listed[ROWS] = listed[ROWS] + over_eight(here)
        if s < NEAR:
            near = places[:, 2 * CAP + s : 2 * CAP + s + 1] - 1
            place = jnp.where(near >= 0, (near >> 1) * COLS + COLS - 2 + (near & 1), -1)
            place = jnp.broadcast_to(place, (MEMBERS, COLS))
            for r in range(DROWS):
                near_ref[at, r * COLS : (r + 1) * COLS] = jnp.where(lane + r * COLS == place, 1.0, 0.0).astype(BF16)
    for r in range(ROWS + 1):
        keep_ref[r] = 1.0 - jnp.broadcast_to(jnp.sum(listed[r], axis=0, keepdims=True), (8, COLS))


def split(x):
    high = x.astype(BF16)
    return high, (x - high.astype(F32)).astype(BF16)


def weights(request_ref, rows_ref, far_ref, near_ref):
    rows_ref[...] = request_ref[:, 0, :]
    request = rows_ref[...]
    whole = request.astype(jnp.int32)
    lane = iota((MEMBERS, COLS), 1)

    def wide(x, f, s):
        at = f * CAP + s
        return jnp.broadcast_to(x[:, at : at + 1], (MEMBERS, COLS))

    for s in range(CAP):
        at = slice(s * MEMBERS, (s + 1) * MEMBERS)
        col = wide(whole, R_COL, s)
        fx = wide(request, R_FX, s) * (1.0 / 16.0)
        fy = wide(request, R_FY, s) * (1.0 / 16.0)
        grid = wide(request, R_GRID, s)
        on_deck = jnp.where(grid == 2.0, 1.0, 0.0)
        first, second = on_deck * (1.0 - fx), on_deck * fx
        share = [first * (1.0 - fy), first * fy, second * (1.0 - fy), second * fy]
        for t in range(DCOLS // COLS):
            low, high = lane + t * COLS == col, lane + t * COLS == col + 1
            for r in range(DROWS):
                here = jnp.where(low, share[2 * r], jnp.where(high, share[2 * r + 1], 0.0))
                start = r * DCOLS + t * COLS
                far_ref[at, start : start + COLS] = here.astype(BF16)
        if s < NEAR:
            row = wide(whole, R_ROW, s)
            on_back = jnp.where(grid == 1.0, 1.0, 0.0)
            across = jnp.where(lane == col, on_back * (1.0 - fy), jnp.where(lane == col + 1, on_back * fy, 0.0))
            first, second = (1.0 - fx) * across, fx * across
            for r in range(ROWS):
                here = jnp.where(row == r, first, jnp.where(row + 1 == r, second, 0.0))
                near_ref[at, r * COLS : (r + 1) * COLS] = here.astype(BF16)


def stack_deck(pieces, r, value):
    high, low = split(value)
    pieces[0:PLANES, r * DCOLS : (r + 1) * DCOLS] = high
    pieces[128 : 128 + PLANES, r * DCOLS : (r + 1) * DCOLS] = low


def stack_back(pieces, r, value):
    high, low = split(value)
    pieces[0:PLANES, r * COLS : (r + 1) * COLS] = high
    pieces[128 : 128 + PLANES, r * COLS : (r + 1) * COLS] = low


def clear_pieces(deck_pieces, back_pieces):
    for pieces in (deck_pieces, back_pieces):
        gap = jnp.zeros((128 - PLANES, pieces.shape[1]), BF16)
        pieces[PLANES:128, :] = gap
        pieces[128 + PLANES : 256, :] = gap


def answer(far_ref, near_ref, deck_pieces, back_pieces, out_ref):
    lane = iota((MEMBERS, 128), 1)
    for q in range(CAP // 4):
        got = dot(far_ref[q * 256 : (q + 1) * 256, :], deck_pieces[...], NT)
        if q == 0:
            got = got + dot(near_ref[...], back_pieces[...], NT)
        got = got[:, 0:128] + got[:, 128:256]
        a = [got[i * MEMBERS : (i + 1) * MEMBERS, :] for i in range(4)]
        base = q * 4 * PLANES
        out_ref[:, 0, base : base + 128] = jnp.where(lane < 96, a[0], pltpu.roll(a[1], 96, 1))
        out_ref[:, 0, base + 128 : base + 256] = jnp.where(
            lane < 64, pltpu.roll(a[1], 96, 1), pltpu.roll(a[2], 64, 1)
        )
        out_ref[:, 0, base + 256 : base + 384] = jnp.where(
            lane < 32, pltpu.roll(a[2], 64, 1), pltpu.roll(a[3], 32, 1)
        )


def first_answer_kernel(
    request_ref, deck_hbm, back_hbm, deck_out, back_out, far_ref, near_ref, out_ref,
    rows_ref, deck_pieces, back_pieces, deck_ref, back_ref, sems,
):
    copies = [
        pltpu.make_async_copy(deck_hbm, deck_ref, sems.at[0]),
        pltpu.make_async_copy(back_hbm, back_ref, sems.at[1]),
    ]
    for c in copies:
        c.start()
    clear_pieces(deck_pieces, back_pieces)
    weights(request_ref, rows_ref, far_ref, near_ref)
    for c in copies:
        c.wait()
    for r in range(DROWS):
        value = deck_ref[:, r, :]
        deck_out[r] = value
        stack_deck(deck_pieces, r, value)
    for r in range(ROWS):
        value = back_ref[:, r, :]
        back_out[r] = value
        stack_back(back_pieces, r, value)
    answer(far_ref, near_ref, deck_pieces, back_pieces, out_ref)


def rim_kernel(
    got_ref, rim_ref, near_ref, keep_ref, deck_ref, back_ref,
    got_pieces, deck_out, column_first, column_second, row_first, row_second,
):
    lane = iota((MEMBERS, 128), 1)
    for q in range(CAP // 4):
        base = q * 4 * PLANES
        c0 = got_ref[:, 0, base : base + 128]
        c1 = got_ref[:, 0, base + 128 : base + 256]
        c2 = got_ref[:, 0, base + 256 : base + 384]
        a0 = jnp.where(lane < 96, c0, 0.0)
        a1 = jnp.where(lane < 32, pltpu.roll(c0, 32, 1), jnp.where(lane < 96, pltpu.roll(c1, 32, 1), 0.0))
        a2 = jnp.where(lane < 64, pltpu.roll(c1, 64, 1), jnp.where(lane < 96, pltpu.roll(c2, 64, 1), 0.0))
        a3 = jnp.where(lane < 96, pltpu.roll(c2, 96, 1), 0.0)
        across = jnp.concatenate([a0, a1, a2, a3], axis=0).T
        high, low = split(across[0:PLANES, :])
        got_pieces[0:PLANES, q * 256 : (q + 1) * 256] = high
        got_pieces[PLANES : 2 * PLANES, q * 256 : (q + 1) * 256] = low
    near = dot(got_pieces[:, 0:256], near_ref[...], NN)
    near = near[0:PLANES] + near[PLANES : 2 * PLANES]
    lane = iota((PLANES, 128), 1)
    column, line, tile = position()
    odd = lax.rem(tile, 2) > 0
    odd_line = lax.rem(line, 2) > 0
    deck = []
    for r in range(DROWS):
        outer = jnp.where(lane >= 126, near[:, r * 128 : (r + 1) * 128], deck_ref[r, :, 256:384])
        deck.append(jnp.concatenate([deck_ref[r, :, 0:256], outer], axis=1))
        deck_out[r] = deck[r]
    row_first[:, 0:DCOLS] = jnp.where(odd, deck[0], deck[1])
    row_second[:, 0:DCOLS] = jnp.where(odd, deck[1], deck[0])
    rim = dot(got_pieces[...], rim_ref[...], NN)
    rim = rim[0:PLANES] + rim[PLANES : 2 * PLANES]
    north = back_ref[0] * keep_ref[0, 0:1, :] + rim[:, 0:COLS]
    south = back_ref[ROWS - 1] * keep_ref[ROWS - 1, 0:1, :] + rim[:, COLS : 2 * COLS]
    column_first[...] = jnp.where(odd_line, north, south)
    column_second[...] = jnp.where(odd_line, south, north)
    ends = jnp.zeros((PLANES, COLS), F32)
    for r in range(ROWS):
        ends = jnp.where(lane == r, back_ref[r, :, 0:1], ends)
        ends = jnp.where(lane == ROWS + r, back_ref[r, :, COLS - 1 : COLS], ends)
    ends = ends * keep_ref[ROWS, 0:1, :] + rim[:, 2 * COLS : 3 * COLS]
    row_first[:, DCOLS : DCOLS + COLS] = ends
    row_second[:, DCOLS : DCOLS + COLS] = ends


def fill_kernel(got_pieces, fill_ref, keep_ref, back_ref, back_out):
    for c in range(ROWS // 2):
        new = dot(got_pieces[...], fill_ref[:, c * 256 : (c + 1) * 256], NN)
        new = new[0:PLANES] + new[PLANES : 2 * PLANES]
        for half in range(2):
            r = 2 * c + half
            back_out[r] = back_ref[r] * keep_ref[r, 0:1, :] + new[:, half * 128 : (half + 1) * 128]


def update(here, minus_xi, plus_xi, minus_eta, plus_eta, metric, keep, base, section):
    d_xi, d_eta, d_span, lap = [], [], [], []
    strain = None
    for c in range(3):
        f = here[c]
        plus_span = jnp.concatenate([f[1:], f[:1]], axis=0)
        minus_span = jnp.concatenate([f[-1:], f[:-1]], axis=0)
        a = plus_xi[c] - minus_xi[c]
        b = plus_eta[c] - minus_eta[c]
        s = plus_span - minus_span
        square = a * a + b * b + s * s
        strain = square if strain is None else strain + square
        doubled = 2.0 * f
        l_xi = plus_xi[c] - doubled + minus_xi[c]
        l_eta = plus_eta[c] - doubled + minus_eta[c]
        if metric is not None:
            l_xi, l_eta = metric[4] * l_xi, metric[5] * l_eta
        lap.append(l_xi + l_eta + (plus_span - doubled + minus_span))
        d_xi.append(a)
        d_eta.append(b)
        d_span.append(s)
    viscosity = SMAGORINSKY * jnp.sqrt(1.0 + 0.25 * strain)
    if metric is None:
        speed_xi, speed_eta = here[0], here[1]
    else:
        speed_xi = metric[0] * here[0] + metric[1] * here[1]
        speed_eta = metric[2] * here[0] + metric[3] * here[1]
    out = []
    for c in range(3):
        advection = 0.5 * (speed_xi * d_xi[c] + speed_eta * d_eta[c] + here[2] * d_span[c])
        tendency = viscosity * lap[c] - advection
        if section == 0:
            out.append(here[c] + (TIME_STEP * keep) * tendency)
        elif section == 1:
            out.append(0.75 * base[c] + 0.25 * here[c] + (0.25 * TIME_STEP * keep) * tendency)
        else:
            out.append(base[c] * (1.0 / 3.0) + (2.0 / 3.0) * here[c] + (2.0 / 3.0 * TIME_STEP * keep) * tendency)
    return out


def fields(ref, at):
    return [ref[at + (slice(c * SPAN, (c + 1) * SPAN), slice(None))] for c in range(3)]


def section_kernel(section, *refs):
    refs = list(refs)
    deck_ref, back_ref, column_first, column_second, row_first, row_second, metric_ref, keep_ref = refs[:8]
    del refs[:8]
    base_deck = base_back = None
    if section > 0:
        base_deck, base_back = refs[:2]
        del refs[:2]
    last = section == 2
    if last:
        deck_out, back_out = refs
    else:
        far_ref, near_ref, deck_out, back_out, answer_out, deck_pieces, back_pieces = refs
        clear_pieces(deck_pieces, back_pieces)
    column, line, tile = position()
    odd = lax.rem(tile, 2) > 0
    odd_line = lax.rem(line, 2) > 0
    west_end = (column > 0).astype(F32)
    east_end = (column < lax.axis_size("gy") - 1).astype(F32)

    def ordered(flag, first, second, at):
        a, b = first[at], second[at]
        return jnp.where(flag, a, b), jnp.where(flag, b, a)

    spans = [slice(c * SPAN, (c + 1) * SPAN) for c in range(3)]
    across = [ordered(odd, row_first, row_second, (at, slice(0, DCOLS))) for at in spans]
    beside = [ordered(odd, row_first, row_second, (at, slice(DCOLS, DCOLS + COLS))) for at in spans]
    along = [ordered(odd_line, column_first, column_second, (at, slice(None))) for at in spans]
    lane = iota((SPAN, DCOLS), 1)
    keep_deck = jnp.where(iota((1, DCOLS), 1) < DCOLS - 2, 1.0, 0.0)
    for r in range(DROWS):
        here = fields(deck_ref, (r,))
        if r == 0:
            minus = [a[0] for a in across]
            plus = fields(deck_ref, (1,))
        else:
            minus = fields(deck_ref, (0,))
            plus = [a[1] for a in across]
        m = [metric_ref[i, r : r + 1, :] for i in range(4)]
        metric = m + [m[0] * m[0] + m[1] * m[1], m[2] * m[2] + m[3] * m[3]]
        plus_eta = [jnp.where(lane == DCOLS - 1, 0.0, pltpu.roll(f, DCOLS - 1, 1)) for f in here]
        minus_eta = [jnp.where(lane == 0, 0.0, pltpu.roll(f, 1, 1)) for f in here]
        base = fields(base_deck, (r,)) if section > 0 else None
        new = update(here, minus, plus, minus_eta, plus_eta, metric, keep_deck, base, section)
        for c in range(3):
            if last:
                deck_out[c * SPAN : (c + 1) * SPAN, r, :] = new[c]
            else:
                deck_out[r, c * SPAN : (c + 1) * SPAN, :] = new[c]
        if not last:
            stack_deck(deck_pieces, r, jnp.concatenate(new, axis=0))
    lane = iota((SPAN, COLS), 1)
    for r in range(ROWS):
        here = fields(back_ref, (r,))
        minus = fields(back_ref, (r - 1,)) if r > 0 else [a[0] for a in along]
        plus = fields(back_ref, (r + 1,)) if r < ROWS - 1 else [a[1] for a in along]
        plus_eta, minus_eta = [], []
        for c in range(3):
            from_west = beside[c][0][:, ROWS + r : ROWS + r + 1] * west_end
            from_east = beside[c][1][:, r : r + 1] * east_end
            plus_eta.append(jnp.where(lane == COLS - 1, from_east, pltpu.roll(here[c], COLS - 1, 1)))
            minus_eta.append(jnp.where(lane == 0, from_west, pltpu.roll(here[c], 1, 1)))
        base = fields(base_back, (r,)) if section > 0 else None
        new = update(here, minus, plus, minus_eta, plus_eta, None, keep_ref[r, 0:1, :], base, section)
        for c in range(3):
            if last:
                back_out[c * SPAN : (c + 1) * SPAN, r, :] = new[c]
            else:
                back_out[r, c * SPAN : (c + 1) * SPAN, :] = new[c]
        if not last:
            stack_back(back_pieces, r, jnp.concatenate(new, axis=0))
    if not last:
        answer(far_ref, near_ref, deck_pieces, back_pieces, answer_out)


def local(deck_fields, back_fields, metrics, donors, stencil, fringe_cells):
    group = ("gx", "gy")
    everyone = ("grid", "gx", "gy")

    def exchange(x):
        return lax.all_to_all(x, group, split_axis=0, concat_axis=0, tiled=True)

    count = lax.axis_size("grid") * lax.axis_size("gx") * lax.axis_size("gy")
    across_y = lax.axis_size("gy")

    def pairs(step, first):
        out = []
        for t in range(count):
            if (t // step) % 2 == first:
                other = t + step
                if other >= count and step > 1:
                    continue
                out += [(t, other % count), (other % count, t)]
        return out

    deck_in = deck_fields.reshape(PLANES, DROWS, DCOLS)
    back_in = back_fields.reshape(PLANES, ROWS, COLS)
    request, fill_map, rim_map, near_map, keep = call(
        route_kernel,
        [
            ((MEMBERS, 1, 128), F32),
            ((SLOTS, ROWS * COLS), BF16),
            ((SLOTS, 3 * COLS), BF16),
            ((NEAR * MEMBERS, 2 * COLS), BF16),
            ((ROWS + 1, 8, COLS), F32),
        ],
        [donors.reshape(1, FRINGE), stencil.reshape(FRINGE, 4).T, fringe_cells],
        scratch=[
            pltpu.VMEM((1, FRINGE), jnp.int32),
            pltpu.VMEM((4, FRINGE), jnp.int32),
            pltpu.VMEM((1, FRINGE - NEAR), jnp.int32),
            pltpu.VMEM((MEMBERS, 3 * CAP), F32),
            pltpu.SemaphoreType.DMA((3,)),
        ],
        hbm_at=(0, 1, 2),
        name="route",
    )
    request = exchange(request)
    pieces = [pltpu.VMEM((256, DROWS * DCOLS), BF16), pltpu.VMEM((256, ROWS * COLS), BF16)]
    deck, back_state, far, near, answers = call(
        first_answer_kernel,
        [
            ((DROWS, PLANES, DCOLS), F32),
            ((ROWS, PLANES, COLS), F32),
            ((SLOTS, DROWS * DCOLS), BF16),
            ((NEAR * MEMBERS, ROWS * COLS), BF16),
            ((MEMBERS, 1, PACKED), F32),
        ],
        [request, deck_in, back_in],
        scratch=[pltpu.VMEM((MEMBERS, 128), F32)]
        + pieces
        + [
            pltpu.VMEM((PLANES, DROWS, DCOLS), F32),
            pltpu.VMEM((PLANES, ROWS, COLS), F32),
            pltpu.SemaphoreType.DMA((2,)),
        ],
        hbm_at=(1, 2),
        name="first_answer",
    )
    base = None
    for section in range(3):
        got = exchange(answers)
        got_pieces, deck, column_first, column_second, row_first, row_second = call(
            rim_kernel,
            [
                ((2 * PLANES, SLOTS), BF16),
                ((DROWS, PLANES, DCOLS), F32),
                ((PLANES, COLS), F32),
                ((PLANES, COLS), F32),
                ((PLANES, DCOLS + COLS), F32),
                ((PLANES, DCOLS + COLS), F32),
            ],
            [got, rim_map, near_map, keep, deck, back_state],
            name="rim",
        )
        row_first = lax.ppermute(row_first, everyone, pairs(1, 0))
        row_second = lax.ppermute(row_second, everyone, pairs(1, 1))
        column_first = lax.ppermute(column_first, everyone, pairs(across_y, 0))
        column_second = lax.ppermute(column_second, everyone, pairs(across_y, 1))
        (back_state,) = call(
            fill_kernel,
            [((ROWS, PLANES, COLS), F32)],
            [got_pieces, fill_map, keep, back_state],
            name="fill",
        )
        if section == 0:
            base = [deck, back_state]
        ins = [deck, back_state, column_first, column_second, row_first, row_second, metrics, keep]
        if section > 0:
            ins += base
        kernel = functools.partial(section_kernel, section)
        if section < 2:
            deck, back_state, answers = call(
                kernel,
                [
                    ((DROWS, PLANES, DCOLS), F32),
                    ((ROWS, PLANES, COLS), F32),
                    ((MEMBERS, 1, PACKED), F32),
                ],
                ins + [far, near],
                scratch=pieces,
                name="section",
            )
        else:
            deck, back_state = call(
                kernel,
                [((PLANES, DROWS, DCOLS), F32), ((PLANES, ROWS, COLS), F32)],
                ins,
                name="section",
            )
    return deck.reshape(deck_fields.shape), back_state.reshape(back_fields.shape)


def solution(mesh):
    return jax.shard_map(
        local,
        mesh=mesh,
        in_specs=(
            P(None, None, ("grid", "gx", "gy"), None),
            P(None, None, ("grid", "gx"), "gy"),
            P(None, ("grid", "gx", "gy"), None),
            P(("grid", "gx", "gy"), None, None),
            P(("grid", "gx", "gy"), None, None),
            P(("grid", "gx", "gy"), None),
        ),
        out_specs=(P(None, None, ("grid", "gx", "gy"), None), P(None, None, ("grid", "gx"), "gy")),
        check_vma=False,
    )
```

profile of v0, /device:TPU:8, one launch (start us, length us, event | category | flops | bytes accessed | tf_op | source)
XLA Modules:
  0.0 141.3 jit_solution(8497014147291447248)
XLA Ops:
  0.6 0.0 copy-start.3
  0.6 0.7 copy-done.3
  1.3 0.0 copy-start.4
  1.3 0.7 copy-done.4
  2.0 0.0 copy-start.5
  2.0 0.7 copy-done.5
  2.7 2.0 %route.1 = (f32[64,1,128]{2,1,0:T(1,128)S(1)}, bf16[1024,2048]{1,0:T(8,128)(2,1)S(1)}, bf16[1024,384]{1,0:T(8,128)(2,1)S(1)}, bf16[256,256]{1,0:T(8,128)(2,1)S(1)}, f32[17,8,128]{2,1,0:T(8,128)S(1)}) custom-call(s32[1,512]{1,0:T(1,128)S(1)} %bitcast.11, s32[4,512]{1,0:T(4,128)S(1)} %bitcast.10, s32[1,508]{1,0:T(1,128)S(1)} %copy-done.5), custom_call_target="tpu_custom_call" | custom-call | tf_op jit(solution)/shard_map/route/pallas_call | solution.py:51
  4.7 21.3 %all_to_all.20.request_ref = f32[64,1,128]{2,1,0:T(1,128)S(1)} all-to-all(f32[64,1,128]{2,1,0:T(1,128)S(1)} %get-tuple-element.38), channel_id=1, replica_groups=mesh['grid'=4,'gx'=8,'gy'=8] {'gx','gy'}, dimensions={0} | all-to-all | bytes 65536 | tf_op jit(solution)/shard_map/all_to_all | solution.py:422
  26.0 1.1 copy-done
  27.2 1.0 copy-done.1
  28.1 5.6 %first_answer.1 = (f32[2,96,384]{2,1,0:T(8,128)S(1)}, f32[16,96,128]{2,1,0:T(8,128)S(1)}, bf16[1024,768]{1,0:T(8,128)(2,1)S(1)}, bf16[256,2048]{1,0:T(8,128)(2,1)S(1)}, f32[64,1,1536]{2,1,0:T(1,128)S(1)}) custom-call(f32[64,1,128]{2,1,0:T(1,128)S(1)} %all_to_all.20.request_ref, f32[96,2,384]{2,1,0:T(2,128)S(1)} %bitcast.9, f32[96,16,128]{2,1,0:T(8,128)S(1)} %bitcast.8), custom_call_target="tpu_custom_call" | custom-call | tf_op jit(solution)/shard_map/first_answer/pallas_call | solution.py:51
  33.7 19.2 %all_to_all.21.got_ref = f32[64,1,1536]{2,1,0:T(1,128)S(1)} all-to-all(f32[64,1,1536]{2,1,0:T(1,128)S(1)} %get-tuple-element.39), channel_id=1, replica_groups=mesh['grid'=4,'gx'=8,'gy'=8] {'gx','gy'}, dimensions={0} | all-to-all | bytes 786432 | tf_op jit(solution)/shard_map/all_to_all | solution.py:422
  52.9 1.1 rim.3
  54.0 1.5 %collective-permute-start.2 = (f32[96,512]{1,0:T(8,128)S(1)}, f32[96,512]{1,0:T(8,128)S(1)}, u32[]{:S(2)}, u32[]{:S(2)}) collective-permute-start(f32[96,512]{1,0:T(8,128)S(1)} %get-tuple-element.50), channel_id=1, source_target_pairs={{0,1},{1,0},{2,3},{3,2},{4,5},{5,4},{6,7},{7,6},{8,9},{9,8},{10,11... | collective-permute-start | bytes 589832 | tf_op jit(solution)/shard_map/ppermute | solution.py:497
  55.5 1.0 collective-permute-start.3
  56.5 0.3 collective-permute-start
  56.9 2.3 %collective-permute-start.1 = (f32[96,128]{1,0:T(8,128)S(1)}, f32[96,128]{1,0:T(8,128)S(1)}, u32[]{:S(2)}, u32[]{:S(2)}) collective-permute-start(f32[96,128]{1,0:T(8,128)S(1)} %get-tuple-element.49), channel_id=1, source_target_pairs={{8,16},{16,8},{9,17},{17,9},{10,18},{18,10},{11,19},{19,11},{12,20... | collective-permute-start | bytes 147464 | tf_op jit(solution)/shard_map/ppermute | solution.py:500
  59.2 1.0 fill.3.refs_1_.refs_9_
  60.2 0.0 collective-permute-done.refs_2_
  60.3 5.1 %collective-permute-done.1.refs_3_ = f32[96,128]{1,0:T(8,128)S(1)} collective-permute-done((f32[96,128]{1,0:T(8,128)S(1)}, f32[96,128]{1,0:T(8,128)S(1)}, u32[]{:S(2)}, u32[]{:S(2)}) %collective-permute-start.1) | collective-permute-done | bytes 49184 | tf_op jit(solution)/shard_map/ppermute | solution.py:500
  65.3 0.0 collective-permute-done.2.refs_4_
  65.3 0.0 collective-permute-done.3.refs_5_
  65.3 0.0 copy-done.2
  65.3 2.7 %section.3 = (f32[2,96,384]{2,1,0:T(8,128)S(1)}, f32[16,96,128]{2,1,0:T(8,128)S(1)}, f32[64,1,1536]{2,1,0:T(1,128)S(1)}) custom-call(f32[2,96,384]{2,1,0:T(8,128)S(1)} %get-tuple-element.45.refs_0_.refs_8_, f32[16,96,128]{2,1,0:T(8,128)S(1)} %fill.3.refs_1_.refs_9_, f32[96,128]{1,0:T(8,128)S(1)} %collective-permute-done.refs_2_, ...), custom_call_target="tpu_custom_call" | custom-call | tf_op jit(solution)/shard_map/section/pallas_call | solution.py:51
  68.1 21.2 %all_to_all.22.got_ref = f32[64,1,1536]{2,1,0:T(1,128)S(1)} all-to-all(f32[64,1,1536]{2,1,0:T(1,128)S(1)} %get-tuple-element.54), channel_id=1, replica_groups=mesh['grid'=4,'gx'=8,'gy'=8] {'gx','gy'}, dimensions={0} | all-to-all | bytes 786432 | tf_op jit(solution)/shard_map/all_to_all | solution.py:422
  89.2 1.1 rim.4
  90.3 1.5 %collective-permute-start.6 = (f32[96,512]{1,0:T(8,128)S(1)}, f32[96,512]{1,0:T(8,128)S(1)}, u32[]{:S(2)}, u32[]{:S(2)}) collective-permute-start(f32[96,512]{1,0:T(8,128)S(1)} %get-tuple-element.61), channel_id=1, source_target_pairs={{0,1},{1,0},{2,3},{3,2},{4,5},{5,4},{6,7},{7,6},{8,9},{9,8},{10,11... | collective-permute-start | bytes 589832 | tf_op jit(solution)/shard_map/ppermute | solution.py:497
  91.8 1.1 collective-permute-start.7
  92.9 0.3 collective-permute-start.4
  93.2 2.2 %collective-permute-start.5 = (f32[96,128]{1,0:T(8,128)S(1)}, f32[96,128]{1,0:T(8,128)S(1)}, u32[]{:S(2)}, u32[]{:S(2)}) collective-permute-start(f32[96,128]{1,0:T(8,128)S(1)} %get-tuple-element.60), channel_id=1, source_target_pairs={{8,16},{16,8},{9,17},{17,9},{10,18},{18,10},{11,19},{19,11},{12,20... | collective-permute-start | bytes 147464 | tf_op jit(solution)/shard_map/ppermute | solution.py:500
  95.4 1.0 fill.4.refs_1_
  96.4 0.0 collective-permute-done.4.refs_2_
  96.4 5.2 %collective-permute-done.5.refs_3_ = f32[96,128]{1,0:T(8,128)S(1)} collective-permute-done((f32[96,128]{1,0:T(8,128)S(1)}, f32[96,128]{1,0:T(8,128)S(1)}, u32[]{:S(2)}, u32[]{:S(2)}) %collective-permute-start.5) | collective-permute-done | bytes 49184 | tf_op jit(solution)/shard_map/ppermute | solution.py:500
  101.7 0.0 collective-permute-done.6.refs_4_
  101.7 0.0 collective-permute-done.7.refs_5_
  101.7 2.9 %section.4 = (f32[2,96,384]{2,1,0:T(8,128)S(1)}, f32[16,96,128]{2,1,0:T(8,128)S(1)}, f32[64,1,1536]{2,1,0:T(1,128)S(1)}) custom-call(f32[2,96,384]{2,1,0:T(8,128)S(1)} %get-tuple-element.57.refs_0_, f32[16,96,128]{2,1,0:T(8,128)S(1)} %fill.4.refs_1_, f32[96,128]{1,0:T(8,128)S(1)} %collective-permute-done.4.refs_2_, ...), custom_call_target="tpu_custom_call" | custom-call | tf_op jit(solution)/shard_map/section/pallas_call | solution.py:51
  104.5 20.9 %all_to_all.23.got_ref = f32[64,1,1536]{2,1,0:T(1,128)S(1)} all-to-all(f32[64,1,1536]{2,1,0:T(1,128)S(1)} %get-tuple-element.63), channel_id=1, replica_groups=mesh['grid'=4,'gx'=8,'gy'=8] {'gx','gy'}, dimensions={0} | all-to-all | bytes 786432 | tf_op jit(solution)/shard_map/all_to_all | solution.py:422
  125.4 1.1 rim.5
  126.5 1.7 %collective-permute-start.10 = (f32[96,512]{1,0:T(8,128)S(1)}, f32[96,512]{1,0:T(8,128)S(1)}, u32[]{:S(2)}, u32[]{:S(2)}) collective-permute-start(f32[96,512]{1,0:T(8,128)S(1)} %get-tuple-element.70), channel_id=1, source_target_pairs={{0,1},{1,0},{2,3},{3,2},{4,5},{5,4},{6,7},{7,6},{8,9},{9,8},{10,11... | collective-permute-start | bytes 589832 | tf_op jit(solution)/shard_map/ppermute | solution.py:497
  128.2 1.4 collective-permute-start.11
  129.6 0.0 collective-permute-start.8
  129.6 2.5 %collective-permute-start.9 = (f32[96,128]{1,0:T(8,128)S(1)}, f32[96,128]{1,0:T(8,128)S(1)}, u32[]{:S(2)}, u32[]{:S(2)}) collective-permute-start(f32[96,128]{1,0:T(8,128)S(1)} %get-tuple-element.69), channel_id=1, source_target_pairs={{8,16},{16,8},{9,17},{17,9},{10,18},{18,10},{11,19},{19,11},{12,20... | collective-permute-start | bytes 147464 | tf_op jit(solution)/shard_map/ppermute | solution.py:500
  132.1 1.0 fill.5.refs_1_
  133.1 0.0 collective-permute-done.8.refs_2_
  133.1 5.0 %collective-permute-done.9.refs_3_ = f32[96,128]{1,0:T(8,128)S(1)} collective-permute-done((f32[96,128]{1,0:T(8,128)S(1)}, f32[96,128]{1,0:T(8,128)S(1)}, u32[]{:S(2)}, u32[]{:S(2)}) %collective-permute-start.9) | collective-permute-done | bytes 49184 | tf_op jit(solution)/shard_map/ppermute | solution.py:500
  138.1 0.0 collective-permute-done.10.refs_4_
  138.1 0.0 collective-permute-done.11.refs_5_
  138.1 3.2 %section.5 = (f32[96,2,384]{2,1,0:T(2,128)}, f32[96,16,128]{2,1,0:T(8,128)}) custom-call(f32[2,96,384]{2,1,0:T(8,128)S(1)} %get-tuple-element.66.refs_0_, f32[16,96,128]{2,1,0:T(8,128)S(1)} %fill.5.refs_1_, f32[96,128]{1,0:T(8,128)S(1)} %collective-permute-done.8.refs_2_, f32[96,128]{1,0:T(8,128)S(1)} %collective-permute-done.9.refs_3_, ...), custom_call_target="tpu_custom_call" | custom-call | tf_op jit(solution)/shard_map/section/pallas_call | solution.py:51
  (3 shorter events, 0.0 us)
Async XLA Ops:
  0.6 0.7 copy-start.3
  1.3 0.7 copy-start.4
  2.0 0.7 copy-start.5
  26.0 1.1 copy-start
  27.2 1.0 copy-start.1
  52.9 12.4 %copy-start.2 = (f32[4,2,384]{2,1,0:T(2,128)S(1)}, f32[4,2,384]{2,1,0:T(2,128)}, u32[]{:S(2)}) copy-start(f32[4,2,384]{2,1,0:T(2,128)} %refs_6_.5) | copy-start | bytes 36868
  54.0 11.3 %collective-permute-start.2 = (f32[96,512]{1,0:T(8,128)S(1)}, f32[96,512]{1,0:T(8,128)S(1)}, u32[]{:S(2)}, u32[]{:S(2)}) collective-permute-start(f32[96,512]{1,0:T(8,128)S(1)} %get-tuple-element.50), channel_id=1, source_target_pairs={{0,1},{1,0},{2,3},{3,2},{4,5},{5,4},{6,7},{7,6},{8,9},{9,8},{10,11... | collective-permute-start | bytes 589832 | tf_op jit(solution)/shard_map/ppermute | solution.py:497
  55.5 9.8 %collective-permute-start.3 = (f32[96,512]{1,0:T(8,128)S(1)}, f32[96,512]{1,0:T(8,128)S(1)}, u32[]{:S(2)}, u32[]{:S(2)}) collective-permute-start(f32[96,512]{1,0:T(8,128)S(1)} %get-tuple-element.51), channel_id=1, source_target_pairs={{1,2},{2,1},{3,4},{4,3},{5,6},{6,5},{7,8},{8,7},{9,10},{10,9},{11,... | collective-permute-start | bytes 589832 | tf_op jit(solution)/shard_map/ppermute | solution.py:498
  56.5 3.7 %collective-permute-start = (f32[96,128]{1,0:T(8,128)S(1)}, f32[96,128]{1,0:T(8,128)S(1)}, u32[]{:S(2)}, u32[]{:S(2)}) collective-permute-start(f32[96,128]{1,0:T(8,128)S(1)} %get-tuple-element.48), channel_id=1, source_target_pairs={{0,8},{8,0},{1,9},{9,1},{2,10},{10,2},{3,11},{11,3},{4,12},{12,4},... | collective-permute-start | bytes 147464 | tf_op jit(solution)/shard_map/ppermute | solution.py:499
  56.9 8.5 %collective-permute-start.1 = (f32[96,128]{1,0:T(8,128)S(1)}, f32[96,128]{1,0:T(8,128)S(1)}, u32[]{:S(2)}, u32[]{:S(2)}) collective-permute-start(f32[96,128]{1,0:T(8,128)S(1)} %get-tuple-element.49), channel_id=1, source_target_pairs={{8,16},{16,8},{9,17},{17,9},{10,18},{18,10},{11,19},{19,11},{12,20... | collective-permute-start | bytes 147464 | tf_op jit(solution)/shard_map/ppermute | solution.py:500
  90.3 11.3 %collective-permute-start.6 = (f32[96,512]{1,0:T(8,128)S(1)}, f32[96,512]{1,0:T(8,128)S(1)}, u32[]{:S(2)}, u32[]{:S(2)}) collective-permute-start(f32[96,512]{1,0:T(8,128)S(1)} %get-tuple-element.61), channel_id=1, source_target_pairs={{0,1},{1,0},{2,3},{3,2},{4,5},{5,4},{6,7},{7,6},{8,9},{9,8},{10,11... | collective-permute-start | bytes 589832 | tf_op jit(solution)/shard_map/ppermute | solution.py:497
  91.8 9.8 %collective-permute-start.7 = (f32[96,512]{1,0:T(8,128)S(1)}, f32[96,512]{1,0:T(8,128)S(1)}, u32[]{:S(2)}, u32[]{:S(2)}) collective-permute-start(f32[96,512]{1,0:T(8,128)S(1)} %get-tuple-element.62), channel_id=1, source_target_pairs={{1,2},{2,1},{3,4},{4,3},{5,6},{6,5},{7,8},{8,7},{9,10},{10,9},{11,... | collective-permute-start | bytes 589832 | tf_op jit(solution)/shard_map/ppermute | solution.py:498
  92.9 3.5 %collective-permute-start.4 = (f32[96,128]{1,0:T(8,128)S(1)}, f32[96,128]{1,0:T(8,128)S(1)}, u32[]{:S(2)}, u32[]{:S(2)}) collective-permute-start(f32[96,128]{1,0:T(8,128)S(1)} %get-tuple-element.59), channel_id=1, source_target_pairs={{0,8},{8,0},{1,9},{9,1},{2,10},{10,2},{3,11},{11,3},{4,12},{12,4},... | collective-permute-start | bytes 147464 | tf_op jit(solution)/shard_map/ppermute | solution.py:499
  93.2 8.4 %collective-permute-start.5 = (f32[96,128]{1,0:T(8,128)S(1)}, f32[96,128]{1,0:T(8,128)S(1)}, u32[]{:S(2)}, u32[]{:S(2)}) collective-permute-start(f32[96,128]{1,0:T(8,128)S(1)} %get-tuple-element.60), channel_id=1, source_target_pairs={{8,16},{16,8},{9,17},{17,9},{10,18},{18,10},{11,19},{19,11},{12,20... | collective-permute-start | bytes 147464 | tf_op jit(solution)/shard_map/ppermute | solution.py:500
  126.5 11.6 %collective-permute-start.10 = (f32[96,512]{1,0:T(8,128)S(1)}, f32[96,512]{1,0:T(8,128)S(1)}, u32[]{:S(2)}, u32[]{:S(2)}) collective-permute-start(f32[96,512]{1,0:T(8,128)S(1)} %get-tuple-element.70), channel_id=1, source_target_pairs={{0,1},{1,0},{2,3},{3,2},{4,5},{5,4},{6,7},{7,6},{8,9},{9,8},{10,11... | collective-permute-start | bytes 589832 | tf_op jit(solution)/shard_map/ppermute | solution.py:497
  128.2 9.8 %collective-permute-start.11 = (f32[96,512]{1,0:T(8,128)S(1)}, f32[96,512]{1,0:T(8,128)S(1)}, u32[]{:S(2)}, u32[]{:S(2)}) collective-permute-start(f32[96,512]{1,0:T(8,128)S(1)} %get-tuple-element.71), channel_id=1, source_target_pairs={{1,2},{2,1},{3,4},{4,3},{5,6},{6,5},{7,8},{8,7},{9,10},{10,9},{11,... | collective-permute-start | bytes 589832 | tf_op jit(solution)/shard_map/ppermute | solution.py:498
  129.6 3.5 %collective-permute-start.8 = (f32[96,128]{1,0:T(8,128)S(1)}, f32[96,128]{1,0:T(8,128)S(1)}, u32[]{:S(2)}, u32[]{:S(2)}) collective-permute-start(f32[96,128]{1,0:T(8,128)S(1)} %get-tuple-element.68), channel_id=1, source_target_pairs={{0,8},{8,0},{1,9},{9,1},{2,10},{10,2},{3,11},{11,3},{4,12},{12,4},... | collective-permute-start | bytes 147464 | tf_op jit(solution)/shard_map/ppermute | solution.py:499
  129.6 8.4 %collective-permute-start.9 = (f32[96,128]{1,0:T(8,128)S(1)}, f32[96,128]{1,0:T(8,128)S(1)}, u32[]{:S(2)}, u32[]{:S(2)}) collective-permute-start(f32[96,128]{1,0:T(8,128)S(1)} %get-tuple-element.69), channel_id=1, source_target_pairs={{8,16},{16,8},{9,17},{17,9},{10,18},{18,10},{11,19},{19,11},{12,20... | collective-permute-start | bytes 147464 | tf_op jit(solution)/shard_map/ppermute | solution.py:500
where the time goes:
time: 142 us; the launch traced here: 141 us
  blocking collectives  82.6 us (58%)
  Pallas kernels  22.7 us (16%)
  starting transfers between devices  15.8 us (11%)
  waiting for transfers between devices  15.3 us (11%)
  local copies, waits for them, and re-layouts  4.15 us (3%)
    all_to_all x4, blocking collectives, exchange(): return lax.all_to_all(x, group, split_axis=0, concat_axis=0, tiled=True)  82.6 us
    pallas_call x11, Pallas kernels, call(): pl.pallas_call(kernel, out_shape=tuple((jax.ShapeDtypeStruct(s, d) for s,...  22.7 us
    ppermute x3, waiting for transfers between devices, local(): column_second = lax.ppermute(column_second, everyone, pairs(across_y, 1))  15.3 us
    ppermute x3, starting transfers between devices, local(): column_second = lax.ppermute(column_second, everyone, pairs(across_y, 1))  6.97 us
    ppermute x3, starting transfers between devices, local(): row_first = lax.ppermute(row_first, everyone, pairs(1, 0))  4.66 us
    unnamed x12, local copies, waits for them, and re-layouts  4.15 us
    ppermute x3, starting transfers between devices, local(): row_second = lax.ppermute(row_second, everyone, pairs(1, 1))  3.46 us
  transfers between devices with their start and end apart: 12, of which 3 were waited for; matrix products, arithmetic and copies ran while one was open for 0% of the time, Pallas kernels for 2%

commit v1 on v0

--- a/solution.py
+++ b/solution.py
@@ -48,6 +48,7 @@
     def spec(i):
         return pl.BlockSpec(memory_space=pltpu.HBM if i in hbm_at else pltpu.VMEM)
 
+    ins = [pltpu.with_memory_space_constraint(x, pltpu.HBM) if i in hbm_at else x for i, x in enumerate(ins)]
     return pl.pallas_call(
         kernel,
         out_shape=tuple(jax.ShapeDtypeStruct(s, d) for s, d in outs),
@@ -60,8 +61,8 @@
 
 
 def route_kernel(
-    donors_hbm, stencil_hbm, cells_hbm, request_ref, fill_ref, rim_ref, near_ref, keep_ref,
-    donors_ref, stencil_ref, cells_ref, local_ref, sems,
+    donors_hbm, stencil_hbm, cells_hbm, request_ref, local_ref, rim_ref, near_ref, keep_ref,
+    donors_ref, stencil_ref, cells_ref, sems,
 ):
     pairs = [(donors_hbm, donors_ref), (stencil_hbm, stencil_ref), (cells_hbm, cells_ref)]
     copies = [pltpu.make_async_copy(a, b, sems.at[i]) for i, (a, b) in enumerate(pairs)]
@@ -100,42 +101,43 @@
             jnp.where(far, 0, lane + 1),
         ]
     )
-    landing(local_ref, fill_ref, rim_ref, near_ref, keep_ref)
-
-
-def landing(local_ref, fill_ref, rim_ref, near_ref, keep_ref):
+    landing(local_ref, rim_ref, near_ref, keep_ref)
+
+
+def over_eight(x):
+    return jnp.sum(x.reshape(MEMBERS // 8, 8, COLS), axis=0)
+
+
+def kept(listed):
+    return 1.0 - jnp.broadcast_to(jnp.sum(listed, axis=0, keepdims=True), (8, COLS))
+
+
+def landing(local_ref, rim_ref, near_ref, keep_ref):
     lane = iota((MEMBERS, COLS), 1)
     places = local_ref[...].astype(jnp.int32)
-    listed = [jnp.zeros((8, COLS), F32) for _ in range(ROWS + 1)]
-
-    def over_eight(x):
-        return jnp.sum(x.reshape(MEMBERS // 8, 8, COLS), axis=0)
+    listed = [jnp.zeros((8, COLS), F32) for _ in range(3)]
 
     for s in range(CAP):
         at = slice(s * MEMBERS, (s + 1) * MEMBERS)
         row = jnp.broadcast_to(places[:, s : s + 1] - 1, (MEMBERS, COLS))
         col = jnp.broadcast_to(places[:, CAP + s : CAP + s + 1], (MEMBERS, COLS))
         hit = jnp.where(lane == col, 1.0, 0.0)
-        for r in range(ROWS):
+        for i, r in enumerate((0, ROWS - 1)):
             here = jnp.where(row == r, hit, 0.0)
-            fill_ref[at, r * COLS : (r + 1) * COLS] = here.astype(BF16)
-            listed[r] = listed[r] + over_eight(here)
-            if r == 0:
-                rim_ref[at, 0:COLS] = here.astype(BF16)
-            if r == ROWS - 1:
-                rim_ref[at, COLS : 2 * COLS] = here.astype(BF16)
+            rim_ref[at, i * COLS : (i + 1) * COLS] = here.astype(BF16)
+            listed[i] = listed[i] + over_eight(here)
         side = jnp.where(col == 0, row, jnp.where(col == COLS - 1, row + ROWS, -1))
         here = jnp.where((lane == side) & (row >= 0), 1.0, 0.0)
         rim_ref[at, 2 * COLS : 3 * COLS] = here.astype(BF16)
-        listed[ROWS] = listed[ROWS] + over_eight(here)
+        listed[2] = listed[2] + over_eight(here)
         if s < NEAR:
             near = places[:, 2 * CAP + s : 2 * CAP + s + 1] - 1
             place = jnp.where(near >= 0, (near >> 1) * COLS + COLS - 2 + (near & 1), -1)
             place = jnp.broadcast_to(place, (MEMBERS, COLS))
             for r in range(DROWS):
                 near_ref[at, r * COLS : (r + 1) * COLS] = jnp.where(lane + r * COLS == place, 1.0, 0.0).astype(BF16)
-    for r in range(ROWS + 1):
-        keep_ref[r] = 1.0 - jnp.broadcast_to(jnp.sum(listed[r], axis=0, keepdims=True), (8, COLS))
+    for i in range(3):
+        keep_ref[i] = kept(listed[i])
 
 
 def split(x):
@@ -269,21 +271,25 @@
         outer = jnp.where(lane >= 126, near[:, r * 128 : (r + 1) * 128], deck_ref[r, :, 256:384])
         deck.append(jnp.concatenate([deck_ref[r, :, 0:256], outer], axis=1))
         deck_out[r] = deck[r]
-    row_first[:, 0:DCOLS] = jnp.where(odd, deck[0], deck[1])
-    row_second[:, 0:DCOLS] = jnp.where(odd, deck[1], deck[0])
+    row_first[0:PLANES, :] = jnp.where(odd, deck[0], deck[1])
+    row_second[0:PLANES, :] = jnp.where(odd, deck[1], deck[0])
     rim = dot(got_pieces[...], rim_ref[...], NN)
     rim = rim[0:PLANES] + rim[PLANES : 2 * PLANES]
     north = back_ref[0] * keep_ref[0, 0:1, :] + rim[:, 0:COLS]
-    south = back_ref[ROWS - 1] * keep_ref[ROWS - 1, 0:1, :] + rim[:, COLS : 2 * COLS]
+    south = back_ref[ROWS - 1] * keep_ref[1, 0:1, :] + rim[:, COLS : 2 * COLS]
     column_first[...] = jnp.where(odd_line, north, south)
     column_second[...] = jnp.where(odd_line, south, north)
     ends = jnp.zeros((PLANES, COLS), F32)
     for r in range(ROWS):
         ends = jnp.where(lane == r, back_ref[r, :, 0:1], ends)
         ends = jnp.where(lane == ROWS + r, back_ref[r, :, COLS - 1 : COLS], ends)
-    ends = ends * keep_ref[ROWS, 0:1, :] + rim[:, 2 * COLS : 3 * COLS]
-    row_first[:, DCOLS : DCOLS + COLS] = ends
-    row_second[:, DCOLS : DCOLS + COLS] = ends
+    ends = ends * keep_ref[2, 0:1, :] + rim[:, 2 * COLS : 3 * COLS]
+    ends = jnp.concatenate([ends, jnp.zeros((COLS - PLANES, COLS), F32)], axis=0).T
+    parts = [ends[i * 8 : (i + 1) * 8, :] for i in range(4)]
+    for side, flag in ((row_first, odd), (row_second, jnp.logical_not(odd))):
+        for i in range(2):
+            side[PLANES : PLANES + 8, i * COLS : (i + 1) * COLS] = jnp.where(flag, parts[i], parts[2 + i])
+        side[PLANES : PLANES + 8, 2 * COLS : 3 * COLS] = jnp.zeros((8, COLS), F32)
 
 
 def fill_kernel(got_pieces, fill_ref, keep_ref, back_ref, back_out):
@@ -295,43 +301,66 @@
             back_out[r] = back_ref[r] * keep_ref[r, 0:1, :] + new[:, half * 128 : (half + 1) * 128]
 
 
+def first_fill_kernel(got_pieces, local_ref, back_ref, back_out, fill_ref, keep_ref):
+    lane = iota((MEMBERS, COLS), 1)
+    places = local_ref[...].astype(jnp.int32)
+    listed = [jnp.zeros((8, COLS), F32) for _ in range(ROWS)]
+    for s in range(CAP):
+        at = slice(s * MEMBERS, (s + 1) * MEMBERS)
+        row = jnp.broadcast_to(places[:, s : s + 1] - 1, (MEMBERS, COLS))
+        col = jnp.broadcast_to(places[:, CAP + s : CAP + s + 1], (MEMBERS, COLS))
+        hit = jnp.where(lane == col, 1.0, 0.0)
+        for r in range(ROWS):
+            here = jnp.where(row == r, hit, 0.0)
+            fill_ref[at, r * COLS : (r + 1) * COLS] = here.astype(BF16)
+            listed[r] = listed[r] + over_eight(here)
+    for r in range(ROWS):
+        keep_ref[r] = kept(listed[r])
+    fill_kernel(got_pieces, fill_ref, keep_ref, back_ref, back_out)
+
+
 def update(here, minus_xi, plus_xi, minus_eta, plus_eta, metric, keep, base, section):
+    weight = (1.0, 0.25, 2.0 / 3.0)[section]
+    step = (weight * TIME_STEP) * keep
     d_xi, d_eta, d_span, lap = [], [], [], []
     strain = None
     for c in range(3):
         f = here[c]
-        plus_span = jnp.concatenate([f[1:], f[:1]], axis=0)
-        minus_span = jnp.concatenate([f[-1:], f[:-1]], axis=0)
+        plus_span = pltpu.roll(f, SPAN - 1, 0)
+        minus_span = pltpu.roll(f, 1, 0)
         a = plus_xi[c] - minus_xi[c]
         b = plus_eta[c] - minus_eta[c]
         s = plus_span - minus_span
         square = a * a + b * b + s * s
         strain = square if strain is None else strain + square
-        doubled = 2.0 * f
-        l_xi = plus_xi[c] - doubled + minus_xi[c]
-        l_eta = plus_eta[c] - doubled + minus_eta[c]
-        if metric is not None:
-            l_xi, l_eta = metric[4] * l_xi, metric[5] * l_eta
-        lap.append(l_xi + l_eta + (plus_span - doubled + minus_span))
+        if metric is None:
+            around = (plus_xi[c] + minus_xi[c]) + (plus_eta[c] + minus_eta[c]) + (plus_span + minus_span)
+            lap.append(around - 6.0 * f)
+        else:
+            doubled = 2.0 * f
+            l_xi = plus_xi[c] - doubled + minus_xi[c]
+            l_eta = plus_eta[c] - doubled + minus_eta[c]
+            lap.append(metric[4] * l_xi + metric[5] * l_eta + (plus_span - doubled + minus_span))
         d_xi.append(a)
         d_eta.append(b)
         d_span.append(s)
-    viscosity = SMAGORINSKY * jnp.sqrt(1.0 + 0.25 * strain)
+    viscosity = (SMAGORINSKY * step) * jnp.sqrt(1.0 + 0.25 * strain)
+    half = 0.5 * step
     if metric is None:
-        speed_xi, speed_eta = here[0], here[1]
+        speed_xi, speed_eta = half * here[0], half * here[1]
     else:
-        speed_xi = metric[0] * here[0] + metric[1] * here[1]
-        speed_eta = metric[2] * here[0] + metric[3] * here[1]
+        speed_xi = half * (metric[0] * here[0] + metric[1] * here[1])
+        speed_eta = half * (metric[2] * here[0] + metric[3] * here[1])
+    speed_span = half * here[2]
     out = []
     for c in range(3):
-        advection = 0.5 * (speed_xi * d_xi[c] + speed_eta * d_eta[c] + here[2] * d_span[c])
-        tendency = viscosity * lap[c] - advection
+        change = viscosity * lap[c] - (speed_xi * d_xi[c] + speed_eta * d_eta[c] + speed_span * d_span[c])
         if section == 0:
-            out.append(here[c] + (TIME_STEP * keep) * tendency)
+            out.append(here[c] + change)
         elif section == 1:
-            out.append(0.75 * base[c] + 0.25 * here[c] + (0.25 * TIME_STEP * keep) * tendency)
+            out.append(0.75 * base[c] + (0.25 * here[c] + change))
         else:
-            out.append(base[c] * (1.0 / 3.0) + (2.0 / 3.0) * here[c] + (2.0 / 3.0 * TIME_STEP * keep) * tendency)
+            out.append(base[c] * (1.0 / 3.0) + ((2.0 / 3.0) * here[c] + change))
     return out
 
 
@@ -364,9 +393,19 @@
         return jnp.where(flag, a, b), jnp.where(flag, b, a)
 
     spans = [slice(c * SPAN, (c + 1) * SPAN) for c in range(3)]
-    across = [ordered(odd, row_first, row_second, (at, slice(0, DCOLS))) for at in spans]
-    beside = [ordered(odd, row_first, row_second, (at, slice(DCOLS, DCOLS + COLS))) for at in spans]
+    across = [ordered(odd, row_first, row_second, (at, slice(None))) for at in spans]
+    beside = []
+    halves = [
+        ordered(odd, row_first, row_second, (slice(PLANES, PLANES + 8), slice(i * COLS, (i + 1) * COLS)))
+        for i in range(2)
+    ]
+    for side in range(2):
+        cells = jnp.concatenate([halves[0][side], halves[1][side], jnp.zeros((COLS - 16, COLS), F32)], axis=0)
+        beside.append(cells.T)
+    north_end = (line > 0).astype(F32)
+    south_end = (line < lax.axis_size("grid") * lax.axis_size("gx") - 1).astype(F32)
     along = [ordered(odd_line, column_first, column_second, (at, slice(None))) for at in spans]
+    along = [(before * north_end, after * south_end) for before, after in along]
     lane = iota((SPAN, DCOLS), 1)
     keep_deck = jnp.where(iota((1, DCOLS), 1) < DCOLS - 2, 1.0, 0.0)
     for r in range(DROWS):
@@ -397,8 +436,8 @@
         plus = fields(back_ref, (r + 1,)) if r < ROWS - 1 else [a[1] for a in along]
         plus_eta, minus_eta = [], []
         for c in range(3):
-            from_west = beside[c][0][:, ROWS + r : ROWS + r + 1] * west_end
-            from_east = beside[c][1][:, r : r + 1] * east_end
+            from_west = beside[0][spans[c], r : r + 1] * west_end
+            from_east = beside[1][spans[c], r : r + 1] * east_end
             plus_eta.append(jnp.where(lane == COLS - 1, from_east, pltpu.roll(here[c], COLS - 1, 1)))
             minus_eta.append(jnp.where(lane == 0, from_west, pltpu.roll(here[c], 1, 1)))
         base = fields(base_back, (r,)) if section > 0 else None
@@ -424,33 +463,33 @@
     count = lax.axis_size("grid") * lax.axis_size("gx") * lax.axis_size("gy")
     across_y = lax.axis_size("gy")
 
-    def pairs(step, first):
+    def pairs(step, first, periodic=False):
         out = []
         for t in range(count):
             if (t // step) % 2 == first:
-                other = t + step
-                if other >= count and step > 1:
-                    continue
-                out += [(t, other % count), (other % count, t)]
+                other = (t + step) % count
+                if periodic or t + step < count:
+                    out += [(t, other), (other, t)]
+                else:
+                    out += [(t, t ^ 1), (other, other ^ 1)]
         return out
 
     deck_in = deck_fields.reshape(PLANES, DROWS, DCOLS)
     back_in = back_fields.reshape(PLANES, ROWS, COLS)
-    request, fill_map, rim_map, near_map, keep = call(
+    request, placing, rim_map, near_map, rim_keep = call(
         route_kernel,
         [
             ((MEMBERS, 1, 128), F32),
-            ((SLOTS, ROWS * COLS), BF16),
+            ((MEMBERS, 3 * CAP), F32),
             ((SLOTS, 3 * COLS), BF16),
             ((NEAR * MEMBERS, 2 * COLS), BF16),
-            ((ROWS + 1, 8, COLS), F32),
+            ((3, 8, COLS), F32),
         ],
         [donors.reshape(1, FRINGE), stencil.reshape(FRINGE, 4).T, fringe_cells],
         scratch=[
             pltpu.VMEM((1, FRINGE), jnp.int32),
             pltpu.VMEM((4, FRINGE), jnp.int32),
             pltpu.VMEM((1, FRINGE - NEAR), jnp.int32),
-            pltpu.VMEM((MEMBERS, 3 * CAP), F32),
             pltpu.SemaphoreType.DMA((3,)),
         ],
         hbm_at=(0, 1, 2),
@@ -488,24 +527,31 @@
                 ((DROWS, PLANES, DCOLS), F32),
                 ((PLANES, COLS), F32),
                 ((PLANES, COLS), F32),
-                ((PLANES, DCOLS + COLS), F32),
-                ((PLANES, DCOLS + COLS), F32),
+                ((PLANES + 8, DCOLS), F32),
+                ((PLANES + 8, DCOLS), F32),
             ],
-            [got, rim_map, near_map, keep, deck, back_state],
+            [got, rim_map, near_map, rim_keep, deck, back_state],
             name="rim",
         )
-        row_first = lax.ppermute(row_first, everyone, pairs(1, 0))
-        row_second = lax.ppermute(row_second, everyone, pairs(1, 1))
+        row_first = lax.ppermute(row_first, everyone, pairs(1, 0, True))
+        row_second = lax.ppermute(row_second, everyone, pairs(1, 1, True))
         column_first = lax.ppermute(column_first, everyone, pairs(across_y, 0))
         column_second = lax.ppermute(column_second, everyone, pairs(across_y, 1))
-        (back_state,) = call(
-            fill_kernel,
-            [((ROWS, PLANES, COLS), F32)],
-            [got_pieces, fill_map, keep, back_state],
-            name="fill",
-        )
         if section == 0:
+            back_state, fill_map, keep = call(
+                first_fill_kernel,
+                [((ROWS, PLANES, COLS), F32), ((SLOTS, ROWS * COLS), BF16), ((ROWS, 8, COLS), F32)],
+                [got_pieces, placing, back_state],
+                name="fill",
+            )
             base = [deck, back_state]
+        else:
+            (back_state,) = call(
+                fill_kernel,
+                [((ROWS, PLANES, COLS), F32)],
+                [got_pieces, fill_map, keep, back_state],
+                name="fill",
+            )
         ins = [deck, back_state, column_first, column_second, row_first, row_second, metrics, keep]
         if section > 0:
             ins += base

time: 142 us -> 133 us (0.937)
  starting transfers between devices: 15.8 us -> 10.1 us
  local copies, waits for them, and re-layouts: 4.15 us -> 0.01 us
    ppermute x3, starting transfers between devices: 6.97 us -> 1.35 us  [local(): column_second = lax.ppermute(column_second, everyone, pairs(across_y, 1))]
    ppermute x6, waiting for transfers between devices: 0.02 us -> 5.5 us  [the longest x3 5.49 us: local(): row_second = lax.ppermute(row_second, everyone, pairs(1, 1, True))]
    unnamed x12 -> x2, local copies, waits for them, and re-layouts: 4.15 us -> 0.01 us
    ppermute x3, waiting for transfers between devices: 15.3 us -> 11.2 us  [local(): column_second = lax.ppermute(column_second, everyone, pairs(across_y, 1))]
  transfers between devices with their start and end apart: 12 -> 12, of which waited for: 3 -> 6; matrix products, arithmetic and copies ran while one was open for 0% -> 0% of each run, Pallas kernels for 2% -> 3%
where the time goes in v1:
time: 133 us
  blocking collectives  81.2 us (61%)
  Pallas kernels  23.9 us (18%)
  waiting for transfers between devices  16.7 us (13%)
  starting transfers between devices  10.1 us (8%)
    all_to_all x4, blocking collectives, exchange(): return lax.all_to_all(x, group, split_axis=0, concat_axis=0, tiled=True)  81.2 us
    pallas_call x11, Pallas kernels, call(): pl.pallas_call(kernel, out_shape=tuple((jax.ShapeDtypeStruct(s, d) for s,...  23.9 us
    ppermute x3, waiting for transfers between devices, local(): column_second = lax.ppermute(column_second, everyone, pairs(across_y, 1))  11.2 us
    ppermute x3, waiting for transfers between devices, local(): row_second = lax.ppermute(row_second, everyone, pairs(1, 1, True))  5.49 us
    ppermute x3, starting transfers between devices, local(): row_first = lax.ppermute(row_first, everyone, pairs(1, 0, True))  4.31 us
    ppermute x3, starting transfers between devices, local(): row_second = lax.ppermute(row_second, everyone, pairs(1, 1, True))  4.01 us
  transfers between devices with their start and end apart: 12, of which 6 were waited for; matrix products, arithmetic and copies ran while one was open for 0% of the time, Pallas kernels for 3%

profile of v1, /device:TPU:8, one launch (start us, length us, event | category | flops | bytes accessed | tf_op | source)
XLA Modules:
  0.0 132.7 jit_solution(16288427754436220960)
XLA Ops:
  0.6 0.0 copy-start
  0.6 1.8 %route.1 = (f32[64,1,128]{2,1,0:T(1,128)S(1)}, f32[64,48]{1,0:T(8,128)S(1)}, bf16[1024,384]{1,0:T(8,128)(2,1)S(1)}, bf16[256,256]{1,0:T(8,128)(2,1)S(1)}, f32[3,8,128]{2,1,0:T(8,128)S(1)}) custom-call(s32[1,512]{1,0:T(1,128)} %bitcast.11, s32[4,512]{1,0:T(4,128)} %bitcast.10, s32[1,508]{1,0:T(1,128)} %cells_hbm.1), custom_call_target="tpu_custom_call" | custom-call | tf_op jit(solution)/shard_map/route/pallas_call | solution.py:52
  2.4 21.3 %all_to_all.20.request_ref = f32[64,1,128]{2,1,0:T(1,128)S(1)} all-to-all(f32[64,1,128]{2,1,0:T(1,128)S(1)} %get-tuple-element.41), channel_id=1, replica_groups=mesh['grid'=4,'gx'=8,'gy'=8] {'gx','gy'}, dimensions={0} | all-to-all | bytes 65536 | tf_op jit(solution)/shard_map/all_to_all | solution.py:461
  23.7 5.5 %first_answer.1 = (f32[2,96,384]{2,1,0:T(8,128)S(1)}, f32[16,96,128]{2,1,0:T(8,128)S(1)}, bf16[1024,768]{1,0:T(8,128)(2,1)S(1)}, bf16[256,2048]{1,0:T(8,128)(2,1)S(1)}, f32[64,1,1536]{2,1,0:T(1,128)S(1)}) custom-call(f32[64,1,128]{2,1,0:T(1,128)S(1)} %all_to_all.20.request_ref, f32[96,2,384]{2,1,0:T(2,128)} %bitcast.9, f32[96,16,128]{2,1,0:T(8,128)} %bitcast.8), custom_call_target="tpu_custom_call" | custom-call | tf_op jit(solution)/shard_map/first_answer/pallas_call | solution.py:52
  29.3 19.2 %all_to_all.21.got_ref = f32[64,1,1536]{2,1,0:T(1,128)S(1)} all-to-all(f32[64,1,1536]{2,1,0:T(1,128)S(1)} %get-tuple-element.42), channel_id=1, replica_groups=mesh['grid'=4,'gx'=8,'gy'=8] {'gx','gy'}, dimensions={0} | all-to-all | bytes 786432 | tf_op jit(solution)/shard_map/all_to_all | solution.py:461
  48.4 1.1 rim.3
  49.6 1.4 %collective-permute-start.2 = (f32[104,384]{1,0:T(8,128)S(1)}, f32[104,384]{1,0:T(8,128)S(1)}, u32[]{:S(2)}, u32[]{:S(2)}) collective-permute-start(f32[104,384]{1,0:T(8,128)S(1)} %get-tuple-element.54), channel_id=1, source_target_pairs={{0,1},{1,0},{2,3},{3,2},{4,5},{5,4},{6,7},{7,6},{8,9},{9,8},{10,11... | collective-permute-start | bytes 479240 | tf_op jit(solution)/shard_map/ppermute | solution.py:536
  51.0 1.1 collective-permute-start.3
  52.1 0.3 collective-permute-start
  52.4 0.3 collective-permute-start.1
  52.7 2.3 %fill.3 = (f32[16,96,128]{2,1,0:T(8,128)S(1)}, bf16[1024,2048]{1,0:T(8,128)(2,1)S(1)}, f32[16,8,128]{2,1,0:T(8,128)S(1)}) custom-call(bf16[192,1024]{1,0:T(8,128)(2,1)S(1)} %get-tuple-element.49.got_pieces, f32[64,48]{1,0:T(8,128)S(1)} %get-tuple-element.50.local_ref, f32[16,96,128]{2,1,0:T(8,128)S(1)} %get-tuple-element.47.back_ref), custom_call_target="tpu_custom_call" | custom-call | tf_op jit(solution)/shard_map/fill/pallas_call | solution.py:52
  55.0 0.0 collective-permute-done.refs_2_
  55.0 3.1 %collective-permute-done.1.refs_3_ = f32[96,128]{1,0:T(8,128)S(1)} collective-permute-done((f32[96,128]{1,0:T(8,128)S(1)}, f32[96,128]{1,0:T(8,128)S(1)}, u32[]{:S(2)}, u32[]{:S(2)}) %collective-permute-start.1) | collective-permute-done | bytes 49184 | tf_op jit(solution)/shard_map/ppermute | solution.py:539
  58.0 0.0 collective-permute-done.2.refs_4_
  58.0 1.9 %collective-permute-done.3.refs_5_ = f32[104,384]{1,0:T(8,128)S(1)} collective-permute-done((f32[104,384]{1,0:T(8,128)S(1)}, f32[104,384]{1,0:T(8,128)S(1)}, u32[]{:S(2)}, u32[]{:S(2)}) %collective-permute-start.3) | collective-permute-done | bytes 159776 | tf_op jit(solution)/shard_map/ppermute | solution.py:537
  59.9 0.0 copy-done
  59.9 2.8 %section.3 = (f32[2,96,384]{2,1,0:T(8,128)S(1)}, f32[16,96,128]{2,1,0:T(8,128)S(1)}, f32[64,1,1536]{2,1,0:T(1,128)S(1)}) custom-call(f32[2,96,384]{2,1,0:T(8,128)S(1)} %get-tuple-element.48.refs_0_.refs_8_, f32[16,96,128]{2,1,0:T(8,128)S(1)} %get-tuple-element.51.refs_1_.refs_9_, f32[96,128]{1,0:T(8,128)S(1)} %collective-permute-done.refs_2_, ...), custom_call_target="tpu_custom_call" | custom-call | tf_op jit(solution)/shard_map/section/pallas_call | solution.py:52
  62.7 20.5 %all_to_all.22.got_ref = f32[64,1,1536]{2,1,0:T(1,128)S(1)} all-to-all(f32[64,1,1536]{2,1,0:T(1,128)S(1)} %get-tuple-element.59), channel_id=1, replica_groups=mesh['grid'=4,'gx'=8,'gy'=8] {'gx','gy'}, dimensions={0} | all-to-all | bytes 786432 | tf_op jit(solution)/shard_map/all_to_all | solution.py:461
  83.2 1.1 rim.4
  84.4 1.5 %collective-permute-start.6 = (f32[104,384]{1,0:T(8,128)S(1)}, f32[104,384]{1,0:T(8,128)S(1)}, u32[]{:S(2)}, u32[]{:S(2)}) collective-permute-start(f32[104,384]{1,0:T(8,128)S(1)} %get-tuple-element.67), channel_id=1, source_target_pairs={{0,1},{1,0},{2,3},{3,2},{4,5},{5,4},{6,7},{7,6},{8,9},{9,8},{10,11... | collective-permute-start | bytes 479240 | tf_op jit(solution)/shard_map/ppermute | solution.py:536
  85.8 1.3 collective-permute-start.7
  87.1 0.1 collective-permute-start.4
  87.2 0.5 collective-permute-start.5
  87.7 1.0 fill.4.refs_1_
  88.7 0.0 collective-permute-done.4.refs_2_
  88.7 4.1 %collective-permute-done.5.refs_3_ = f32[96,128]{1,0:T(8,128)S(1)} collective-permute-done((f32[96,128]{1,0:T(8,128)S(1)}, f32[96,128]{1,0:T(8,128)S(1)}, u32[]{:S(2)}, u32[]{:S(2)}) %collective-permute-start.5) | collective-permute-done | bytes 49184 | tf_op jit(solution)/shard_map/ppermute | solution.py:539
  92.8 0.0 collective-permute-done.6.refs_4_
  92.8 1.9 %collective-permute-done.7.refs_5_ = f32[104,384]{1,0:T(8,128)S(1)} collective-permute-done((f32[104,384]{1,0:T(8,128)S(1)}, f32[104,384]{1,0:T(8,128)S(1)}, u32[]{:S(2)}, u32[]{:S(2)}) %collective-permute-start.7) | collective-permute-done | bytes 159776 | tf_op jit(solution)/shard_map/ppermute | solution.py:537
  94.7 2.9 %section.4 = (f32[2,96,384]{2,1,0:T(8,128)S(1)}, f32[16,96,128]{2,1,0:T(8,128)S(1)}, f32[64,1,1536]{2,1,0:T(1,128)S(1)}) custom-call(f32[2,96,384]{2,1,0:T(8,128)S(1)} %get-tuple-element.62.refs_0_, f32[16,96,128]{2,1,0:T(8,128)S(1)} %fill.4.refs_1_, f32[96,128]{1,0:T(8,128)S(1)} %collective-permute-done.4.refs_2_, ...), custom_call_target="tpu_custom_call" | custom-call | tf_op jit(solution)/shard_map/section/pallas_call | solution.py:52
  97.6 20.2 %all_to_all.23.got_ref = f32[64,1,1536]{2,1,0:T(1,128)S(1)} all-to-all(f32[64,1,1536]{2,1,0:T(1,128)S(1)} %get-tuple-element.69), channel_id=1, replica_groups=mesh['grid'=4,'gx'=8,'gy'=8] {'gx','gy'}, dimensions={0} | all-to-all | bytes 786432 | tf_op jit(solution)/shard_map/all_to_all | solution.py:461
  117.8 1.1 rim.5
  119.0 1.4 %collective-permute-start.10 = (f32[104,384]{1,0:T(8,128)S(1)}, f32[104,384]{1,0:T(8,128)S(1)}, u32[]{:S(2)}, u32[]{:S(2)}) collective-permute-start(f32[104,384]{1,0:T(8,128)S(1)} %get-tuple-element.76), channel_id=1, source_target_pairs={{0,1},{1,0},{2,3},{3,2},{4,5},{5,4},{6,7},{7,6},{8,9},{9,8},{10,11... | collective-permute-start | bytes 479240 | tf_op jit(solution)/shard_map/ppermute | solution.py:536
  120.4 1.7 %collective-permute-start.11 = (f32[104,384]{1,0:T(8,128)S(1)}, f32[104,384]{1,0:T(8,128)S(1)}, u32[]{:S(2)}, u32[]{:S(2)}) collective-permute-start(f32[104,384]{1,0:T(8,128)S(1)} %get-tuple-element.77), channel_id=1, source_target_pairs={{1,2},{2,1},{3,4},{4,3},{5,6},{6,5},{7,8},{8,7},{9,10},{10,9},{11,... | collective-permute-start | bytes 479240 | tf_op jit(solution)/shard_map/ppermute | solution.py:537
  122.1 0.0 collective-permute-start.8
  122.1 0.6 collective-permute-start.9
  122.7 1.0 fill.5.refs_1_
  123.7 0.0 collective-permute-done.8.refs_2_
  123.8 4.0 %collective-permute-done.9.refs_3_ = f32[96,128]{1,0:T(8,128)S(1)} collective-permute-done((f32[96,128]{1,0:T(8,128)S(1)}, f32[96,128]{1,0:T(8,128)S(1)}, u32[]{:S(2)}, u32[]{:S(2)}) %collective-permute-start.9) | collective-permute-done | bytes 49184 | tf_op jit(solution)/shard_map/ppermute | solution.py:539
  127.7 0.0 collective-permute-done.10.refs_4_
  127.7 1.7 %collective-permute-done.11.refs_5_ = f32[104,384]{1,0:T(8,128)S(1)} collective-permute-done((f32[104,384]{1,0:T(8,128)S(1)}, f32[104,384]{1,0:T(8,128)S(1)}, u32[]{:S(2)}, u32[]{:S(2)}) %collective-permute-start.11) | collective-permute-done | bytes 159776 | tf_op jit(solution)/shard_map/ppermute | solution.py:537
  129.4 3.2 %section.5 = (f32[96,2,384]{2,1,0:T(2,128)}, f32[96,16,128]{2,1,0:T(8,128)}) custom-call(f32[2,96,384]{2,1,0:T(8,128)S(1)} %get-tuple-element.72.refs_0_, f32[16,96,128]{2,1,0:T(8,128)S(1)} %fill.5.refs_1_, f32[96,128]{1,0:T(8,128)S(1)} %collective-permute-done.8.refs_2_, f32[96,128]{1,0:T(8,128)S(1)} %collective-permute-done.9.refs_3_, ...), custom_call_target="tpu_custom_call" | custom-call | tf_op jit(solution)/shard_map/section/pallas_call | solution.py:52
Async XLA Ops:
  0.6 59.3 %copy-start = (f32[4,2,384]{2,1,0:T(2,128)S(1)}, f32[4,2,384]{2,1,0:T(2,128)}, u32[]{:S(2)}) copy-start(f32[4,2,384]{2,1,0:T(2,128)} %refs_6_.5) | copy-start | bytes 36868
  49.6 8.4 %collective-permute-start.2 = (f32[104,384]{1,0:T(8,128)S(1)}, f32[104,384]{1,0:T(8,128)S(1)}, u32[]{:S(2)}, u32[]{:S(2)}) collective-permute-start(f32[104,384]{1,0:T(8,128)S(1)} %get-tuple-element.54), channel_id=1, source_target_pairs={{0,1},{1,0},{2,3},{3,2},{4,5},{5,4},{6,7},{7,6},{8,9},{9,8},{10,11... | collective-permute-start | bytes 479240 | tf_op jit(solution)/shard_map/ppermute | solution.py:536
  51.0 8.9 %collective-permute-start.3 = (f32[104,384]{1,0:T(8,128)S(1)}, f32[104,384]{1,0:T(8,128)S(1)}, u32[]{:S(2)}, u32[]{:S(2)}) collective-permute-start(f32[104,384]{1,0:T(8,128)S(1)} %get-tuple-element.55), channel_id=1, source_target_pairs={{1,2},{2,1},{3,4},{4,3},{5,6},{6,5},{7,8},{8,7},{9,10},{10,9},{11,... | collective-permute-start | bytes 479240 | tf_op jit(solution)/shard_map/ppermute | solution.py:537
  52.1 2.9 %collective-permute-start = (f32[96,128]{1,0:T(8,128)S(1)}, f32[96,128]{1,0:T(8,128)S(1)}, u32[]{:S(2)}, u32[]{:S(2)}) collective-permute-start(f32[96,128]{1,0:T(8,128)S(1)} %get-tuple-element.52), channel_id=1, source_target_pairs={{0,8},{8,0},{1,9},{9,1},{2,10},{10,2},{3,11},{11,3},{4,12},{12,4},... | collective-permute-start | bytes 147464 | tf_op jit(solution)/shard_map/ppermute | solution.py:538
  52.4 5.6 %collective-permute-start.1 = (f32[96,128]{1,0:T(8,128)S(1)}, f32[96,128]{1,0:T(8,128)S(1)}, u32[]{:S(2)}, u32[]{:S(2)}) collective-permute-start(f32[96,128]{1,0:T(8,128)S(1)} %get-tuple-element.53), channel_id=1, source_target_pairs={{8,16},{16,8},{9,17},{17,9},{10,18},{18,10},{11,19},{19,11},{12,20... | collective-permute-start | bytes 147464 | tf_op jit(solution)/shard_map/ppermute | solution.py:539
  84.4 8.5 %collective-permute-start.6 = (f32[104,384]{1,0:T(8,128)S(1)}, f32[104,384]{1,0:T(8,128)S(1)}, u32[]{:S(2)}, u32[]{:S(2)}) collective-permute-start(f32[104,384]{1,0:T(8,128)S(1)} %get-tuple-element.67), channel_id=1, source_target_pairs={{0,1},{1,0},{2,3},{3,2},{4,5},{5,4},{6,7},{7,6},{8,9},{9,8},{10,11... | collective-permute-start | bytes 479240 | tf_op jit(solution)/shard_map/ppermute | solution.py:536
  85.8 8.9 %collective-permute-start.7 = (f32[104,384]{1,0:T(8,128)S(1)}, f32[104,384]{1,0:T(8,128)S(1)}, u32[]{:S(2)}, u32[]{:S(2)}) collective-permute-start(f32[104,384]{1,0:T(8,128)S(1)} %get-tuple-element.68), channel_id=1, source_target_pairs={{1,2},{2,1},{3,4},{4,3},{5,6},{6,5},{7,8},{8,7},{9,10},{10,9},{11,... | collective-permute-start | bytes 479240 | tf_op jit(solution)/shard_map/ppermute | solution.py:537
  87.1 1.6 %collective-permute-start.4 = (f32[96,128]{1,0:T(8,128)S(1)}, f32[96,128]{1,0:T(8,128)S(1)}, u32[]{:S(2)}, u32[]{:S(2)}) collective-permute-start(f32[96,128]{1,0:T(8,128)S(1)} %get-tuple-element.65), channel_id=1, source_target_pairs={{0,8},{8,0},{1,9},{9,1},{2,10},{10,2},{3,11},{11,3},{4,12},{12,4},... | collective-permute-start | bytes 147464 | tf_op jit(solution)/shard_map/ppermute | solution.py:538
  87.2 5.6 %collective-permute-start.5 = (f32[96,128]{1,0:T(8,128)S(1)}, f32[96,128]{1,0:T(8,128)S(1)}, u32[]{:S(2)}, u32[]{:S(2)}) collective-permute-start(f32[96,128]{1,0:T(8,128)S(1)} %get-tuple-element.66), channel_id=1, source_target_pairs={{8,16},{16,8},{9,17},{17,9},{10,18},{18,10},{11,19},{19,11},{12,20... | collective-permute-start | bytes 147464 | tf_op jit(solution)/shard_map/ppermute | solution.py:539
  119.0 8.8 %collective-permute-start.10 = (f32[104,384]{1,0:T(8,128)S(1)}, f32[104,384]{1,0:T(8,128)S(1)}, u32[]{:S(2)}, u32[]{:S(2)}) collective-permute-start(f32[104,384]{1,0:T(8,128)S(1)} %get-tuple-element.76), channel_id=1, source_target_pairs={{0,1},{1,0},{2,3},{3,2},{4,5},{5,4},{6,7},{7,6},{8,9},{9,8},{10,11... | collective-permute-start | bytes 479240 | tf_op jit(solution)/shard_map/ppermute | solution.py:536
  120.4 9.0 %collective-permute-start.11 = (f32[104,384]{1,0:T(8,128)S(1)}, f32[104,384]{1,0:T(8,128)S(1)}, u32[]{:S(2)}, u32[]{:S(2)}) collective-permute-start(f32[104,384]{1,0:T(8,128)S(1)} %get-tuple-element.77), channel_id=1, source_target_pairs={{1,2},{2,1},{3,4},{4,3},{5,6},{6,5},{7,8},{8,7},{9,10},{10,9},{11,... | collective-permute-start | bytes 479240 | tf_op jit(solution)/shard_map/ppermute | solution.py:537
  122.1 1.6 %collective-permute-start.8 = (f32[96,128]{1,0:T(8,128)S(1)}, f32[96,128]{1,0:T(8,128)S(1)}, u32[]{:S(2)}, u32[]{:S(2)}) collective-permute-start(f32[96,128]{1,0:T(8,128)S(1)} %get-tuple-element.74), channel_id=1, source_target_pairs={{0,8},{8,0},{1,9},{9,1},{2,10},{10,2},{3,11},{11,3},{4,12},{12,4},... | collective-permute-start | bytes 147464 | tf_op jit(solution)/shard_map/ppermute | solution.py:538
  122.1 5.6 %collective-permute-start.9 = (f32[96,128]{1,0:T(8,128)S(1)}, f32[96,128]{1,0:T(8,128)S(1)}, u32[]{:S(2)}, u32[]{:S(2)}) collective-permute-start(f32[96,128]{1,0:T(8,128)S(1)} %get-tuple-element.75), channel_id=1, source_target_pairs={{8,16},{16,8},{9,17},{17,9},{10,18},{18,10},{11,19},{19,11},{12,20... | collective-permute-start | bytes 147464 | tf_op jit(solution)/shard_map/ppermute | solution.py:539

commit v2 on v1

--- a/solution.py
+++ b/solution.py
@@ -44,7 +44,7 @@
     return lax.broadcasted_iota(jnp.int32, shape, dim)
 
 
-def call(kernel, outs, ins, scratch=(), hbm_at=(), name=None):
+def call(kernel, outs, ins, scratch=(), hbm_at=(), outs_in=pltpu.VMEM, name=None):
     def spec(i):
         return pl.BlockSpec(memory_space=pltpu.HBM if i in hbm_at else pltpu.VMEM)
 
@@ -53,7 +53,7 @@
         kernel,
         out_shape=tuple(jax.ShapeDtypeStruct(s, d) for s, d in outs),
         in_specs=[spec(i) for i in range(len(ins))],
-        out_specs=tuple(pl.BlockSpec(memory_space=pltpu.VMEM) for _ in outs),
+        out_specs=tuple(pl.BlockSpec(memory_space=outs_in) for _ in outs),
         scratch_shapes=list(scratch),
         compiler_params=pltpu.CompilerParams(vmem_limit_bytes=VMEM_LIMIT),
         name=name,
@@ -219,12 +219,11 @@
 
 def first_answer_kernel(
     request_ref, deck_hbm, back_hbm, deck_out, back_out, far_ref, near_ref, out_ref,
-    rows_ref, deck_pieces, back_pieces, deck_ref, back_ref, sems,
+    rows_ref, deck_pieces, back_pieces, deck_sems, back_sems,
 ):
     copies = [
-        pltpu.make_async_copy(deck_hbm, deck_ref, sems.at[0]),
-        pltpu.make_async_copy(back_hbm, back_ref, sems.at[1]),
-    ]
+        pltpu.make_async_copy(deck_hbm.at[:, r, :], deck_out.at[r], deck_sems.at[r]) for r in range(DROWS)
+    ] + [pltpu.make_async_copy(back_hbm.at[:, r, :], back_out.at[r], back_sems.at[r]) for r in range(ROWS)]
     for c in copies:
         c.start()
     clear_pieces(deck_pieces, back_pieces)
@@ -232,26 +231,23 @@
     for c in copies:
         c.wait()
     for r in range(DROWS):
-        value = deck_ref[:, r, :]
-        deck_out[r] = value
-        stack_deck(deck_pieces, r, value)
+        stack_deck(deck_pieces, r, deck_out[r])
     for r in range(ROWS):
-        value = back_ref[:, r, :]
-        back_out[r] = value
-        stack_back(back_pieces, r, value)
+        stack_back(back_pieces, r, back_out[r])
     answer(far_ref, near_ref, deck_pieces, back_pieces, out_ref)
 
 
 def rim_kernel(
     got_ref, rim_ref, near_ref, keep_ref, deck_ref, back_ref,
-    got_pieces, deck_out, column_first, column_second, row_first, row_second,
+    got_pieces, deck_out, column_first, column_second, row_first, row_second, plain_ref,
 ):
+    plain_ref[...] = got_ref[:, 0, :]
     lane = iota((MEMBERS, 128), 1)
     for q in range(CAP // 4):
         base = q * 4 * PLANES
-        c0 = got_ref[:, 0, base : base + 128]
-        c1 = got_ref[:, 0, base + 128 : base + 256]
-        c2 = got_ref[:, 0, base + 256 : base + 384]
+        c0 = plain_ref[:, base : base + 128]
+        c1 = plain_ref[:, base + 128 : base + 256]
+        c2 = plain_ref[:, base + 256 : base + 384]
         a0 = jnp.where(lane < 96, c0, 0.0)
         a1 = jnp.where(lane < 32, pltpu.roll(c0, 32, 1), jnp.where(lane < 96, pltpu.roll(c1, 32, 1), 0.0))
         a2 = jnp.where(lane < 64, pltpu.roll(c1, 64, 1), jnp.where(lane < 96, pltpu.roll(c2, 64, 1), 0.0))
@@ -264,8 +260,8 @@
     near = near[0:PLANES] + near[PLANES : 2 * PLANES]
     lane = iota((PLANES, 128), 1)
     column, line, tile = position()
-    odd = lax.rem(tile, 2) > 0
-    odd_line = lax.rem(line, 2) > 0
+    odd = lax.rem(tile, 2) == 0
+    odd_line = lax.rem(line, 2) == 0
     deck = []
     for r in range(DROWS):
         outer = jnp.where(lane >= 126, near[:, r * 128 : (r + 1) * 128], deck_ref[r, :, 256:384])
@@ -378,13 +374,19 @@
         del refs[:2]
     last = section == 2
     if last:
-        deck_out, back_out = refs
+        deck_hbm, back_hbm, deck_out, back_out, deck_sems, back_sems = refs
+        copies = []
+
+        def send(rows, r, whole, sems):
+            copies.append(pltpu.make_async_copy(rows.at[r], whole.at[:, r, :], sems.at[r]))
+            copies[-1].start()
+
     else:
         far_ref, near_ref, deck_out, back_out, answer_out, deck_pieces, back_pieces = refs
         clear_pieces(deck_pieces, back_pieces)
     column, line, tile = position()
-    odd = lax.rem(tile, 2) > 0
-    odd_line = lax.rem(line, 2) > 0
+    odd = lax.rem(tile, 2) == 0
+    odd_line = lax.rem(line, 2) == 0
     west_end = (column > 0).astype(F32)
     east_end = (column < lax.axis_size("gy") - 1).astype(F32)
 
@@ -423,11 +425,10 @@
         base = fields(base_deck, (r,)) if section > 0 else None
         new = update(here, minus, plus, minus_eta, plus_eta, metric, keep_deck, base, section)
         for c in range(3):
-            if last:
-                deck_out[c * SPAN : (c + 1) * SPAN, r, :] = new[c]
-            else:
-                deck_out[r, c * SPAN : (c + 1) * SPAN, :] = new[c]
-        if not last:
+            deck_out[r, c * SPAN : (c + 1) * SPAN, :] = new[c]
+        if last:
+            send(deck_out, r, deck_hbm, deck_sems)
+        else:
             stack_deck(deck_pieces, r, jnp.concatenate(new, axis=0))
     lane = iota((SPAN, COLS), 1)
     for r in range(ROWS):
@@ -443,13 +444,15 @@
         base = fields(base_back, (r,)) if section > 0 else None
         new = update(here, minus, plus, minus_eta, plus_eta, None, keep_ref[r, 0:1, :], base, section)
         for c in range(3):
-            if last:
-                back_out[c * SPAN : (c + 1) * SPAN, r, :] = new[c]
-            else:
-                back_out[r, c * SPAN : (c + 1) * SPAN, :] = new[c]
-        if not last:
+            back_out[r, c * SPAN : (c + 1) * SPAN, :] = new[c]
+        if last:
+            send(back_out, r, back_hbm, back_sems)
+        else:
             stack_back(back_pieces, r, jnp.concatenate(new, axis=0))
-    if not last:
+    if last:
+        for c in copies:
+            c.wait()
+    else:
         answer(far_ref, near_ref, deck_pieces, back_pieces, answer_out)
 
 
@@ -510,9 +513,8 @@
         scratch=[pltpu.VMEM((MEMBERS, 128), F32)]
         + pieces
         + [
-            pltpu.VMEM((PLANES, DROWS, DCOLS), F32),
-            pltpu.VMEM((PLANES, ROWS, COLS), F32),
-            pltpu.SemaphoreType.DMA((2,)),
+            pltpu.SemaphoreType.DMA((DROWS,)),
+            pltpu.SemaphoreType.DMA((ROWS,)),
         ],
         hbm_at=(1, 2),
         name="first_answer",
@@ -531,12 +533,13 @@
                 ((PLANES + 8, DCOLS), F32),
             ],
             [got, rim_map, near_map, rim_keep, deck, back_state],
+            scratch=[pltpu.VMEM((MEMBERS, PACKED), F32)],
             name="rim",
         )
-        row_first = lax.ppermute(row_first, everyone, pairs(1, 0, True))
-        row_second = lax.ppermute(row_second, everyone, pairs(1, 1, True))
-        column_first = lax.ppermute(column_first, everyone, pairs(across_y, 0))
-        column_second = lax.ppermute(column_second, everyone, pairs(across_y, 1))
+        row_first = lax.ppermute(row_first, everyone, pairs(1, 1, True))
+        row_second = lax.ppermute(row_second, everyone, pairs(1, 0, True))
+        column_first = lax.ppermute(column_first, everyone, pairs(across_y, 1))
+        column_second = lax.ppermute(column_second, everyone, pairs(across_y, 0))
         if section == 0:
             back_state, fill_map, keep = call(
                 first_fill_kernel,
@@ -573,6 +576,13 @@
                 kernel,
                 [((PLANES, DROWS, DCOLS), F32), ((PLANES, ROWS, COLS), F32)],
                 ins,
+                scratch=[
+                    pltpu.VMEM((DROWS, PLANES, DCOLS), F32),
+                    pltpu.VMEM((ROWS, PLANES, COLS), F32),
+                    pltpu.SemaphoreType.DMA((DROWS,)),
+                    pltpu.SemaphoreType.DMA((ROWS,)),
+                ],
+                outs_in=pl.ANY,
                 name="section",
             )
     return deck.reshape(deck_fields.shape), back_state.reshape(back_fields.shape)

time: 133 us -> 128 us (0.962)
  Pallas kernels: 23.9 us -> 20.3 us
  waiting for transfers between devices: 16.7 us -> 14.6 us
    pallas_call x11, Pallas kernels: 23.9 us -> 20.3 us  [call(): pl.pallas_call(kernel, out_shape=tuple((jax.ShapeDtypeStruct(s, d) for s,...]
    ppermute x12, waiting for transfers between devices: 16.7 us -> 14.6 us  [the longest x3 14.6 us: local(): column_first = lax.ppermute(column_first, everyone, pairs(across_y, 1))]
  transfers between devices with their start and end apart: 12 -> 12, of which waited for: 6 -> 3; matrix products, arithmetic and copies ran while one was open for 0% -> 0% of each run, Pallas kernels for 3% -> 3%
where the time goes in v2:
time: 128 us; the launch traced here: 127 us
  blocking collectives  82 us (64%)
  Pallas kernels  20.3 us (16%)
  waiting for transfers between devices  14.6 us (11%)
  starting transfers between devices  9.57 us (7%)
    all_to_all x4, blocking collectives, exchange(): return lax.all_to_all(x, group, split_axis=0, concat_axis=0, tiled=True)  82 us
    pallas_call x11, Pallas kernels, call(): pl.pallas_call(kernel, out_shape=tuple((jax.ShapeDtypeStruct(s, d) for s,...  20.3 us
    ppermute x3, waiting for transfers between devices, local(): column_first = lax.ppermute(column_first, everyone, pairs(across_y, 1))  14.6 us
    ppermute x3, starting transfers between devices, local(): row_first = lax.ppermute(row_first, everyone, pairs(1, 1, True))  5.18 us
  transfers between devices with their start and end apart: 12, of which 3 were waited for; matrix products, arithmetic and copies ran while one was open for 0% of the time, Pallas kernels for 3%

profile of v2, /device:TPU:8, one launch (start us, length us, event | category | flops | bytes accessed | tf_op | source)
XLA Modules:
  0.0 127.3 jit_solution(2867244280904459519)
XLA Ops:
  0.6 0.0 copy-start
  0.6 1.8 %route.1 = (f32[64,1,128]{2,1,0:T(1,128)S(1)}, f32[64,48]{1,0:T(8,128)S(1)}, bf16[1024,384]{1,0:T(8,128)(2,1)S(1)}, bf16[256,256]{1,0:T(8,128)(2,1)S(1)}, f32[3,8,128]{2,1,0:T(8,128)S(1)}) custom-call(s32[1,512]{1,0:T(1,128)} %bitcast.11, s32[4,512]{1,0:T(4,128)} %bitcast.10, s32[1,508]{1,0:T(1,128)} %cells_hbm.1), custom_call_target="tpu_custom_call" | custom-call | tf_op jit(solution)/shard_map/route/pallas_call | solution.py:52
  2.4 21.3 %all_to_all.20.request_ref = f32[64,1,128]{2,1,0:T(1,128)S(1)} all-to-all(f32[64,1,128]{2,1,0:T(1,128)S(1)} %get-tuple-element.41), channel_id=1, replica_groups=mesh['grid'=4,'gx'=8,'gy'=8] {'gx','gy'}, dimensions={0} | all-to-all | bytes 65536 | tf_op jit(solution)/shard_map/all_to_all | solution.py:464
  23.7 2.6 %first_answer.1 = (f32[2,96,384]{2,1,0:T(8,128)S(1)}, f32[16,96,128]{2,1,0:T(8,128)S(1)}, bf16[1024,768]{1,0:T(8,128)(2,1)S(1)}, bf16[256,2048]{1,0:T(8,128)(2,1)S(1)}, f32[64,1,1536]{2,1,0:T(1,128)S(1)}) custom-call(f32[64,1,128]{2,1,0:T(1,128)S(1)} %all_to_all.20.request_ref, f32[96,2,384]{2,1,0:T(2,128)} %bitcast.9, f32[96,16,128]{2,1,0:T(8,128)} %bitcast.8), custom_call_target="tpu_custom_call" | custom-call | tf_op jit(solution)/shard_map/first_answer/pallas_call | solution.py:52
  26.3 19.2 %all_to_all.21.got_ref = f32[64,1,1536]{2,1,0:T(1,128)S(1)} all-to-all(f32[64,1,1536]{2,1,0:T(1,128)S(1)} %get-tuple-element.42), channel_id=1, replica_groups=mesh['grid'=4,'gx'=8,'gy'=8] {'gx','gy'}, dimensions={0} | all-to-all | bytes 786432 | tf_op jit(solution)/shard_map/all_to_all | solution.py:464
  45.5 1.1 rim.3
  46.6 1.6 %collective-permute-start.2 = (f32[104,384]{1,0:T(8,128)S(1)}, f32[104,384]{1,0:T(8,128)S(1)}, u32[]{:S(2)}, u32[]{:S(2)}) collective-permute-start(f32[104,384]{1,0:T(8,128)S(1)} %get-tuple-element.54), channel_id=1, source_target_pairs={{1,2},{2,1},{3,4},{4,3},{5,6},{6,5},{7,8},{8,7},{9,10},{10,9},{11,... | collective-permute-start | bytes 479240 | tf_op jit(solution)/shard_map/ppermute | solution.py:539
  48.2 0.8 collective-permute-start.3
  49.0 0.3 collective-permute-start
  49.3 0.5 collective-permute-start.1
  49.8 2.3 %fill.3 = (f32[16,96,128]{2,1,0:T(8,128)S(1)}, bf16[1024,2048]{1,0:T(8,128)(2,1)S(1)}, f32[16,8,128]{2,1,0:T(8,128)S(1)}) custom-call(bf16[192,1024]{1,0:T(8,128)(2,1)S(1)} %get-tuple-element.49.got_pieces, f32[64,48]{1,0:T(8,128)S(1)} %get-tuple-element.50.local_ref, f32[16,96,128]{2,1,0:T(8,128)S(1)} %get-tuple-element.47.back_ref), custom_call_target="tpu_custom_call" | custom-call | tf_op jit(solution)/shard_map/fill/pallas_call | solution.py:52
  52.1 4.0 %collective-permute-done.refs_2_ = f32[96,128]{1,0:T(8,128)S(1)} collective-permute-done((f32[96,128]{1,0:T(8,128)S(1)}, f32[96,128]{1,0:T(8,128)S(1)}, u32[]{:S(2)}, u32[]{:S(2)}) %collective-permute-start) | collective-permute-done | bytes 49184 | tf_op jit(solution)/shard_map/ppermute | solution.py:541
  56.1 0.0 collective-permute-done.1.refs_3_
  56.1 0.0 collective-permute-done.2.refs_4_
  56.1 0.0 collective-permute-done.3.refs_5_
  56.1 0.0 copy-done
  56.1 2.8 %section.3 = (f32[2,96,384]{2,1,0:T(8,128)S(1)}, f32[16,96,128]{2,1,0:T(8,128)S(1)}, f32[64,1,1536]{2,1,0:T(1,128)S(1)}) custom-call(f32[2,96,384]{2,1,0:T(8,128)S(1)} %get-tuple-element.48.refs_0_.refs_8_, f32[16,96,128]{2,1,0:T(8,128)S(1)} %get-tuple-element.51.refs_1_.refs_9_, f32[96,128]{1,0:T(8,128)S(1)} %collective-permute-done.refs_2_, ...), custom_call_target="tpu_custom_call" | custom-call | tf_op jit(solution)/shard_map/section/pallas_call | solution.py:52
  58.9 20.9 %all_to_all.22.got_ref = f32[64,1,1536]{2,1,0:T(1,128)S(1)} all-to-all(f32[64,1,1536]{2,1,0:T(1,128)S(1)} %get-tuple-element.59), channel_id=1, replica_groups=mesh['grid'=4,'gx'=8,'gy'=8] {'gx','gy'}, dimensions={0} | all-to-all | bytes 786432 | tf_op jit(solution)/shard_map/all_to_all | solution.py:464
  79.8 1.1 rim.4
  80.9 1.7 %collective-permute-start.6 = (f32[104,384]{1,0:T(8,128)S(1)}, f32[104,384]{1,0:T(8,128)S(1)}, u32[]{:S(2)}, u32[]{:S(2)}) collective-permute-start(f32[104,384]{1,0:T(8,128)S(1)} %get-tuple-element.67), channel_id=1, source_target_pairs={{1,2},{2,1},{3,4},{4,3},{5,6},{6,5},{7,8},{8,7},{9,10},{10,9},{11,... | collective-permute-start | bytes 479240 | tf_op jit(solution)/shard_map/ppermute | solution.py:539
  82.5 0.8 collective-permute-start.7
  83.3 0.3 collective-permute-start.4
  83.6 0.5 collective-permute-start.5
  84.1 1.0 fill.4.refs_1_
  85.1 5.3 %collective-permute-done.4.refs_2_ = f32[96,128]{1,0:T(8,128)S(1)} collective-permute-done((f32[96,128]{1,0:T(8,128)S(1)}, f32[96,128]{1,0:T(8,128)S(1)}, u32[]{:S(2)}, u32[]{:S(2)}) %collective-permute-start.4) | collective-permute-done | bytes 49184 | tf_op jit(solution)/shard_map/ppermute | solution.py:541
  90.4 0.0 collective-permute-done.5.refs_3_
  90.4 0.0 collective-permute-done.6.refs_4_
  90.4 0.0 collective-permute-done.7.refs_5_
  90.4 2.9 %section.4 = (f32[2,96,384]{2,1,0:T(8,128)S(1)}, f32[16,96,128]{2,1,0:T(8,128)S(1)}, f32[64,1,1536]{2,1,0:T(1,128)S(1)}) custom-call(f32[2,96,384]{2,1,0:T(8,128)S(1)} %get-tuple-element.62.refs_0_, f32[16,96,128]{2,1,0:T(8,128)S(1)} %fill.4.refs_1_, f32[96,128]{1,0:T(8,128)S(1)} %collective-permute-done.4.refs_2_, ...), custom_call_target="tpu_custom_call" | custom-call | tf_op jit(solution)/shard_map/section/pallas_call | solution.py:52
  93.3 20.6 %all_to_all.23.got_ref = f32[64,1,1536]{2,1,0:T(1,128)S(1)} all-to-all(f32[64,1,1536]{2,1,0:T(1,128)S(1)} %get-tuple-element.69), channel_id=1, replica_groups=mesh['grid'=4,'gx'=8,'gy'=8] {'gx','gy'}, dimensions={0} | all-to-all | bytes 786432 | tf_op jit(solution)/shard_map/all_to_all | solution.py:464
  113.9 1.1 rim.5
  115.0 1.9 %collective-permute-start.10 = (f32[104,384]{1,0:T(8,128)S(1)}, f32[104,384]{1,0:T(8,128)S(1)}, u32[]{:S(2)}, u32[]{:S(2)}) collective-permute-start(f32[104,384]{1,0:T(8,128)S(1)} %get-tuple-element.76), channel_id=1, source_target_pairs={{1,2},{2,1},{3,4},{4,3},{5,6},{6,5},{7,8},{8,7},{9,10},{10,9},{11,... | collective-permute-start | bytes 479240 | tf_op jit(solution)/shard_map/ppermute | solution.py:539
  116.9 0.5 collective-permute-start.11
  117.4 0.5 collective-permute-start.8
  117.9 0.2 collective-permute-start.9
  118.2 1.0 fill.5.refs_1_
  119.2 5.3 %collective-permute-done.8.refs_2_ = f32[96,128]{1,0:T(8,128)S(1)} collective-permute-done((f32[96,128]{1,0:T(8,128)S(1)}, f32[96,128]{1,0:T(8,128)S(1)}, u32[]{:S(2)}, u32[]{:S(2)}) %collective-permute-start.8) | collective-permute-done | bytes 49184 | tf_op jit(solution)/shard_map/ppermute | solution.py:541
  124.5 0.0 collective-permute-done.9.refs_3_
  124.5 0.0 collective-permute-done.10.refs_4_
  124.5 0.0 collective-permute-done.11.refs_5_
  124.5 2.7 %section.5 = (f32[96,2,384]{2,1,0:T(2,128)}, f32[96,16,128]{2,1,0:T(8,128)}) custom-call(f32[2,96,384]{2,1,0:T(8,128)S(1)} %get-tuple-element.72.refs_0_, f32[16,96,128]{2,1,0:T(8,128)S(1)} %fill.5.refs_1_, f32[96,128]{1,0:T(8,128)S(1)} %collective-permute-done.8.refs_2_, f32[96,128]{1,0:T(8,128)S(1)} %collective-permute-done.9.refs_3_, ...), custom_call_target="tpu_custom_call" | custom-call | tf_op jit(solution)/shard_map/section/pallas_call | solution.py:52
Async XLA Ops:
  0.6 55.5 %copy-start = (f32[4,2,384]{2,1,0:T(2,128)S(1)}, f32[4,2,384]{2,1,0:T(2,128)}, u32[]{:S(2)}) copy-start(f32[4,2,384]{2,1,0:T(2,128)} %refs_6_.5) | copy-start | bytes 36868
  46.6 9.5 %collective-permute-start.2 = (f32[104,384]{1,0:T(8,128)S(1)}, f32[104,384]{1,0:T(8,128)S(1)}, u32[]{:S(2)}, u32[]{:S(2)}) collective-permute-start(f32[104,384]{1,0:T(8,128)S(1)} %get-tuple-element.54), channel_id=1, source_target_pairs={{1,2},{2,1},{3,4},{4,3},{5,6},{6,5},{7,8},{8,7},{9,10},{10,9},{11,... | collective-permute-start | bytes 479240 | tf_op jit(solution)/shard_map/ppermute | solution.py:539
  48.2 7.9 %collective-permute-start.3 = (f32[104,384]{1,0:T(8,128)S(1)}, f32[104,384]{1,0:T(8,128)S(1)}, u32[]{:S(2)}, u32[]{:S(2)}) collective-permute-start(f32[104,384]{1,0:T(8,128)S(1)} %get-tuple-element.55), channel_id=1, source_target_pairs={{0,1},{1,0},{2,3},{3,2},{4,5},{5,4},{6,7},{7,6},{8,9},{9,8},{10,11... | collective-permute-start | bytes 479240 | tf_op jit(solution)/shard_map/ppermute | solution.py:540
  49.0 7.1 %collective-permute-start = (f32[96,128]{1,0:T(8,128)S(1)}, f32[96,128]{1,0:T(8,128)S(1)}, u32[]{:S(2)}, u32[]{:S(2)}) collective-permute-start(f32[96,128]{1,0:T(8,128)S(1)} %get-tuple-element.52), channel_id=1, source_target_pairs={{8,16},{16,8},{9,17},{17,9},{10,18},{18,10},{11,19},{19,11},{12,20... | collective-permute-start | bytes 147464 | tf_op jit(solution)/shard_map/ppermute | solution.py:541
  49.3 6.9 %collective-permute-start.1 = (f32[96,128]{1,0:T(8,128)S(1)}, f32[96,128]{1,0:T(8,128)S(1)}, u32[]{:S(2)}, u32[]{:S(2)}) collective-permute-start(f32[96,128]{1,0:T(8,128)S(1)} %get-tuple-element.53), channel_id=1, source_target_pairs={{0,8},{8,0},{1,9},{9,1},{2,10},{10,2},{3,11},{11,3},{4,12},{12,4},... | collective-permute-start | bytes 147464 | tf_op jit(solution)/shard_map/ppermute | solution.py:542
  80.9 9.5 %collective-permute-start.6 = (f32[104,384]{1,0:T(8,128)S(1)}, f32[104,384]{1,0:T(8,128)S(1)}, u32[]{:S(2)}, u32[]{:S(2)}) collective-permute-start(f32[104,384]{1,0:T(8,128)S(1)} %get-tuple-element.67), channel_id=1, source_target_pairs={{1,2},{2,1},{3,4},{4,3},{5,6},{6,5},{7,8},{8,7},{9,10},{10,9},{11,... | collective-permute-start | bytes 479240 | tf_op jit(solution)/shard_map/ppermute | solution.py:539
  82.5 7.9 %collective-permute-start.7 = (f32[104,384]{1,0:T(8,128)S(1)}, f32[104,384]{1,0:T(8,128)S(1)}, u32[]{:S(2)}, u32[]{:S(2)}) collective-permute-start(f32[104,384]{1,0:T(8,128)S(1)} %get-tuple-element.68), channel_id=1, source_target_pairs={{0,1},{1,0},{2,3},{3,2},{4,5},{5,4},{6,7},{7,6},{8,9},{9,8},{10,11... | collective-permute-start | bytes 479240 | tf_op jit(solution)/shard_map/ppermute | solution.py:540
  83.3 7.1 %collective-permute-start.4 = (f32[96,128]{1,0:T(8,128)S(1)}, f32[96,128]{1,0:T(8,128)S(1)}, u32[]{:S(2)}, u32[]{:S(2)}) collective-permute-start(f32[96,128]{1,0:T(8,128)S(1)} %get-tuple-element.65), channel_id=1, source_target_pairs={{8,16},{16,8},{9,17},{17,9},{10,18},{18,10},{11,19},{19,11},{12,20... | collective-permute-start | bytes 147464 | tf_op jit(solution)/shard_map/ppermute | solution.py:541
  83.6 6.8 %collective-permute-start.5 = (f32[96,128]{1,0:T(8,128)S(1)}, f32[96,128]{1,0:T(8,128)S(1)}, u32[]{:S(2)}, u32[]{:S(2)}) collective-permute-start(f32[96,128]{1,0:T(8,128)S(1)} %get-tuple-element.66), channel_id=1, source_target_pairs={{0,8},{8,0},{1,9},{9,1},{2,10},{10,2},{3,11},{11,3},{4,12},{12,4},... | collective-permute-start | bytes 147464 | tf_op jit(solution)/shard_map/ppermute | solution.py:542
  115.0 9.5 %collective-permute-start.10 = (f32[104,384]{1,0:T(8,128)S(1)}, f32[104,384]{1,0:T(8,128)S(1)}, u32[]{:S(2)}, u32[]{:S(2)}) collective-permute-start(f32[104,384]{1,0:T(8,128)S(1)} %get-tuple-element.76), channel_id=1, source_target_pairs={{1,2},{2,1},{3,4},{4,3},{5,6},{6,5},{7,8},{8,7},{9,10},{10,9},{11,... | collective-permute-start | bytes 479240 | tf_op jit(solution)/shard_map/ppermute | solution.py:539
  116.9 7.6 %collective-permute-start.11 = (f32[104,384]{1,0:T(8,128)S(1)}, f32[104,384]{1,0:T(8,128)S(1)}, u32[]{:S(2)}, u32[]{:S(2)}) collective-permute-start(f32[104,384]{1,0:T(8,128)S(1)} %get-tuple-element.77), channel_id=1, source_target_pairs={{0,1},{1,0},{2,3},{3,2},{4,5},{5,4},{6,7},{7,6},{8,9},{9,8},{10,11... | collective-permute-start | bytes 479240 | tf_op jit(solution)/shard_map/ppermute | solution.py:540
  117.4 7.1 %collective-permute-start.8 = (f32[96,128]{1,0:T(8,128)S(1)}, f32[96,128]{1,0:T(8,128)S(1)}, u32[]{:S(2)}, u32[]{:S(2)}) collective-permute-start(f32[96,128]{1,0:T(8,128)S(1)} %get-tuple-element.74), channel_id=1, source_target_pairs={{8,16},{16,8},{9,17},{17,9},{10,18},{18,10},{11,19},{19,11},{12,20... | collective-permute-start | bytes 147464 | tf_op jit(solution)/shard_map/ppermute | solution.py:541
  117.9 6.5 %collective-permute-start.9 = (f32[96,128]{1,0:T(8,128)S(1)}, f32[96,128]{1,0:T(8,128)S(1)}, u32[]{:S(2)}, u32[]{:S(2)}) collective-permute-start(f32[96,128]{1,0:T(8,128)S(1)} %get-tuple-element.75), channel_id=1, source_target_pairs={{0,8},{8,0},{1,9},{9,1},{2,10},{10,2},{3,11},{11,3},{4,12},{12,4},... | collective-permute-start | bytes 147464 | tf_op jit(solution)/shard_map/ppermute | solution.py:542

commit v3 on v2

--- a/solution.py
+++ b/solution.py
@@ -71,6 +71,7 @@
     for c in copies:
         c.wait()
     donors = donors_ref[...]
+    donors = (donors & 7) * 8 + (donors >> 3)
     member = (iota((MEMBERS, FRINGE), 0) == donors).astype(F32)
     before = (iota((FRINGE, FRINGE), 0) < iota((FRINGE, FRINGE), 1)).astype(BF16)
     member_b = member.astype(BF16)
@@ -340,7 +341,8 @@
         d_xi.append(a)
         d_eta.append(b)
         d_span.append(s)
-    viscosity = (SMAGORINSKY * step) * jnp.sqrt(1.0 + 0.25 * strain)
+    stretched = 1.0 + 0.25 * strain
+    viscosity = (SMAGORINSKY * step) * (stretched * lax.rsqrt(stretched))
     half = 0.5 * step
     if metric is None:
         speed_xi, speed_eta = half * here[0], half * here[1]
@@ -457,7 +459,7 @@
 
 
 def local(deck_fields, back_fields, metrics, donors, stencil, fringe_cells):
-    group = ("gx", "gy")
+    group = ("gy", "gx")
     everyone = ("grid", "gx", "gy")
 
     def exchange(x):

time: 128 us -> 126 us (0.984)
  starting transfers between devices: 9.57 us -> 11.9 us
  waiting for transfers between devices: 14.6 us -> 12.4 us
  blocking collectives: 82 us -> 80.6 us
    ppermute x3, starting transfers between devices: 2.02 us -> 4.32 us  [local(): row_second = lax.ppermute(row_second, everyone, pairs(1, 0, True))]
    ppermute x3, waiting for transfers between devices: 14.6 us -> 12.4 us  [local(): column_first = lax.ppermute(column_first, everyone, pairs(across_y, 1))]
    all_to_all x4, blocking collectives: 82 us -> 80.6 us  [exchange(): return lax.all_to_all(x, group, split_axis=0, concat_axis=0, tiled=True)]
where the time goes in v3:
time: 126 us
  blocking collectives  80.6 us (64%)
  Pallas kernels  20.1 us (16%)
  waiting for transfers between devices  12.4 us (10%)
  starting transfers between devices  11.9 us (9%)
    all_to_all x4, blocking collectives, exchange(): return lax.all_to_all(x, group, split_axis=0, concat_axis=0, tiled=True)  80.6 us
    pallas_call x11, Pallas kernels, call(): pl.pallas_call(kernel, out_shape=tuple((jax.ShapeDtypeStruct(s, d) for s,...  20.1 us
    ppermute x3, waiting for transfers between devices, local(): column_first = lax.ppermute(column_first, everyone, pairs(across_y, 1))  12.4 us
    ppermute x3, starting transfers between devices, local(): row_first = lax.ppermute(row_first, everyone, pairs(1, 1, True))  5.6 us
    ppermute x3, starting transfers between devices, local(): row_second = lax.ppermute(row_second, everyone, pairs(1, 0, True))  4.32 us
  transfers between devices with their start and end apart: 12, of which 3 were waited for; matrix products, arithmetic and copies ran while one was open for 0% of the time, Pallas kernels for 3%

profile of v3, /device:TPU:8, one launch (start us, length us, event | category | flops | bytes accessed | tf_op | source)
XLA Modules:
  0.0 125.9 jit_solution(8726375937522536759)
XLA Ops:
  0.6 0.0 copy-start
  0.6 1.8 %route.1 = (f32[64,1,128]{2,1,0:T(1,128)S(1)}, f32[64,48]{1,0:T(8,128)S(1)}, bf16[1024,384]{1,0:T(8,128)(2,1)S(1)}, bf16[256,256]{1,0:T(8,128)(2,1)S(1)}, f32[3,8,128]{2,1,0:T(8,128)S(1)}) custom-call(s32[1,512]{1,0:T(1,128)} %bitcast.11, s32[4,512]{1,0:T(4,128)} %bitcast.10, s32[1,508]{1,0:T(1,128)} %cells_hbm.1), custom_call_target="tpu_custom_call" | custom-call | tf_op jit(solution)/shard_map/route/pallas_call | solution.py:52
  2.4 21.3 %all_to_all.20.request_ref = f32[64,1,128]{2,1,0:T(1,128)S(1)} all-to-all(f32[64,1,128]{2,1,0:T(1,128)S(1)} %get-tuple-element.41), channel_id=1, replica_groups=mesh['grid'=4,'gx'=8,'gy'=8] {'gy','gx'}, dimensions={0} | all-to-all | bytes 65536 | tf_op jit(solution)/shard_map/all_to_all | solution.py:466
  23.7 2.6 %first_answer.1 = (f32[2,96,384]{2,1,0:T(8,128)S(1)}, f32[16,96,128]{2,1,0:T(8,128)S(1)}, bf16[1024,768]{1,0:T(8,128)(2,1)S(1)}, bf16[256,2048]{1,0:T(8,128)(2,1)S(1)}, f32[64,1,1536]{2,1,0:T(1,128)S(1)}) custom-call(f32[64,1,128]{2,1,0:T(1,128)S(1)} %all_to_all.20.request_ref, f32[96,2,384]{2,1,0:T(2,128)} %bitcast.9, f32[96,16,128]{2,1,0:T(8,128)} %bitcast.8), custom_call_target="tpu_custom_call" | custom-call | tf_op jit(solution)/shard_map/first_answer/pallas_call | solution.py:52
  26.3 18.7 %all_to_all.21.got_ref = f32[64,1,1536]{2,1,0:T(1,128)S(1)} all-to-all(f32[64,1,1536]{2,1,0:T(1,128)S(1)} %get-tuple-element.42), channel_id=1, replica_groups=mesh['grid'=4,'gx'=8,'gy'=8] {'gy','gx'}, dimensions={0} | all-to-all | bytes 786432 | tf_op jit(solution)/shard_map/all_to_all | solution.py:466
  45.1 1.1 rim.3
  46.2 1.7 %collective-permute-start.2 = (f32[104,384]{1,0:T(8,128)S(1)}, f32[104,384]{1,0:T(8,128)S(1)}, u32[]{:S(2)}, u32[]{:S(2)}) collective-permute-start(f32[104,384]{1,0:T(8,128)S(1)} %get-tuple-element.54), channel_id=1, source_target_pairs={{1,2},{2,1},{3,4},{4,3},{5,6},{6,5},{7,8},{8,7},{9,10},{10,9},{11,... | collective-permute-start | bytes 479240 | tf_op jit(solution)/shard_map/ppermute | solution.py:541
  47.9 1.6 %collective-permute-start.3 = (f32[104,384]{1,0:T(8,128)S(1)}, f32[104,384]{1,0:T(8,128)S(1)}, u32[]{:S(2)}, u32[]{:S(2)}) collective-permute-start(f32[104,384]{1,0:T(8,128)S(1)} %get-tuple-element.55), channel_id=1, source_target_pairs={{0,1},{1,0},{2,3},{3,2},{4,5},{5,4},{6,7},{7,6},{8,9},{9,8},{10,11... | collective-permute-start | bytes 479240 | tf_op jit(solution)/shard_map/ppermute | solution.py:542
  49.4 0.0 collective-permute-start
  49.4 0.7 collective-permute-start.1
  50.1 2.3 %fill.3 = (f32[16,96,128]{2,1,0:T(8,128)S(1)}, bf16[1024,2048]{1,0:T(8,128)(2,1)S(1)}, f32[16,8,128]{2,1,0:T(8,128)S(1)}) custom-call(bf16[192,1024]{1,0:T(8,128)(2,1)S(1)} %get-tuple-element.49.got_pieces, f32[64,48]{1,0:T(8,128)S(1)} %get-tuple-element.50.local_ref, f32[16,96,128]{2,1,0:T(8,128)S(1)} %get-tuple-element.47.back_ref), custom_call_target="tpu_custom_call" | custom-call | tf_op jit(solution)/shard_map/fill/pallas_call | solution.py:52
  52.4 3.3 %collective-permute-done.refs_2_ = f32[96,128]{1,0:T(8,128)S(1)} collective-permute-done((f32[96,128]{1,0:T(8,128)S(1)}, f32[96,128]{1,0:T(8,128)S(1)}, u32[]{:S(2)}, u32[]{:S(2)}) %collective-permute-start) | collective-permute-done | bytes 49184 | tf_op jit(solution)/shard_map/ppermute | solution.py:543
  55.7 0.0 collective-permute-done.1.refs_3_
  55.7 0.0 collective-permute-done.2.refs_4_
  55.7 0.0 collective-permute-done.3.refs_5_
  55.7 0.0 copy-done
  55.7 2.7 %section.3 = (f32[2,96,384]{2,1,0:T(8,128)S(1)}, f32[16,96,128]{2,1,0:T(8,128)S(1)}, f32[64,1,1536]{2,1,0:T(1,128)S(1)}) custom-call(f32[2,96,384]{2,1,0:T(8,128)S(1)} %get-tuple-element.48.refs_0_.refs_8_, f32[16,96,128]{2,1,0:T(8,128)S(1)} %get-tuple-element.51.refs_1_.refs_9_, f32[96,128]{1,0:T(8,128)S(1)} %collective-permute-done.refs_2_, ...), custom_call_target="tpu_custom_call" | custom-call | tf_op jit(solution)/shard_map/section/pallas_call | solution.py:52
  58.4 20.4 %all_to_all.22.got_ref = f32[64,1,1536]{2,1,0:T(1,128)S(1)} all-to-all(f32[64,1,1536]{2,1,0:T(1,128)S(1)} %get-tuple-element.59), channel_id=1, replica_groups=mesh['grid'=4,'gx'=8,'gy'=8] {'gy','gx'}, dimensions={0} | all-to-all | bytes 786432 | tf_op jit(solution)/shard_map/all_to_all | solution.py:466
  78.8 1.1 rim.4
  79.9 1.8 %collective-permute-start.6 = (f32[104,384]{1,0:T(8,128)S(1)}, f32[104,384]{1,0:T(8,128)S(1)}, u32[]{:S(2)}, u32[]{:S(2)}) collective-permute-start(f32[104,384]{1,0:T(8,128)S(1)} %get-tuple-element.67), channel_id=1, source_target_pairs={{1,2},{2,1},{3,4},{4,3},{5,6},{6,5},{7,8},{8,7},{9,10},{10,9},{11,... | collective-permute-start | bytes 479240 | tf_op jit(solution)/shard_map/ppermute | solution.py:541
  81.8 1.5 %collective-permute-start.7 = (f32[104,384]{1,0:T(8,128)S(1)}, f32[104,384]{1,0:T(8,128)S(1)}, u32[]{:S(2)}, u32[]{:S(2)}) collective-permute-start(f32[104,384]{1,0:T(8,128)S(1)} %get-tuple-element.68), channel_id=1, source_target_pairs={{0,1},{1,0},{2,3},{3,2},{4,5},{5,4},{6,7},{7,6},{8,9},{9,8},{10,11... | collective-permute-start | bytes 479240 | tf_op jit(solution)/shard_map/ppermute | solution.py:542
  83.3 0.0 collective-permute-start.4
  83.3 0.6 collective-permute-start.5
  83.9 1.0 fill.4.refs_1_
  84.9 4.5 %collective-permute-done.4.refs_2_ = f32[96,128]{1,0:T(8,128)S(1)} collective-permute-done((f32[96,128]{1,0:T(8,128)S(1)}, f32[96,128]{1,0:T(8,128)S(1)}, u32[]{:S(2)}, u32[]{:S(2)}) %collective-permute-start.4) | collective-permute-done | bytes 49184 | tf_op jit(solution)/shard_map/ppermute | solution.py:543
  89.4 0.0 collective-permute-done.5.refs_3_
  89.4 0.0 collective-permute-done.6.refs_4_
  89.4 0.0 collective-permute-done.7.refs_5_
  89.4 2.9 %section.4 = (f32[2,96,384]{2,1,0:T(8,128)S(1)}, f32[16,96,128]{2,1,0:T(8,128)S(1)}, f32[64,1,1536]{2,1,0:T(1,128)S(1)}) custom-call(f32[2,96,384]{2,1,0:T(8,128)S(1)} %get-tuple-element.62.refs_0_, f32[16,96,128]{2,1,0:T(8,128)S(1)} %fill.4.refs_1_, f32[96,128]{1,0:T(8,128)S(1)} %collective-permute-done.4.refs_2_, ...), custom_call_target="tpu_custom_call" | custom-call | tf_op jit(solution)/shard_map/section/pallas_call | solution.py:52
  92.3 20.1 %all_to_all.23.got_ref = f32[64,1,1536]{2,1,0:T(1,128)S(1)} all-to-all(f32[64,1,1536]{2,1,0:T(1,128)S(1)} %get-tuple-element.69), channel_id=1, replica_groups=mesh['grid'=4,'gx'=8,'gy'=8] {'gy','gx'}, dimensions={0} | all-to-all | bytes 786432 | tf_op jit(solution)/shard_map/all_to_all | solution.py:466
  112.4 1.1 rim.5
  113.5 2.1 %collective-permute-start.10 = (f32[104,384]{1,0:T(8,128)S(1)}, f32[104,384]{1,0:T(8,128)S(1)}, u32[]{:S(2)}, u32[]{:S(2)}) collective-permute-start(f32[104,384]{1,0:T(8,128)S(1)} %get-tuple-element.76), channel_id=1, source_target_pairs={{1,2},{2,1},{3,4},{4,3},{5,6},{6,5},{7,8},{8,7},{9,10},{10,9},{11,... | collective-permute-start | bytes 479240 | tf_op jit(solution)/shard_map/ppermute | solution.py:541
  115.6 1.3 %collective-permute-start.11 = (f32[104,384]{1,0:T(8,128)S(1)}, f32[104,384]{1,0:T(8,128)S(1)}, u32[]{:S(2)}, u32[]{:S(2)}) collective-permute-start(f32[104,384]{1,0:T(8,128)S(1)} %get-tuple-element.77), channel_id=1, source_target_pairs={{0,1},{1,0},{2,3},{3,2},{4,5},{5,4},{6,7},{7,6},{8,9},{9,8},{10,11... | collective-permute-start | bytes 479240 | tf_op jit(solution)/shard_map/ppermute | solution.py:542
  116.9 0.0 collective-permute-start.8
  116.9 0.6 collective-permute-start.9
  117.5 1.0 fill.5.refs_1_
  118.5 4.6 %collective-permute-done.8.refs_2_ = f32[96,128]{1,0:T(8,128)S(1)} collective-permute-done((f32[96,128]{1,0:T(8,128)S(1)}, f32[96,128]{1,0:T(8,128)S(1)}, u32[]{:S(2)}, u32[]{:S(2)}) %collective-permute-start.8) | collective-permute-done | bytes 49184 | tf_op jit(solution)/shard_map/ppermute | solution.py:543
  123.1 0.0 collective-permute-done.9.refs_3_
  123.1 0.0 collective-permute-done.10.refs_4_
  123.1 0.0 collective-permute-done.11.refs_5_
  123.2 2.6 %section.5 = (f32[96,2,384]{2,1,0:T(2,128)}, f32[96,16,128]{2,1,0:T(8,128)}) custom-call(f32[2,96,384]{2,1,0:T(8,128)S(1)} %get-tuple-element.72.refs_0_, f32[16,96,128]{2,1,0:T(8,128)S(1)} %fill.5.refs_1_, f32[96,128]{1,0:T(8,128)S(1)} %collective-permute-done.8.refs_2_, f32[96,128]{1,0:T(8,128)S(1)} %collective-permute-done.9.refs_3_, ...), custom_call_target="tpu_custom_call" | custom-call | tf_op jit(solution)/shard_map/section/pallas_call | solution.py:52
Async XLA Ops:
  0.6 55.1 %copy-start = (f32[4,2,384]{2,1,0:T(2,128)S(1)}, f32[4,2,384]{2,1,0:T(2,128)}, u32[]{:S(2)}) copy-start(f32[4,2,384]{2,1,0:T(2,128)} %refs_6_.5) | copy-start | bytes 36868
  46.2 9.5 %collective-permute-start.2 = (f32[104,384]{1,0:T(8,128)S(1)}, f32[104,384]{1,0:T(8,128)S(1)}, u32[]{:S(2)}, u32[]{:S(2)}) collective-permute-start(f32[104,384]{1,0:T(8,128)S(1)} %get-tuple-element.54), channel_id=1, source_target_pairs={{1,2},{2,1},{3,4},{4,3},{5,6},{6,5},{7,8},{8,7},{9,10},{10,9},{11,... | collective-permute-start | bytes 479240 | tf_op jit(solution)/shard_map/ppermute | solution.py:541
  47.9 7.8 %collective-permute-start.3 = (f32[104,384]{1,0:T(8,128)S(1)}, f32[104,384]{1,0:T(8,128)S(1)}, u32[]{:S(2)}, u32[]{:S(2)}) collective-permute-start(f32[104,384]{1,0:T(8,128)S(1)} %get-tuple-element.55), channel_id=1, source_target_pairs={{0,1},{1,0},{2,3},{3,2},{4,5},{5,4},{6,7},{7,6},{8,9},{9,8},{10,11... | collective-permute-start | bytes 479240 | tf_op jit(solution)/shard_map/ppermute | solution.py:542
  49.4 6.2 %collective-permute-start = (f32[96,128]{1,0:T(8,128)S(1)}, f32[96,128]{1,0:T(8,128)S(1)}, u32[]{:S(2)}, u32[]{:S(2)}) collective-permute-start(f32[96,128]{1,0:T(8,128)S(1)} %get-tuple-element.52), channel_id=1, source_target_pairs={{8,16},{16,8},{9,17},{17,9},{10,18},{18,10},{11,19},{19,11},{12,20... | collective-permute-start | bytes 147464 | tf_op jit(solution)/shard_map/ppermute | solution.py:543
  49.4 6.2 %collective-permute-start.1 = (f32[96,128]{1,0:T(8,128)S(1)}, f32[96,128]{1,0:T(8,128)S(1)}, u32[]{:S(2)}, u32[]{:S(2)}) collective-permute-start(f32[96,128]{1,0:T(8,128)S(1)} %get-tuple-element.53), channel_id=1, source_target_pairs={{0,8},{8,0},{1,9},{9,1},{2,10},{10,2},{3,11},{11,3},{4,12},{12,4},... | collective-permute-start | bytes 147464 | tf_op jit(solution)/shard_map/ppermute | solution.py:544
  79.9 9.5 %collective-permute-start.6 = (f32[104,384]{1,0:T(8,128)S(1)}, f32[104,384]{1,0:T(8,128)S(1)}, u32[]{:S(2)}, u32[]{:S(2)}) collective-permute-start(f32[104,384]{1,0:T(8,128)S(1)} %get-tuple-element.67), channel_id=1, source_target_pairs={{1,2},{2,1},{3,4},{4,3},{5,6},{6,5},{7,8},{8,7},{9,10},{10,9},{11,... | collective-permute-start | bytes 479240 | tf_op jit(solution)/shard_map/ppermute | solution.py:541
  81.8 7.7 %collective-permute-start.7 = (f32[104,384]{1,0:T(8,128)S(1)}, f32[104,384]{1,0:T(8,128)S(1)}, u32[]{:S(2)}, u32[]{:S(2)}) collective-permute-start(f32[104,384]{1,0:T(8,128)S(1)} %get-tuple-element.68), channel_id=1, source_target_pairs={{0,1},{1,0},{2,3},{3,2},{4,5},{5,4},{6,7},{7,6},{8,9},{9,8},{10,11... | collective-permute-start | bytes 479240 | tf_op jit(solution)/shard_map/ppermute | solution.py:542
  83.3 6.2 %collective-permute-start.4 = (f32[96,128]{1,0:T(8,128)S(1)}, f32[96,128]{1,0:T(8,128)S(1)}, u32[]{:S(2)}, u32[]{:S(2)}) collective-permute-start(f32[96,128]{1,0:T(8,128)S(1)} %get-tuple-element.65), channel_id=1, source_target_pairs={{8,16},{16,8},{9,17},{17,9},{10,18},{18,10},{11,19},{19,11},{12,20... | collective-permute-start | bytes 147464 | tf_op jit(solution)/shard_map/ppermute | solution.py:543
  83.3 6.2 %collective-permute-start.5 = (f32[96,128]{1,0:T(8,128)S(1)}, f32[96,128]{1,0:T(8,128)S(1)}, u32[]{:S(2)}, u32[]{:S(2)}) collective-permute-start(f32[96,128]{1,0:T(8,128)S(1)} %get-tuple-element.66), channel_id=1, source_target_pairs={{0,8},{8,0},{1,9},{9,1},{2,10},{10,2},{3,11},{11,3},{4,12},{12,4},... | collective-permute-start | bytes 147464 | tf_op jit(solution)/shard_map/ppermute | solution.py:544
  113.5 9.6 %collective-permute-start.10 = (f32[104,384]{1,0:T(8,128)S(1)}, f32[104,384]{1,0:T(8,128)S(1)}, u32[]{:S(2)}, u32[]{:S(2)}) collective-permute-start(f32[104,384]{1,0:T(8,128)S(1)} %get-tuple-element.76), channel_id=1, source_target_pairs={{1,2},{2,1},{3,4},{4,3},{5,6},{6,5},{7,8},{8,7},{9,10},{10,9},{11,... | collective-permute-start | bytes 479240 | tf_op jit(solution)/shard_map/ppermute | solution.py:541
  115.6 7.6 %collective-permute-start.11 = (f32[104,384]{1,0:T(8,128)S(1)}, f32[104,384]{1,0:T(8,128)S(1)}, u32[]{:S(2)}, u32[]{:S(2)}) collective-permute-start(f32[104,384]{1,0:T(8,128)S(1)} %get-tuple-element.77), channel_id=1, source_target_pairs={{0,1},{1,0},{2,3},{3,2},{4,5},{5,4},{6,7},{7,6},{8,9},{9,8},{10,11... | collective-permute-start | bytes 479240 | tf_op jit(solution)/shard_map/ppermute | solution.py:542
  116.9 6.3 %collective-permute-start.8 = (f32[96,128]{1,0:T(8,128)S(1)}, f32[96,128]{1,0:T(8,128)S(1)}, u32[]{:S(2)}, u32[]{:S(2)}) collective-permute-start(f32[96,128]{1,0:T(8,128)S(1)} %get-tuple-element.74), channel_id=1, source_target_pairs={{8,16},{16,8},{9,17},{17,9},{10,18},{18,10},{11,19},{19,11},{12,20... | collective-permute-start | bytes 147464 | tf_op jit(solution)/shard_map/ppermute | solution.py:543
  116.9 6.3 %collective-permute-start.9 = (f32[96,128]{1,0:T(8,128)S(1)}, f32[96,128]{1,0:T(8,128)S(1)}, u32[]{:S(2)}, u32[]{:S(2)}) collective-permute-start(f32[96,128]{1,0:T(8,128)S(1)} %get-tuple-element.75), channel_id=1, source_target_pairs={{0,8},{8,0},{1,9},{9,1},{2,10},{10,2},{3,11},{11,3},{4,12},{12,4},... | collective-permute-start | bytes 147464 | tf_op jit(solution)/shard_map/ppermute | solution.py:544

commit v4 on v3

--- a/solution.py
+++ b/solution.py
@@ -289,7 +289,7 @@
         side[PLANES : PLANES + 8, 2 * COLS : 3 * COLS] = jnp.zeros((8, COLS), F32)
 
 
-def fill_kernel(got_pieces, fill_ref, keep_ref, back_ref, back_out):
+def fill_rows(got_pieces, fill_ref, keep_ref, back_ref, back_out):
     for c in range(ROWS // 2):
         new = dot(got_pieces[...], fill_ref[:, c * 256 : (c + 1) * 256], NN)
         new = new[0:PLANES] + new[PLANES : 2 * PLANES]
@@ -298,7 +298,12 @@
             back_out[r] = back_ref[r] * keep_ref[r, 0:1, :] + new[:, half * 128 : (half + 1) * 128]
 
 
-def first_fill_kernel(got_pieces, local_ref, back_ref, back_out, fill_ref, keep_ref):
+def fill_kernel(section, got_pieces, fill_ref, keep_ref, back_ref, base_ref, back_out, *inner):
+    fill_rows(got_pieces, fill_ref, keep_ref, back_ref, back_out)
+    inner_rows(section, back_out, keep_ref, base_ref, *inner)
+
+
+def first_fill_kernel(got_pieces, local_ref, back_ref, back_out, fill_ref, keep_ref, *inner):
     lane = iota((MEMBERS, COLS), 1)
     places = local_ref[...].astype(jnp.int32)
     listed = [jnp.zeros((8, COLS), F32) for _ in range(ROWS)]
@@ -313,10 +318,11 @@
             listed[r] = listed[r] + over_eight(here)
     for r in range(ROWS):
         keep_ref[r] = kept(listed[r])
-    fill_kernel(got_pieces, fill_ref, keep_ref, back_ref, back_out)
-
-
-def update(here, minus_xi, plus_xi, minus_eta, plus_eta, metric, keep, base, section):
+    fill_rows(got_pieces, fill_ref, keep_ref, back_ref, back_out)
+    inner_rows(0, back_out, keep_ref, None, *inner)
+
+
+def deck_update(here, minus_xi, plus_xi, minus_eta, plus_eta, metric, keep, base, section):
     weight = (1.0, 0.25, 2.0 / 3.0)[section]
     step = (weight * TIME_STEP) * keep
     d_xi, d_eta, d_span, lap = [], [], [], []
@@ -330,25 +336,18 @@
         s = plus_span - minus_span
         square = a * a + b * b + s * s
         strain = square if strain is None else strain + square
-        if metric is None:
-            around = (plus_xi[c] + minus_xi[c]) + (plus_eta[c] + minus_eta[c]) + (plus_span + minus_span)
-            lap.append(around - 6.0 * f)
-        else:
-            doubled = 2.0 * f
-            l_xi = plus_xi[c] - doubled + minus_xi[c]
-            l_eta = plus_eta[c] - doubled + minus_eta[c]
-            lap.append(metric[4] * l_xi + metric[5] * l_eta + (plus_span - doubled + minus_span))
+        doubled = 2.0 * f
+        l_xi = plus_xi[c] - doubled + minus_xi[c]
+        l_eta = plus_eta[c] - doubled + minus_eta[c]
+        lap.append(metric[4] * l_xi + metric[5] * l_eta + (plus_span - doubled + minus_span))
         d_xi.append(a)
         d_eta.append(b)
         d_span.append(s)
     stretched = 1.0 + 0.25 * strain
     viscosity = (SMAGORINSKY * step) * (stretched * lax.rsqrt(stretched))
     half = 0.5 * step
-    if metric is None:
-        speed_xi, speed_eta = half * here[0], half * here[1]
-    else:
-        speed_xi = half * (metric[0] * here[0] + metric[1] * here[1])
-        speed_eta = half * (metric[2] * here[0] + metric[3] * here[1])
+    speed_xi = half * (metric[0] * here[0] + metric[1] * here[1])
+    speed_eta = half * (metric[2] * here[0] + metric[3] * here[1])
     speed_span = half * here[2]
     out = []
     for c in range(3):
@@ -362,6 +361,60 @@
     return out
 
 
+def inner_part(here, minus_xi, plus_xi, keep, base, section):
+    weight = (1.0, 0.25, 2.0 / 3.0)[section]
+    half = (0.5 * weight * TIME_STEP) * keep
+    speed_xi, speed_span = half * here[0], half * here[2]
+    strain, lap, rest = None, [], []
+    for c in range(3):
+        f = here[c]
+        plus_span = pltpu.roll(f, SPAN - 1, 0)
+        minus_span = pltpu.roll(f, 1, 0)
+        a = plus_xi[c] - minus_xi[c]
+        s = plus_span - minus_span
+        square = a * a + s * s
+        strain = square if strain is None else strain + square
+        lap.append((plus_xi[c] + minus_xi[c]) + (plus_span + minus_span) - 6.0 * f)
+        advection = speed_xi * a + speed_span * s
+        if section == 0:
+            rest.append(f - advection)
+        elif section == 1:
+            rest.append(0.75 * base[c] + (0.25 * f - advection))
+        else:
+            rest.append(base[c] * (1.0 / 3.0) + ((2.0 / 3.0) * f - advection))
+    return strain, lap, rest
+
+
+def outer_part(here, minus_eta, plus_eta, part, keep, section):
+    strain, lap, rest = part
+    step = ((1.0, 0.25, 2.0 / 3.0)[section] * TIME_STEP) * keep
+    b = [plus_eta[c] - minus_eta[c] for c in range(3)]
+    strain = strain + (b[0] * b[0] + b[1] * b[1] + b[2] * b[2])
+    stretched = 1.0 + 0.25 * strain
+    viscosity = (SMAGORINSKY * step) * (stretched * lax.rsqrt(stretched))
+    speed_eta = (0.5 * step) * here[1]
+    return [
+        rest[c] + (viscosity * (lap[c] + (plus_eta[c] + minus_eta[c])) - speed_eta * b[c])
+        for c in range(3)
+    ]
+
+
+def inner_rows(section, back_ref, keep_ref, base_ref, strain_out, lap_out, rest_out):
+    for r in range(1, ROWS - 1):
+        strain, lap, rest = inner_part(
+            fields(back_ref, (r,)),
+            fields(back_ref, (r - 1,)),
+            fields(back_ref, (r + 1,)),
+            keep_ref[r, 0:1, :],
+            None if base_ref is None else fields(base_ref, (r,)),
+            section,
+        )
+        strain_out[r - 1] = strain
+        for c in range(3):
+            lap_out[r - 1, c * SPAN : (c + 1) * SPAN, :] = lap[c]
+            rest_out[r - 1, c * SPAN : (c + 1) * SPAN, :] = rest[c]
+
+
 def fields(ref, at):
     return [ref[at + (slice(c * SPAN, (c + 1) * SPAN), slice(None))] for c in range(3)]
 
@@ -369,7 +422,8 @@
 def section_kernel(section, *refs):
     refs = list(refs)
     deck_ref, back_ref, column_first, column_second, row_first, row_second, metric_ref, keep_ref = refs[:8]
-    del refs[:8]
+    strain_ref, lap_ref, rest_ref = refs[8:11]
+    del refs[:11]
     base_deck = base_back = None
     if section > 0:
         base_deck, base_back = refs[:2]
@@ -425,7 +479,7 @@
         plus_eta = [jnp.where(lane == DCOLS - 1, 0.0, pltpu.roll(f, DCOLS - 1, 1)) for f in here]
         minus_eta = [jnp.where(lane == 0, 0.0, pltpu.roll(f, 1, 1)) for f in here]
         base = fields(base_deck, (r,)) if section > 0 else None
-        new = update(here, minus, plus, minus_eta, plus_eta, metric, keep_deck, base, section)
+        new = deck_update(here, minus, plus, minus_eta, plus_eta, metric, keep_deck, base, section)
         for c in range(3):
             deck_out[r, c * SPAN : (c + 1) * SPAN, :] = new[c]
         if last:
@@ -435,16 +489,21 @@
     lane = iota((SPAN, COLS), 1)
     for r in range(ROWS):
         here = fields(back_ref, (r,))
-        minus = fields(back_ref, (r - 1,)) if r > 0 else [a[0] for a in along]
-        plus = fields(back_ref, (r + 1,)) if r < ROWS - 1 else [a[1] for a in along]
         plus_eta, minus_eta = [], []
         for c in range(3):
             from_west = beside[0][spans[c], r : r + 1] * west_end
             from_east = beside[1][spans[c], r : r + 1] * east_end
             plus_eta.append(jnp.where(lane == COLS - 1, from_east, pltpu.roll(here[c], COLS - 1, 1)))
             minus_eta.append(jnp.where(lane == 0, from_west, pltpu.roll(here[c], 1, 1)))
-        base = fields(base_back, (r,)) if section > 0 else None
-        new = update(here, minus, plus, minus_eta, plus_eta, None, keep_ref[r, 0:1, :], base, section)
+        keep = keep_ref[r, 0:1, :]
+        if 0 < r < ROWS - 1:
+            part = strain_ref[r - 1], fields(lap_ref, (r - 1,)), fields(rest_ref, (r - 1,))
+        else:
+            minus = fields(back_ref, (r - 1,)) if r > 0 else [a[0] for a in along]
+            plus = fields(back_ref, (r + 1,)) if r < ROWS - 1 else [a[1] for a in along]
+            base = fields(base_back, (r,)) if section > 0 else None
+            part = inner_part(here, minus, plus, keep, base, section)
+        new = outer_part(here, minus_eta, plus_eta, part, keep, section)
         for c in range(3):
             back_out[r, c * SPAN : (c + 1) * SPAN, :] = new[c]
         if last:
@@ -476,7 +535,7 @@
                 if periodic or t + step < count:
                     out += [(t, other), (other, t)]
                 else:
-                    out += [(t, t ^ 1), (other, other ^ 1)]
+                    out += [(t, t ^ 2), (other, other ^ 2)]
         return out
 
     deck_in = deck_fields.reshape(PLANES, DROWS, DCOLS)
@@ -542,22 +601,27 @@
         row_second = lax.ppermute(row_second, everyone, pairs(1, 0, True))
         column_first = lax.ppermute(column_first, everyone, pairs(across_y, 1))
         column_second = lax.ppermute(column_second, everyone, pairs(across_y, 0))
+        inner = [
+            ((ROWS - 2, SPAN, COLS), F32),
+            ((ROWS - 2, PLANES, COLS), F32),
+            ((ROWS - 2, PLANES, COLS), F32),
+        ]
         if section == 0:
-            back_state, fill_map, keep = call(
+            back_state, fill_map, keep, *inner = call(
                 first_fill_kernel,
-                [((ROWS, PLANES, COLS), F32), ((SLOTS, ROWS * COLS), BF16), ((ROWS, 8, COLS), F32)],
+                [((ROWS, PLANES, COLS), F32), ((SLOTS, ROWS * COLS), BF16), ((ROWS, 8, COLS), F32)] + inner,
                 [got_pieces, placing, back_state],
                 name="fill",
             )
             base = [deck, back_state]
         else:
-            (back_state,) = call(
-                fill_kernel,
-                [((ROWS, PLANES, COLS), F32)],
-                [got_pieces, fill_map, keep, back_state],
+            back_state, *inner = call(
+                functools.partial(fill_kernel, section),
+                [((ROWS, PLANES, COLS), F32)] + inner,
+                [got_pieces, fill_map, keep, back_state, base[1]],
                 name="fill",
             )
-        ins = [deck, back_state, column_first, column_second, row_first, row_second, metrics, keep]
+        ins = [deck, back_state, column_first, column_second, row_first, row_second, metrics, keep] + inner
         if section > 0:
             ins += base
         kernel = functools.partial(section_kernel, section)

time: 126 us -> 125 us (level)
  waiting for transfers between devices: 12.4 us -> 10.9 us
    ppermute x3, waiting for transfers between devices: 12.4 us -> 10.9 us  [local(): column_first = lax.ppermute(column_first, everyone, pairs(across_y, 1))]
  transfers between devices with their start and end apart: 12 -> 12, of which waited for: 3 -> 3; matrix products, arithmetic and copies ran while one was open for 0% -> 0% of each run, Pallas kernels for 3% -> 5%
where the time goes in v4:
time: 125 us
  blocking collectives  80.6 us (64%)
  Pallas kernels  20.7 us (17%)
  starting transfers between devices  11.9 us (10%)
  waiting for transfers between devices  10.9 us (9%)
    all_to_all x4, blocking collectives, exchange(): return lax.all_to_all(x, group, split_axis=0, concat_axis=0, tiled=True)  80.6 us
    pallas_call x11, Pallas kernels, call(): pl.pallas_call(kernel, out_shape=tuple((jax.ShapeDtypeStruct(s, d) for s,...  20.7 us
    ppermute x3, waiting for transfers between devices, local(): column_first = lax.ppermute(column_first, everyone, pairs(across_y, 1))  10.9 us
    ppermute x3, starting transfers between devices, local(): row_first = lax.ppermute(row_first, everyone, pairs(1, 1, True))  5.57 us
    ppermute x3, starting transfers between devices, local(): row_second = lax.ppermute(row_second, everyone, pairs(1, 0, True))  4.31 us
  transfers between devices with their start and end apart: 12, of which 3 were waited for; matrix products, arithmetic and copies ran while one was open for 0% of the time, Pallas kernels for 5%

profile of v4, /device:TPU:8, one launch (start us, length us, event | category | flops | bytes accessed | tf_op | source)
XLA Modules:
  0.0 124.9 jit_solution(12866455844984764435)
XLA Ops:
  0.6 0.0 copy-start
  0.6 1.8 %route.1 = (f32[64,1,128]{2,1,0:T(1,128)S(1)}, f32[64,48]{1,0:T(8,128)S(1)}, bf16[1024,384]{1,0:T(8,128)(2,1)S(1)}, bf16[256,256]{1,0:T(8,128)(2,1)S(1)}, f32[3,8,128]{2,1,0:T(8,128)S(1)}) custom-call(s32[1,512]{1,0:T(1,128)} %bitcast.11, s32[4,512]{1,0:T(4,128)} %bitcast.10, s32[1,508]{1,0:T(1,128)} %cells_hbm.1), custom_call_target="tpu_custom_call" | custom-call | tf_op jit(solution)/shard_map/route/pallas_call | solution.py:52
  2.4 21.3 %all_to_all.20.request_ref = f32[64,1,128]{2,1,0:T(1,128)S(1)} all-to-all(f32[64,1,128]{2,1,0:T(1,128)S(1)} %get-tuple-element.52), channel_id=1, replica_groups=mesh['grid'=4,'gx'=8,'gy'=8] {'gy','gx'}, dimensions={0} | all-to-all | bytes 65536 | tf_op jit(solution)/shard_map/all_to_all | solution.py:525
  23.7 2.5 %first_answer.1 = (f32[2,96,384]{2,1,0:T(8,128)S(1)}, f32[16,96,128]{2,1,0:T(8,128)S(1)}, bf16[1024,768]{1,0:T(8,128)(2,1)S(1)}, bf16[256,2048]{1,0:T(8,128)(2,1)S(1)}, f32[64,1,1536]{2,1,0:T(1,128)S(1)}) custom-call(f32[64,1,128]{2,1,0:T(1,128)S(1)} %all_to_all.20.request_ref, f32[96,2,384]{2,1,0:T(2,128)} %bitcast.9, f32[96,16,128]{2,1,0:T(8,128)} %bitcast.8), custom_call_target="tpu_custom_call" | custom-call | tf_op jit(solution)/shard_map/first_answer/pallas_call | solution.py:52
  26.3 18.7 %all_to_all.21.got_ref = f32[64,1,1536]{2,1,0:T(1,128)S(1)} all-to-all(f32[64,1,1536]{2,1,0:T(1,128)S(1)} %get-tuple-element.53), channel_id=1, replica_groups=mesh['grid'=4,'gx'=8,'gy'=8] {'gy','gx'}, dimensions={0} | all-to-all | bytes 786432 | tf_op jit(solution)/shard_map/all_to_all | solution.py:525
  45.0 1.1 rim.3
  46.1 1.7 %collective-permute-start.2 = (f32[104,384]{1,0:T(8,128)S(1)}, f32[104,384]{1,0:T(8,128)S(1)}, u32[]{:S(2)}, u32[]{:S(2)}) collective-permute-start(f32[104,384]{1,0:T(8,128)S(1)} %get-tuple-element.65), channel_id=1, source_target_pairs={{1,2},{2,1},{3,4},{4,3},{5,6},{6,5},{7,8},{8,7},{9,10},{10,9},{11,... | collective-permute-start | bytes 479240 | tf_op jit(solution)/shard_map/ppermute | solution.py:600
  47.8 1.6 %collective-permute-start.3 = (f32[104,384]{1,0:T(8,128)S(1)}, f32[104,384]{1,0:T(8,128)S(1)}, u32[]{:S(2)}, u32[]{:S(2)}) collective-permute-start(f32[104,384]{1,0:T(8,128)S(1)} %get-tuple-element.66), channel_id=1, source_target_pairs={{0,1},{1,0},{2,3},{3,2},{4,5},{5,4},{6,7},{7,6},{8,9},{9,8},{10,11... | collective-permute-start | bytes 479240 | tf_op jit(solution)/shard_map/ppermute | solution.py:601
  49.4 0.0 collective-permute-start
  49.4 0.7 collective-permute-start.1
  50.1 2.7 %fill.3 = (f32[16,96,128]{2,1,0:T(8,128)S(1)}, bf16[1024,2048]{1,0:T(8,128)(2,1)S(1)}, f32[16,8,128]{2,1,0:T(8,128)S(1)}, f32[14,32,128]{2,1,0:T(8,128)S(1)}, f3...) custom-call(bf16[192,1024]{1,0:T(8,128)(2,1)S(1)} %get-tuple-element.60.got_pieces, ...), custom_call_target="tpu_custom_call" | custom-call | tf_op jit(solution)/shard_map/fill/pallas_call | solution.py:52
  52.8 2.8 %collective-permute-done.refs_2_ = f32[96,128]{1,0:T(8,128)S(1)} collective-permute-done((f32[96,128]{1,0:T(8,128)S(1)}, f32[96,128]{1,0:T(8,128)S(1)}, u32[]{:S(2)}, u32[]{:S(2)}) %collective-permute-start) | collective-permute-done | bytes 49184 | tf_op jit(solution)/shard_map/ppermute | solution.py:602
  55.6 0.0 collective-permute-done.1.refs_3_
  55.6 0.0 collective-permute-done.2.refs_4_
  55.6 0.0 collective-permute-done.3.refs_5_
  55.6 0.0 copy-done
  55.6 2.4 %section.3 = (f32[2,96,384]{2,1,0:T(8,128)S(1)}, f32[16,96,128]{2,1,0:T(8,128)S(1)}, f32[64,1,1536]{2,1,0:T(1,128)S(1)}) custom-call(f32[2,96,384]{2,1,0:T(8,128)S(1)} %get-tuple-element.59.refs_0_.refs_11_, f32[16,96,128]{2,1,0:T(8,128)S(1)} %get-tuple-element.62.refs_1_.base_ref.refs_12_, f32[96,128]{1,0:T(8,128)S(1)} %collective-permute-done.refs_2_, ...), custom_call_target="tpu_custom_call" | custom-call | tf_op jit(solution)/shard_map/section/pallas_call | solution.py:52
  58.0 20.4 %all_to_all.22.got_ref = f32[64,1,1536]{2,1,0:T(1,128)S(1)} all-to-all(f32[64,1,1536]{2,1,0:T(1,128)S(1)} %get-tuple-element.73), channel_id=1, replica_groups=mesh['grid'=4,'gx'=8,'gy'=8] {'gy','gx'}, dimensions={0} | all-to-all | bytes 786432 | tf_op jit(solution)/shard_map/all_to_all | solution.py:525
  78.4 1.1 rim.4
  79.5 1.8 %collective-permute-start.6 = (f32[104,384]{1,0:T(8,128)S(1)}, f32[104,384]{1,0:T(8,128)S(1)}, u32[]{:S(2)}, u32[]{:S(2)}) collective-permute-start(f32[104,384]{1,0:T(8,128)S(1)} %get-tuple-element.82), channel_id=1, source_target_pairs={{1,2},{2,1},{3,4},{4,3},{5,6},{6,5},{7,8},{8,7},{9,10},{10,9},{11,... | collective-permute-start | bytes 479240 | tf_op jit(solution)/shard_map/ppermute | solution.py:600
  81.3 1.5 %collective-permute-start.7 = (f32[104,384]{1,0:T(8,128)S(1)}, f32[104,384]{1,0:T(8,128)S(1)}, u32[]{:S(2)}, u32[]{:S(2)}) collective-permute-start(f32[104,384]{1,0:T(8,128)S(1)} %get-tuple-element.83), channel_id=1, source_target_pairs={{0,1},{1,0},{2,3},{3,2},{4,5},{5,4},{6,7},{7,6},{8,9},{9,8},{10,11... | collective-permute-start | bytes 479240 | tf_op jit(solution)/shard_map/ppermute | solution.py:601
  82.8 0.0 collective-permute-start.4
  82.9 0.6 collective-permute-start.5
  83.5 1.6 %fill.4 = (f32[16,96,128]{2,1,0:T(8,128)S(1)}, f32[14,32,128]{2,1,0:T(8,128)S(1)}, f32[14,96,128]{2,1,0:T(8,128)S(1)}, f32[14,96,128]{2,1,0:T(8,128)S(1)}) custom-call(bf16[192,1024]{1,0:T(8,128)(2,1)S(1)} %get-tuple-element.77.got_pieces, bf16[1024,2048]{1,0:T(8,128)(2,1)S(1)} %get-tuple-element.78.fill_ref, ...), custom_call_target="tpu_custom_call" | custom-call | tf_op jit(solution)/shard_map/fill/pallas_call | solution.py:52
  85.1 4.0 %collective-permute-done.4.refs_2_ = f32[96,128]{1,0:T(8,128)S(1)} collective-permute-done((f32[96,128]{1,0:T(8,128)S(1)}, f32[96,128]{1,0:T(8,128)S(1)}, u32[]{:S(2)}, u32[]{:S(2)}) %collective-permute-start.4) | collective-permute-done | bytes 49184 | tf_op jit(solution)/shard_map/ppermute | solution.py:602
  89.0 0.0 collective-permute-done.5.refs_3_
  89.0 0.0 collective-permute-done.6.refs_4_
  89.0 0.0 collective-permute-done.7.refs_5_
  89.0 2.5 %section.4 = (f32[2,96,384]{2,1,0:T(8,128)S(1)}, f32[16,96,128]{2,1,0:T(8,128)S(1)}, f32[64,1,1536]{2,1,0:T(1,128)S(1)}) custom-call(f32[2,96,384]{2,1,0:T(8,128)S(1)} %get-tuple-element.76.refs_0_, f32[16,96,128]{2,1,0:T(8,128)S(1)} %get-tuple-element.79.refs_1_, f32[96,128]{1,0:T(8,128)S(1)} %collective-permute-done.4.refs_2_, ...), custom_call_target="tpu_custom_call" | custom-call | tf_op jit(solution)/shard_map/section/pallas_call | solution.py:52
  91.5 20.1 %all_to_all.23.got_ref = f32[64,1,1536]{2,1,0:T(1,128)S(1)} all-to-all(f32[64,1,1536]{2,1,0:T(1,128)S(1)} %get-tuple-element.87), channel_id=1, replica_groups=mesh['grid'=4,'gx'=8,'gy'=8] {'gy','gx'}, dimensions={0} | all-to-all | bytes 786432 | tf_op jit(solution)/shard_map/all_to_all | solution.py:525
  111.7 1.1 rim.5
  112.8 2.1 %collective-permute-start.10 = (f32[104,384]{1,0:T(8,128)S(1)}, f32[104,384]{1,0:T(8,128)S(1)}, u32[]{:S(2)}, u32[]{:S(2)}) collective-permute-start(f32[104,384]{1,0:T(8,128)S(1)} %get-tuple-element.95), channel_id=1, source_target_pairs={{1,2},{2,1},{3,4},{4,3},{5,6},{6,5},{7,8},{8,7},{9,10},{10,9},{11,... | collective-permute-start | bytes 479240 | tf_op jit(solution)/shard_map/ppermute | solution.py:600
  114.8 1.3 %collective-permute-start.11 = (f32[104,384]{1,0:T(8,128)S(1)}, f32[104,384]{1,0:T(8,128)S(1)}, u32[]{:S(2)}, u32[]{:S(2)}) collective-permute-start(f32[104,384]{1,0:T(8,128)S(1)} %get-tuple-element.96), channel_id=1, source_target_pairs={{0,1},{1,0},{2,3},{3,2},{4,5},{5,4},{6,7},{7,6},{8,9},{9,8},{10,11... | collective-permute-start | bytes 479240 | tf_op jit(solution)/shard_map/ppermute | solution.py:601
  116.1 0.0 collective-permute-start.8
  116.1 0.6 collective-permute-start.9
  116.7 1.5 %fill.5 = (f32[16,96,128]{2,1,0:T(8,128)S(1)}, f32[14,32,128]{2,1,0:T(8,128)S(1)}, f32[14,96,128]{2,1,0:T(8,128)S(1)}, f32[14,96,128]{2,1,0:T(8,128)S(1)}) custom-call(bf16[192,1024]{1,0:T(8,128)(2,1)S(1)} %get-tuple-element.91.got_pieces, bf16[1024,2048]{1,0:T(8,128)(2,1)S(1)} %get-tuple-element.78.fill_ref, ...), custom_call_target="tpu_custom_call" | custom-call | tf_op jit(solution)/shard_map/fill/pallas_call | solution.py:52
  118.3 4.1 %collective-permute-done.8.refs_2_ = f32[96,128]{1,0:T(8,128)S(1)} collective-permute-done((f32[96,128]{1,0:T(8,128)S(1)}, f32[96,128]{1,0:T(8,128)S(1)}, u32[]{:S(2)}, u32[]{:S(2)}) %collective-permute-start.8) | collective-permute-done | bytes 49184 | tf_op jit(solution)/shard_map/ppermute | solution.py:602
  122.4 0.0 collective-permute-done.9.refs_3_
  122.4 0.0 collective-permute-done.10.refs_4_
  122.4 0.0 collective-permute-done.11.refs_5_
  122.4 2.4 %section.5 = (f32[96,2,384]{2,1,0:T(2,128)}, f32[96,16,128]{2,1,0:T(8,128)}) custom-call(f32[2,96,384]{2,1,0:T(8,128)S(1)} %get-tuple-element.90.refs_0_, f32[16,96,128]{2,1,0:T(8,128)S(1)} %get-tuple-element.92.refs_1_, f32[96,128]{1,0:T(8,128)S(1)} %collective-permute-done.8.refs_2_, f32[96,128]{1,0:T(8,128)S(1)} %collective-permute-done.9.refs_3_, ...), custom_call_target="tpu_custom_call" | custom-call | tf_op jit(solution)/shard_map/section/pallas_call | solution.py:52
Async XLA Ops:
  0.6 55.0 %copy-start = (f32[4,2,384]{2,1,0:T(2,128)S(1)}, f32[4,2,384]{2,1,0:T(2,128)}, u32[]{:S(2)}) copy-start(f32[4,2,384]{2,1,0:T(2,128)} %refs_6_.5) | copy-start | bytes 36868
  46.1 9.5 %collective-permute-start.2 = (f32[104,384]{1,0:T(8,128)S(1)}, f32[104,384]{1,0:T(8,128)S(1)}, u32[]{:S(2)}, u32[]{:S(2)}) collective-permute-start(f32[104,384]{1,0:T(8,128)S(1)} %get-tuple-element.65), channel_id=1, source_target_pairs={{1,2},{2,1},{3,4},{4,3},{5,6},{6,5},{7,8},{8,7},{9,10},{10,9},{11,... | collective-permute-start | bytes 479240 | tf_op jit(solution)/shard_map/ppermute | solution.py:600
  47.8 7.8 %collective-permute-start.3 = (f32[104,384]{1,0:T(8,128)S(1)}, f32[104,384]{1,0:T(8,128)S(1)}, u32[]{:S(2)}, u32[]{:S(2)}) collective-permute-start(f32[104,384]{1,0:T(8,128)S(1)} %get-tuple-element.66), channel_id=1, source_target_pairs={{0,1},{1,0},{2,3},{3,2},{4,5},{5,4},{6,7},{7,6},{8,9},{9,8},{10,11... | collective-permute-start | bytes 479240 | tf_op jit(solution)/shard_map/ppermute | solution.py:601
  49.4 6.2 %collective-permute-start = (f32[96,128]{1,0:T(8,128)S(1)}, f32[96,128]{1,0:T(8,128)S(1)}, u32[]{:S(2)}, u32[]{:S(2)}) collective-permute-start(f32[96,128]{1,0:T(8,128)S(1)} %get-tuple-element.63), channel_id=1, source_target_pairs={{8,16},{16,8},{9,17},{17,9},{10,18},{18,10},{11,19},{19,11},{12,20... | collective-permute-start | bytes 147464 | tf_op jit(solution)/shard_map/ppermute | solution.py:602
  49.4 6.2 %collective-permute-start.1 = (f32[96,128]{1,0:T(8,128)S(1)}, f32[96,128]{1,0:T(8,128)S(1)}, u32[]{:S(2)}, u32[]{:S(2)}) collective-permute-start(f32[96,128]{1,0:T(8,128)S(1)} %get-tuple-element.64), channel_id=1, source_target_pairs={{0,8},{8,0},{1,9},{9,1},{2,10},{10,2},{3,11},{11,3},{4,12},{12,4},... | collective-permute-start | bytes 147464 | tf_op jit(solution)/shard_map/ppermute | solution.py:603
  79.5 9.5 %collective-permute-start.6 = (f32[104,384]{1,0:T(8,128)S(1)}, f32[104,384]{1,0:T(8,128)S(1)}, u32[]{:S(2)}, u32[]{:S(2)}) collective-permute-start(f32[104,384]{1,0:T(8,128)S(1)} %get-tuple-element.82), channel_id=1, source_target_pairs={{1,2},{2,1},{3,4},{4,3},{5,6},{6,5},{7,8},{8,7},{9,10},{10,9},{11,... | collective-permute-start | bytes 479240 | tf_op jit(solution)/shard_map/ppermute | solution.py:600
  81.3 7.7 %collective-permute-start.7 = (f32[104,384]{1,0:T(8,128)S(1)}, f32[104,384]{1,0:T(8,128)S(1)}, u32[]{:S(2)}, u32[]{:S(2)}) collective-permute-start(f32[104,384]{1,0:T(8,128)S(1)} %get-tuple-element.83), channel_id=1, source_target_pairs={{0,1},{1,0},{2,3},{3,2},{4,5},{5,4},{6,7},{7,6},{8,9},{9,8},{10,11... | collective-permute-start | bytes 479240 | tf_op jit(solution)/shard_map/ppermute | solution.py:601
  82.8 6.2 %collective-permute-start.4 = (f32[96,128]{1,0:T(8,128)S(1)}, f32[96,128]{1,0:T(8,128)S(1)}, u32[]{:S(2)}, u32[]{:S(2)}) collective-permute-start(f32[96,128]{1,0:T(8,128)S(1)} %get-tuple-element.80), channel_id=1, source_target_pairs={{8,16},{16,8},{9,17},{17,9},{10,18},{18,10},{11,19},{19,11},{12,20... | collective-permute-start | bytes 147464 | tf_op jit(solution)/shard_map/ppermute | solution.py:602
  82.9 6.2 %collective-permute-start.5 = (f32[96,128]{1,0:T(8,128)S(1)}, f32[96,128]{1,0:T(8,128)S(1)}, u32[]{:S(2)}, u32[]{:S(2)}) collective-permute-start(f32[96,128]{1,0:T(8,128)S(1)} %get-tuple-element.81), channel_id=1, source_target_pairs={{0,8},{8,0},{1,9},{9,1},{2,10},{10,2},{3,11},{11,3},{4,12},{12,4},... | collective-permute-start | bytes 147464 | tf_op jit(solution)/shard_map/ppermute | solution.py:603
  112.8 9.6 %collective-permute-start.10 = (f32[104,384]{1,0:T(8,128)S(1)}, f32[104,384]{1,0:T(8,128)S(1)}, u32[]{:S(2)}, u32[]{:S(2)}) collective-permute-start(f32[104,384]{1,0:T(8,128)S(1)} %get-tuple-element.95), channel_id=1, source_target_pairs={{1,2},{2,1},{3,4},{4,3},{5,6},{6,5},{7,8},{8,7},{9,10},{10,9},{11,... | collective-permute-start | bytes 479240 | tf_op jit(solution)/shard_map/ppermute | solution.py:600
  114.8 7.6 %collective-permute-start.11 = (f32[104,384]{1,0:T(8,128)S(1)}, f32[104,384]{1,0:T(8,128)S(1)}, u32[]{:S(2)}, u32[]{:S(2)}) collective-permute-start(f32[104,384]{1,0:T(8,128)S(1)} %get-tuple-element.96), channel_id=1, source_target_pairs={{0,1},{1,0},{2,3},{3,2},{4,5},{5,4},{6,7},{7,6},{8,9},{9,8},{10,11... | collective-permute-start | bytes 479240 | tf_op jit(solution)/shard_map/ppermute | solution.py:601
  116.1 6.3 %collective-permute-start.8 = (f32[96,128]{1,0:T(8,128)S(1)}, f32[96,128]{1,0:T(8,128)S(1)}, u32[]{:S(2)}, u32[]{:S(2)}) collective-permute-start(f32[96,128]{1,0:T(8,128)S(1)} %get-tuple-element.93), channel_id=1, source_target_pairs={{8,16},{16,8},{9,17},{17,9},{10,18},{18,10},{11,19},{19,11},{12,20... | collective-permute-start | bytes 147464 | tf_op jit(solution)/shard_map/ppermute | solution.py:602
  116.1 6.3 %collective-permute-start.9 = (f32[96,128]{1,0:T(8,128)S(1)}, f32[96,128]{1,0:T(8,128)S(1)}, u32[]{:S(2)}, u32[]{:S(2)}) collective-permute-start(f32[96,128]{1,0:T(8,128)S(1)} %get-tuple-element.94), channel_id=1, source_target_pairs={{0,8},{8,0},{1,9},{9,1},{2,10},{10,2},{3,11},{11,3},{4,12},{12,4},... | collective-permute-start | bytes 147464 | tf_op jit(solution)/shard_map/ppermute | solution.py:603

commit v5 on v4

--- a/solution.py
+++ b/solution.py
@@ -20,6 +20,7 @@
 NEAR = 4
 TIME_STEP = 0.05
 SMAGORINSKY = 0.02
+WEIGHTS = (1.0, 0.25, 2.0 / 3.0)
 F32 = jnp.float32
 BF16 = jnp.bfloat16
 NT = (((1,), (1,)), ((), ()))
@@ -298,12 +299,17 @@
             back_out[r] = back_ref[r] * keep_ref[r, 0:1, :] + new[:, half * 128 : (half + 1) * 128]
 
 
-def fill_kernel(section, got_pieces, fill_ref, keep_ref, back_ref, base_ref, back_out, *inner):
+def fill_kernel(
+    section, got_pieces, fill_ref, keep_ref, back_ref, deck_ref, metric_ref, base_deck, base_back, back_out, *inner
+):
     fill_rows(got_pieces, fill_ref, keep_ref, back_ref, back_out)
-    inner_rows(section, back_out, keep_ref, base_ref, *inner)
-
-
-def first_fill_kernel(got_pieces, local_ref, back_ref, back_out, fill_ref, keep_ref, *inner):
+    inner_rows(section, back_out, keep_ref, base_back, *inner[:3])
+    deck_inner(section, deck_ref, metric_ref, base_deck, *inner[3:])
+
+
+def first_fill_kernel(
+    got_pieces, local_ref, back_ref, deck_ref, metric_ref, back_out, fill_ref, keep_ref, *inner
+):
     lane = iota((MEMBERS, COLS), 1)
     places = local_ref[...].astype(jnp.int32)
     listed = [jnp.zeros((8, COLS), F32) for _ in range(ROWS)]
@@ -319,51 +325,69 @@
     for r in range(ROWS):
         keep_ref[r] = kept(listed[r])
     fill_rows(got_pieces, fill_ref, keep_ref, back_ref, back_out)
-    inner_rows(0, back_out, keep_ref, None, *inner)
-
-
-def deck_update(here, minus_xi, plus_xi, minus_eta, plus_eta, metric, keep, base, section):
-    weight = (1.0, 0.25, 2.0 / 3.0)[section]
-    step = (weight * TIME_STEP) * keep
-    d_xi, d_eta, d_span, lap = [], [], [], []
-    strain = None
-    for c in range(3):
-        f = here[c]
-        plus_span = pltpu.roll(f, SPAN - 1, 0)
-        minus_span = pltpu.roll(f, 1, 0)
-        a = plus_xi[c] - minus_xi[c]
-        b = plus_eta[c] - minus_eta[c]
-        s = plus_span - minus_span
-        square = a * a + b * b + s * s
-        strain = square if strain is None else strain + square
-        doubled = 2.0 * f
-        l_xi = plus_xi[c] - doubled + minus_xi[c]
-        l_eta = plus_eta[c] - doubled + minus_eta[c]
-        lap.append(metric[4] * l_xi + metric[5] * l_eta + (plus_span - doubled + minus_span))
-        d_xi.append(a)
-        d_eta.append(b)
-        d_span.append(s)
+    inner_rows(0, back_out, keep_ref, None, *inner[:3])
+    deck_inner(0, deck_ref, metric_ref, None, *inner[3:])
+
+
+def deck_metric(metric_ref, r):
+    return [metric_ref[i, r : r + 1, :] for i in range(4)]
+
+
+def deck_keep():
+    return jnp.where(iota((1, DCOLS), 1) < DCOLS - 2, 1.0, 0.0)
+
+
+def deck_inner(section, deck_ref, metric_ref, base_ref, strain_out, lap_out, rest_out):
+    lane = iota((SPAN, DCOLS), 1)
+    half = (0.5 * WEIGHTS[section] * TIME_STEP) * deck_keep()
+    for r in range(DROWS):
+        here = fields(deck_ref, (r,))
+        base = None if base_ref is None else fields(base_ref, (r,))
+        m = deck_metric(metric_ref, r)
+        g1, g2 = m[0] * m[0] + m[1] * m[1], m[2] * m[2] + m[3] * m[3]
+        speed_eta, speed_span = half * (m[2] * here[0] + m[3] * here[1]), half * here[2]
+        strain = None
+        for c in range(3):
+            f = here[c]
+            plus_eta = jnp.where(lane == DCOLS - 1, 0.0, pltpu.roll(f, DCOLS - 1, 1))
+            minus_eta = jnp.where(lane == 0, 0.0, pltpu.roll(f, 1, 1))
+            plus_span = pltpu.roll(f, SPAN - 1, 0)
+            minus_span = pltpu.roll(f, 1, 0)
+            b, s = plus_eta - minus_eta, plus_span - minus_span
+            square = b * b + s * s
+            strain = square if strain is None else strain + square
+            doubled = 2.0 * f
+            at = slice(c * SPAN, (c + 1) * SPAN)
+            lap_out[r, at, :] = g2 * (plus_eta - doubled + minus_eta) + (plus_span - doubled + minus_span) - g1 * doubled
+            rest_out[r, at, :] = carried(section, f, base, c) - (speed_eta * b + speed_span * s)
+        strain_out[r] = strain
+
+
+def deck_outer(section, here, minus_xi, plus_xi, m, part):
+    strain, lap, rest = part
+    step = (WEIGHTS[section] * TIME_STEP) * deck_keep()
+    a = [plus_xi[c] - minus_xi[c] for c in range(3)]
+    strain = strain + (a[0] * a[0] + a[1] * a[1] + a[2] * a[2])
     stretched = 1.0 + 0.25 * strain
     viscosity = (SMAGORINSKY * step) * (stretched * lax.rsqrt(stretched))
-    half = 0.5 * step
-    speed_xi = half * (metric[0] * here[0] + metric[1] * here[1])
-    speed_eta = half * (metric[2] * here[0] + metric[3] * here[1])
-    speed_span = half * here[2]
-    out = []
-    for c in range(3):
-        change = viscosity * lap[c] - (speed_xi * d_xi[c] + speed_eta * d_eta[c] + speed_span * d_span[c])
-        if section == 0:
-            out.append(here[c] + change)
-        elif section == 1:
-            out.append(0.75 * base[c] + (0.25 * here[c] + change))
-        else:
-            out.append(base[c] * (1.0 / 3.0) + ((2.0 / 3.0) * here[c] + change))
-    return out
+    speed_xi = (0.5 * step) * (m[0] * here[0] + m[1] * here[1])
+    g1 = m[0] * m[0] + m[1] * m[1]
+    return [
+        rest[c] + (viscosity * (lap[c] + g1 * (plus_xi[c] + minus_xi[c])) - speed_xi * a[c])
+        for c in range(3)
+    ]
+
+
+def carried(section, f, base, c):
+    if section == 0:
+        return f
+    if section == 1:
+        return 0.75 * base[c] + 0.25 * f
+    return base[c] * (1.0 / 3.0) + (2.0 / 3.0) * f
 
 
 def inner_part(here, minus_xi, plus_xi, keep, base, section):
-    weight = (1.0, 0.25, 2.0 / 3.0)[section]
-    half = (0.5 * weight * TIME_STEP) * keep
+    half = (0.5 * WEIGHTS[section] * TIME_STEP) * keep
     speed_xi, speed_span = half * here[0], half * here[2]
     strain, lap, rest = None, [], []
     for c in range(3):
@@ -376,18 +400,13 @@
         strain = square if strain is None else strain + square
         lap.append((plus_xi[c] + minus_xi[c]) + (plus_span + minus_span) - 6.0 * f)
         advection = speed_xi * a + speed_span * s
-        if section == 0:
-            rest.append(f - advection)
-        elif section == 1:
-            rest.append(0.75 * base[c] + (0.25 * f - advection))
-        else:
-            rest.append(base[c] * (1.0 / 3.0) + ((2.0 / 3.0) * f - advection))
+        rest.append(carried(section, f, base, c) - advection)
     return strain, lap, rest
 
 
 def outer_part(here, minus_eta, plus_eta, part, keep, section):
     strain, lap, rest = part
-    step = ((1.0, 0.25, 2.0 / 3.0)[section] * TIME_STEP) * keep
+    step = (WEIGHTS[section] * TIME_STEP) * keep
     b = [plus_eta[c] - minus_eta[c] for c in range(3)]
     strain = strain + (b[0] * b[0] + b[1] * b[1] + b[2] * b[2])
     stretched = 1.0 + 0.25 * strain
@@ -422,12 +441,12 @@
 def section_kernel(section, *refs):
     refs = list(refs)
     deck_ref, back_ref, column_first, column_second, row_first, row_second, metric_ref, keep_ref = refs[:8]
-    strain_ref, lap_ref, rest_ref = refs[8:11]
-    del refs[:11]
-    base_deck = base_back = None
+    strain_ref, lap_ref, rest_ref, deck_strain, deck_lap, deck_rest = refs[8:14]
+    del refs[:14]
+    base_back = None
     if section > 0:
-        base_deck, base_back = refs[:2]
-        del refs[:2]
+        base_back = refs[0]
+        del refs[0]
     last = section == 2
     if last:
         deck_hbm, back_hbm, deck_out, back_out, deck_sems, back_sems = refs
@@ -464,22 +483,15 @@
     south_end = (line < lax.axis_size("grid") * lax.axis_size("gx") - 1).astype(F32)
     along = [ordered(odd_line, column_first, column_second, (at, slice(None))) for at in spans]
     along = [(before * north_end, after * south_end) for before, after in along]
-    lane = iota((SPAN, DCOLS), 1)
-    keep_deck = jnp.where(iota((1, DCOLS), 1) < DCOLS - 2, 1.0, 0.0)
     for r in range(DROWS):
-        here = fields(deck_ref, (r,))
         if r == 0:
             minus = [a[0] for a in across]
             plus = fields(deck_ref, (1,))
         else:
             minus = fields(deck_ref, (0,))
             plus = [a[1] for a in across]
-        m = [metric_ref[i, r : r + 1, :] for i in range(4)]
-        metric = m + [m[0] * m[0] + m[1] * m[1], m[2] * m[2] + m[3] * m[3]]
-        plus_eta = [jnp.where(lane == DCOLS - 1, 0.0, pltpu.roll(f, DCOLS - 1, 1)) for f in here]
-        minus_eta = [jnp.where(lane == 0, 0.0, pltpu.roll(f, 1, 1)) for f in here]
-        base = fields(base_deck, (r,)) if section > 0 else None
-        new = deck_update(here, minus, plus, minus_eta, plus_eta, metric, keep_deck, base, section)
+        part = deck_strain[r], fields(deck_lap, (r,)), fields(deck_rest, (r,))
+        new = deck_outer(section, fields(deck_ref, (r,)), minus, plus, deck_metric(metric_ref, r), part)
         for c in range(3):
             deck_out[r, c * SPAN : (c + 1) * SPAN, :] = new[c]
         if last:
@@ -605,12 +617,15 @@
             ((ROWS - 2, SPAN, COLS), F32),
             ((ROWS - 2, PLANES, COLS), F32),
             ((ROWS - 2, PLANES, COLS), F32),
+            ((DROWS, SPAN, DCOLS), F32),
+            ((DROWS, PLANES, DCOLS), F32),
+            ((DROWS, PLANES, DCOLS), F32),
         ]
         if section == 0:
             back_state, fill_map, keep, *inner = call(
                 first_fill_kernel,
                 [((ROWS, PLANES, COLS), F32), ((SLOTS, ROWS * COLS), BF16), ((ROWS, 8, COLS), F32)] + inner,
-                [got_pieces, placing, back_state],
+                [got_pieces, placing, back_state, deck, metrics],
                 name="fill",
             )
             base = [deck, back_state]
@@ -618,12 +633,12 @@
             back_state, *inner = call(
                 functools.partial(fill_kernel, section),
                 [((ROWS, PLANES, COLS), F32)] + inner,
-                [got_pieces, fill_map, keep, back_state, base[1]],
+                [got_pieces, fill_map, keep, back_state, deck, metrics] + base,
                 name="fill",
             )
         ins = [deck, back_state, column_first, column_second, row_first, row_second, metrics, keep] + inner
         if section > 0:
-            ins += base
+            ins.append(base[1])
         kernel = functools.partial(section_kernel, section)
         if section < 2:
             deck, back_state, answers = call(

time: 125 us -> 124 us (level)
  no operation moved by 1% of the time
where the time goes in v5:
time: 124 us
  blocking collectives  80.6 us (65%)
  Pallas kernels  20.3 us (16%)
  starting transfers between devices  11.9 us (10%)
  waiting for transfers between devices  10.2 us (8%)
    all_to_all x4, blocking collectives, exchange(): return lax.all_to_all(x, group, split_axis=0, concat_axis=0, tiled=True)  80.6 us
    pallas_call x11, Pallas kernels, call(): pl.pallas_call(kernel, out_shape=tuple((jax.ShapeDtypeStruct(s, d) for s,...  20.3 us
    ppermute x3, waiting for transfers between devices, local(): column_first = lax.ppermute(column_first, everyone, pairs(across_y, 1))  10.2 us
    ppermute x3, starting transfers between devices, local(): row_first = lax.ppermute(row_first, everyone, pairs(1, 1, True))  5.57 us
    ppermute x3, starting transfers between devices, local(): row_second = lax.ppermute(row_second, everyone, pairs(1, 0, True))  4.31 us
  transfers between devices with their start and end apart: 12, of which 3 were waited for; matrix products, arithmetic and copies ran while one was open for 0% of the time, Pallas kernels for 5%

profile of v5, /device:TPU:8, one launch (start us, length us, event | category | flops | bytes accessed | tf_op | source)
XLA Modules:
  0.0 123.9 jit_solution(15199423321822592880)
XLA Ops:
  0.6 0.0 copy-start
  0.6 1.8 %route.1 = (f32[64,1,128]{2,1,0:T(1,128)S(1)}, f32[64,48]{1,0:T(8,128)S(1)}, bf16[1024,384]{1,0:T(8,128)(2,1)S(1)}, bf16[256,256]{1,0:T(8,128)(2,1)S(1)}, f32[3,8,128]{2,1,0:T(8,128)S(1)}) custom-call(s32[1,512]{1,0:T(1,128)} %bitcast.11, s32[4,512]{1,0:T(4,128)} %bitcast.10, s32[1,508]{1,0:T(1,128)} %cells_hbm.1), custom_call_target="tpu_custom_call" | custom-call | tf_op jit(solution)/shard_map/route/pallas_call | solution.py:53
  2.4 21.3 %all_to_all.20.request_ref = f32[64,1,128]{2,1,0:T(1,128)S(1)} all-to-all(f32[64,1,128]{2,1,0:T(1,128)S(1)} %get-tuple-element.61), channel_id=1, replica_groups=mesh['grid'=4,'gx'=8,'gy'=8] {'gy','gx'}, dimensions={0} | all-to-all | bytes 65536 | tf_op jit(solution)/shard_map/all_to_all | solution.py:537
  23.7 2.5 %first_answer.1 = (f32[2,96,384]{2,1,0:T(8,128)S(1)}, f32[16,96,128]{2,1,0:T(8,128)S(1)}, bf16[1024,768]{1,0:T(8,128)(2,1)S(1)}, bf16[256,2048]{1,0:T(8,128)(2,1)S(1)}, f32[64,1,1536]{2,1,0:T(1,128)S(1)}) custom-call(f32[64,1,128]{2,1,0:T(1,128)S(1)} %all_to_all.20.request_ref, f32[96,2,384]{2,1,0:T(2,128)} %bitcast.9, f32[96,16,128]{2,1,0:T(8,128)} %bitcast.8), custom_call_target="tpu_custom_call" | custom-call | tf_op jit(solution)/shard_map/first_answer/pallas_call | solution.py:53
  26.3 18.7 %all_to_all.21.got_ref = f32[64,1,1536]{2,1,0:T(1,128)S(1)} all-to-all(f32[64,1,1536]{2,1,0:T(1,128)S(1)} %get-tuple-element.62), channel_id=1, replica_groups=mesh['grid'=4,'gx'=8,'gy'=8] {'gy','gx'}, dimensions={0} | all-to-all | bytes 786432 | tf_op jit(solution)/shard_map/all_to_all | solution.py:537
  45.0 1.1 rim.3
  46.1 1.7 %collective-permute-start.2 = (f32[104,384]{1,0:T(8,128)S(1)}, f32[104,384]{1,0:T(8,128)S(1)}, u32[]{:S(2)}, u32[]{:S(2)}) collective-permute-start(f32[104,384]{1,0:T(8,128)S(1)} %get-tuple-element.74), channel_id=1, source_target_pairs={{1,2},{2,1},{3,4},{4,3},{5,6},{6,5},{7,8},{8,7},{9,10},{10,9},{11,... | collective-permute-start | bytes 479240 | tf_op jit(solution)/shard_map/ppermute | solution.py:612
  47.8 1.6 %collective-permute-start.3 = (f32[104,384]{1,0:T(8,128)S(1)}, f32[104,384]{1,0:T(8,128)S(1)}, u32[]{:S(2)}, u32[]{:S(2)}) collective-permute-start(f32[104,384]{1,0:T(8,128)S(1)} %get-tuple-element.75), channel_id=1, source_target_pairs={{0,1},{1,0},{2,3},{3,2},{4,5},{5,4},{6,7},{7,6},{8,9},{9,8},{10,11... | collective-permute-start | bytes 479240 | tf_op jit(solution)/shard_map/ppermute | solution.py:613
  49.4 0.0 collective-permute-start
  49.4 0.7 collective-permute-start.1
  50.1 0.0 copy-done
  50.1 2.9 %fill.3 = (f32[16,96,128]{2,1,0:T(8,128)S(1)}, bf16[1024,2048]{1,0:T(8,128)(2,1)S(1)}, f32[16,8,128]{2,1,0:T(8,128)S(1)}, f32[14,32,128]{2,1,0:T(8,128)S(1)}, f3...) custom-call(bf16[192,1024]{1,0:T(8,128)(2,1)S(1)} %get-tuple-element, ...), custom_call_target="tpu_custom_call" | custom-call | tf_op jit(solution)/shard_map/fill/pallas_call | solution.py:53
  53.1 2.6 %collective-permute-done.refs_2_ = f32[96,128]{1,0:T(8,128)S(1)} collective-permute-done((f32[96,128]{1,0:T(8,128)S(1)}, f32[96,128]{1,0:T(8,128)S(1)}, u32[]{:S(2)}, u32[]{:S(2)}) %collective-permute-start) | collective-permute-done | bytes 49184 | tf_op jit(solution)/shard_map/ppermute | solution.py:614
  55.6 0.0 collective-permute-done.1.refs_3_
  55.6 0.0 collective-permute-done.2.refs_4_
  55.6 0.0 collective-permute-done.3.refs_5_
  55.7 2.1 %section.3 = (f32[2,96,384]{2,1,0:T(8,128)S(1)}, f32[16,96,128]{2,1,0:T(8,128)S(1)}, f32[64,1,1536]{2,1,0:T(1,128)S(1)}) custom-call(f32[2,96,384]{2,1,0:T(8,128)S(1)} %get-tuple-element.68.deck_ref.refs_0_.base_deck, f32[16,96,128]{2,1,0:T(8,128)S(1)} %get-tuple-element.71.refs_1_.base_back.refs_14_, f32[96,128]{1,0:T(8,128)S(1)} %collective-permute-done.refs_2_, ...), custom_call_target="tpu_custom_call" | custom-call | tf_op jit(solution)/shard_map/section/pallas_call | solution.py:53
  57.7 20.4 %all_to_all.22.got_ref = f32[64,1,1536]{2,1,0:T(1,128)S(1)} all-to-all(f32[64,1,1536]{2,1,0:T(1,128)S(1)} %get-tuple-element.85), channel_id=1, replica_groups=mesh['grid'=4,'gx'=8,'gy'=8] {'gy','gx'}, dimensions={0} | all-to-all | bytes 786432 | tf_op jit(solution)/shard_map/all_to_all | solution.py:537
  78.1 1.1 rim.4
  79.3 1.8 %collective-permute-start.6 = (f32[104,384]{1,0:T(8,128)S(1)}, f32[104,384]{1,0:T(8,128)S(1)}, u32[]{:S(2)}, u32[]{:S(2)}) collective-permute-start(f32[104,384]{1,0:T(8,128)S(1)} %get-tuple-element.94), channel_id=1, source_target_pairs={{1,2},{2,1},{3,4},{4,3},{5,6},{6,5},{7,8},{8,7},{9,10},{10,9},{11,... | collective-permute-start | bytes 479240 | tf_op jit(solution)/shard_map/ppermute | solution.py:612
  81.1 1.5 %collective-permute-start.7 = (f32[104,384]{1,0:T(8,128)S(1)}, f32[104,384]{1,0:T(8,128)S(1)}, u32[]{:S(2)}, u32[]{:S(2)}) collective-permute-start(f32[104,384]{1,0:T(8,128)S(1)} %get-tuple-element.95), channel_id=1, source_target_pairs={{0,1},{1,0},{2,3},{3,2},{4,5},{5,4},{6,7},{7,6},{8,9},{9,8},{10,11... | collective-permute-start | bytes 479240 | tf_op jit(solution)/shard_map/ppermute | solution.py:613
  82.6 0.0 collective-permute-start.4
  82.6 0.6 collective-permute-start.5
  83.2 1.8 %fill.4 = (f32[16,96,128]{2,1,0:T(8,128)S(1)}, f32[14,32,128]{2,1,0:T(8,128)S(1)}, f32[14,96,128]{2,1,0:T(8,128)S(1)}, f32[14,96,128]{2,1,0:T(8,128)S(1)}, f32[2...) custom-call(bf16[192,1024]{1,0:T(8,128)(2,1)S(1)} %get-tuple-element.89.got_pieces, ...), custom_call_target="tpu_custom_call" | custom-call | tf_op jit(solution)/shard_map/fill/pallas_call | solution.py:53
  85.0 3.8 %collective-permute-done.4.refs_2_ = f32[96,128]{1,0:T(8,128)S(1)} collective-permute-done((f32[96,128]{1,0:T(8,128)S(1)}, f32[96,128]{1,0:T(8,128)S(1)}, u32[]{:S(2)}, u32[]{:S(2)}) %collective-permute-start.4) | collective-permute-done | bytes 49184 | tf_op jit(solution)/shard_map/ppermute | solution.py:614
  88.7 0.0 collective-permute-done.5.refs_3_
  88.8 0.0 collective-permute-done.6.refs_4_
  88.8 0.0 collective-permute-done.7.refs_5_
  88.8 2.1 %section.4 = (f32[2,96,384]{2,1,0:T(8,128)S(1)}, f32[16,96,128]{2,1,0:T(8,128)S(1)}, f32[64,1,1536]{2,1,0:T(1,128)S(1)}) custom-call(f32[2,96,384]{2,1,0:T(8,128)S(1)} %get-tuple-element.88.deck_ref.refs_0_, f32[16,96,128]{2,1,0:T(8,128)S(1)} %get-tuple-element.91.refs_1_, f32[96,128]{1,0:T(8,128)S(1)} %collective-permute-done.4.refs_2_, ...), custom_call_target="tpu_custom_call" | custom-call | tf_op jit(solution)/shard_map/section/pallas_call | solution.py:53
  90.9 20.1 %all_to_all.23.got_ref = f32[64,1,1536]{2,1,0:T(1,128)S(1)} all-to-all(f32[64,1,1536]{2,1,0:T(1,128)S(1)} %get-tuple-element.102), channel_id=1, replica_groups=mesh['grid'=4,'gx'=8,'gy'=8] {'gy','gx'}, dimensions={0} | all-to-all | bytes 786432 | tf_op jit(solution)/shard_map/all_to_all | solution.py:537
  111.0 1.1 rim.5
  112.1 2.1 %collective-permute-start.10 = (f32[104,384]{1,0:T(8,128)S(1)}, f32[104,384]{1,0:T(8,128)S(1)}, u32[]{:S(2)}, u32[]{:S(2)}) collective-permute-start(f32[104,384]{1,0:T(8,128)S(1)} %get-tuple-element.110), channel_id=1, source_target_pairs={{1,2},{2,1},{3,4},{4,3},{5,6},{6,5},{7,8},{8,7},{9,10},{10,9},{11,... | collective-permute-start | bytes 479240 | tf_op jit(solution)/shard_map/ppermute | solution.py:612
  114.1 1.3 %collective-permute-start.11 = (f32[104,384]{1,0:T(8,128)S(1)}, f32[104,384]{1,0:T(8,128)S(1)}, u32[]{:S(2)}, u32[]{:S(2)}) collective-permute-start(f32[104,384]{1,0:T(8,128)S(1)} %get-tuple-element.111), channel_id=1, source_target_pairs={{0,1},{1,0},{2,3},{3,2},{4,5},{5,4},{6,7},{7,6},{8,9},{9,8},{10,11... | collective-permute-start | bytes 479240 | tf_op jit(solution)/shard_map/ppermute | solution.py:613
  115.4 0.0 collective-permute-start.8
  115.4 0.6 collective-permute-start.9
  116.0 1.8 %fill.5 = (f32[16,96,128]{2,1,0:T(8,128)S(1)}, f32[14,32,128]{2,1,0:T(8,128)S(1)}, f32[14,96,128]{2,1,0:T(8,128)S(1)}, f32[14,96,128]{2,1,0:T(8,128)S(1)}, f32[2...) custom-call(bf16[192,1024]{1,0:T(8,128)(2,1)S(1)} %get-tuple-element.106.got_pieces, ...), custom_call_target="tpu_custom_call" | custom-call | tf_op jit(solution)/shard_map/fill/pallas_call | solution.py:53
  117.8 3.9 %collective-permute-done.8.refs_2_ = f32[96,128]{1,0:T(8,128)S(1)} collective-permute-done((f32[96,128]{1,0:T(8,128)S(1)}, f32[96,128]{1,0:T(8,128)S(1)}, u32[]{:S(2)}, u32[]{:S(2)}) %collective-permute-start.8) | collective-permute-done | bytes 49184 | tf_op jit(solution)/shard_map/ppermute | solution.py:614
  121.7 0.0 collective-permute-done.9.refs_3_
  121.7 0.0 collective-permute-done.10.refs_4_
  121.7 0.0 collective-permute-done.11.refs_5_
  121.7 2.0 %section.5 = (f32[96,2,384]{2,1,0:T(2,128)}, f32[96,16,128]{2,1,0:T(8,128)}) custom-call(f32[2,96,384]{2,1,0:T(8,128)S(1)} %get-tuple-element.105.deck_ref.refs_0_, f32[16,96,128]{2,1,0:T(8,128)S(1)} %get-tuple-element.107.refs_1_, f32[96,128]{1,0:T(8,128)S(1)} %collective-permute-done.8.refs_2_, f32[96,128]{1,0:T(8,128)S(1)} %collective-permute-done.9.refs_3_, ...), custom_call_target="tpu_custom_call" | custom-call | tf_op jit(solution)/shard_map/section/pallas_call | solution.py:53
Async XLA Ops:
  0.6 49.5 %copy-start = (f32[4,2,384]{2,1,0:T(2,128)S(1)}, f32[4,2,384]{2,1,0:T(2,128)}, u32[]{:S(2)}) copy-start(f32[4,2,384]{2,1,0:T(2,128)} %refs_6_.5) | copy-start | bytes 36868
  46.1 9.5 %collective-permute-start.2 = (f32[104,384]{1,0:T(8,128)S(1)}, f32[104,384]{1,0:T(8,128)S(1)}, u32[]{:S(2)}, u32[]{:S(2)}) collective-permute-start(f32[104,384]{1,0:T(8,128)S(1)} %get-tuple-element.74), channel_id=1, source_target_pairs={{1,2},{2,1},{3,4},{4,3},{5,6},{6,5},{7,8},{8,7},{9,10},{10,9},{11,... | collective-permute-start | bytes 479240 | tf_op jit(solution)/shard_map/ppermute | solution.py:612
  47.8 7.8 %collective-permute-start.3 = (f32[104,384]{1,0:T(8,128)S(1)}, f32[104,384]{1,0:T(8,128)S(1)}, u32[]{:S(2)}, u32[]{:S(2)}) collective-permute-start(f32[104,384]{1,0:T(8,128)S(1)} %get-tuple-element.75), channel_id=1, source_target_pairs={{0,1},{1,0},{2,3},{3,2},{4,5},{5,4},{6,7},{7,6},{8,9},{9,8},{10,11... | collective-permute-start | bytes 479240 | tf_op jit(solution)/shard_map/ppermute | solution.py:613
  49.4 6.2 %collective-permute-start = (f32[96,128]{1,0:T(8,128)S(1)}, f32[96,128]{1,0:T(8,128)S(1)}, u32[]{:S(2)}, u32[]{:S(2)}) collective-permute-start(f32[96,128]{1,0:T(8,128)S(1)} %get-tuple-element.72), channel_id=1, source_target_pairs={{8,16},{16,8},{9,17},{17,9},{10,18},{18,10},{11,19},{19,11},{12,20... | collective-permute-start | bytes 147464 | tf_op jit(solution)/shard_map/ppermute | solution.py:614
  49.4 6.2 %collective-permute-start.1 = (f32[96,128]{1,0:T(8,128)S(1)}, f32[96,128]{1,0:T(8,128)S(1)}, u32[]{:S(2)}, u32[]{:S(2)}) collective-permute-start(f32[96,128]{1,0:T(8,128)S(1)} %get-tuple-element.73), channel_id=1, source_target_pairs={{0,8},{8,0},{1,9},{9,1},{2,10},{10,2},{3,11},{11,3},{4,12},{12,4},... | collective-permute-start | bytes 147464 | tf_op jit(solution)/shard_map/ppermute | solution.py:615
  79.3 9.5 %collective-permute-start.6 = (f32[104,384]{1,0:T(8,128)S(1)}, f32[104,384]{1,0:T(8,128)S(1)}, u32[]{:S(2)}, u32[]{:S(2)}) collective-permute-start(f32[104,384]{1,0:T(8,128)S(1)} %get-tuple-element.94), channel_id=1, source_target_pairs={{1,2},{2,1},{3,4},{4,3},{5,6},{6,5},{7,8},{8,7},{9,10},{10,9},{11,... | collective-permute-start | bytes 479240 | tf_op jit(solution)/shard_map/ppermute | solution.py:612
  81.1 7.7 %collective-permute-start.7 = (f32[104,384]{1,0:T(8,128)S(1)}, f32[104,384]{1,0:T(8,128)S(1)}, u32[]{:S(2)}, u32[]{:S(2)}) collective-permute-start(f32[104,384]{1,0:T(8,128)S(1)} %get-tuple-element.95), channel_id=1, source_target_pairs={{0,1},{1,0},{2,3},{3,2},{4,5},{5,4},{6,7},{7,6},{8,9},{9,8},{10,11... | collective-permute-start | bytes 479240 | tf_op jit(solution)/shard_map/ppermute | solution.py:613
  82.6 6.2 %collective-permute-start.4 = (f32[96,128]{1,0:T(8,128)S(1)}, f32[96,128]{1,0:T(8,128)S(1)}, u32[]{:S(2)}, u32[]{:S(2)}) collective-permute-start(f32[96,128]{1,0:T(8,128)S(1)} %get-tuple-element.92), channel_id=1, source_target_pairs={{8,16},{16,8},{9,17},{17,9},{10,18},{18,10},{11,19},{19,11},{12,20... | collective-permute-start | bytes 147464 | tf_op jit(solution)/shard_map/ppermute | solution.py:614
  82.6 6.2 %collective-permute-start.5 = (f32[96,128]{1,0:T(8,128)S(1)}, f32[96,128]{1,0:T(8,128)S(1)}, u32[]{:S(2)}, u32[]{:S(2)}) collective-permute-start(f32[96,128]{1,0:T(8,128)S(1)} %get-tuple-element.93), channel_id=1, source_target_pairs={{0,8},{8,0},{1,9},{9,1},{2,10},{10,2},{3,11},{11,3},{4,12},{12,4},... | collective-permute-start | bytes 147464 | tf_op jit(solution)/shard_map/ppermute | solution.py:615
  112.1 9.6 %collective-permute-start.10 = (f32[104,384]{1,0:T(8,128)S(1)}, f32[104,384]{1,0:T(8,128)S(1)}, u32[]{:S(2)}, u32[]{:S(2)}) collective-permute-start(f32[104,384]{1,0:T(8,128)S(1)} %get-tuple-element.110), channel_id=1, source_target_pairs={{1,2},{2,1},{3,4},{4,3},{5,6},{6,5},{7,8},{8,7},{9,10},{10,9},{11,... | collective-permute-start | bytes 479240 | tf_op jit(solution)/shard_map/ppermute | solution.py:612
  114.1 7.6 %collective-permute-start.11 = (f32[104,384]{1,0:T(8,128)S(1)}, f32[104,384]{1,0:T(8,128)S(1)}, u32[]{:S(2)}, u32[]{:S(2)}) collective-permute-start(f32[104,384]{1,0:T(8,128)S(1)} %get-tuple-element.111), channel_id=1, source_target_pairs={{0,1},{1,0},{2,3},{3,2},{4,5},{5,4},{6,7},{7,6},{8,9},{9,8},{10,11... | collective-permute-start | bytes 479240 | tf_op jit(solution)/shard_map/ppermute | solution.py:613
  115.4 6.3 %collective-permute-start.8 = (f32[96,128]{1,0:T(8,128)S(1)}, f32[96,128]{1,0:T(8,128)S(1)}, u32[]{:S(2)}, u32[]{:S(2)}) collective-permute-start(f32[96,128]{1,0:T(8,128)S(1)} %get-tuple-element.108), channel_id=1, source_target_pairs={{8,16},{16,8},{9,17},{17,9},{10,18},{18,10},{11,19},{19,11},{12,20... | collective-permute-start | bytes 147464 | tf_op jit(solution)/shard_map/ppermute | solution.py:614
  115.4 6.3 %collective-permute-start.9 = (f32[96,128]{1,0:T(8,128)S(1)}, f32[96,128]{1,0:T(8,128)S(1)}, u32[]{:S(2)}, u32[]{:S(2)}) collective-permute-start(f32[96,128]{1,0:T(8,128)S(1)} %get-tuple-element.109), channel_id=1, source_target_pairs={{0,8},{8,0},{1,9},{9,1},{2,10},{10,2},{3,11},{11,3},{4,12},{12,4},... | collective-permute-start | bytes 147464 | tf_op jit(solution)/shard_map/ppermute | solution.py:615

commit v6 on v5

--- a/solution.py
+++ b/solution.py
@@ -201,9 +201,9 @@
         pieces[128 + PLANES : 256, :] = gap
 
 
-def answer(far_ref, near_ref, deck_pieces, back_pieces, out_ref):
+def answer(far_ref, near_ref, deck_pieces, back_pieces, out_ref, quarters=range(CAP // 4)):
     lane = iota((MEMBERS, 128), 1)
-    for q in range(CAP // 4):
+    for q in quarters:
         got = dot(far_ref[q * 256 : (q + 1) * 256, :], deck_pieces[...], NT)
         if q == 0:
             got = got + dot(near_ref[...], back_pieces[...], NT)
@@ -522,11 +522,13 @@
             send(back_out, r, back_hbm, back_sems)
         else:
             stack_back(back_pieces, r, jnp.concatenate(new, axis=0))
+            if r in (1, 5, 9):
+                answer(far_ref, near_ref, deck_pieces, back_pieces, answer_out, [(r + 3) // 4])
     if last:
         for c in copies:
             c.wait()
     else:
-        answer(far_ref, near_ref, deck_pieces, back_pieces, answer_out)
+        answer(far_ref, near_ref, deck_pieces, back_pieces, answer_out, [0])
 
 
 def local(deck_fields, back_fields, metrics, donors, stencil, fringe_cells):

time: 124 us -> 124 us (level)
  no operation moved by 1% of the time
where the time goes in v6:
time: 124 us
  blocking collectives  80.6 us (65%)
  Pallas kernels  20.2 us (16%)
  starting transfers between devices  11.9 us (10%)
  waiting for transfers between devices  10.2 us (8%)
    all_to_all x4, blocking collectives, exchange(): return lax.all_to_all(x, group, split_axis=0, concat_axis=0, tiled=True)  80.6 us
    pallas_call x11, Pallas kernels, call(): pl.pallas_call(kernel, out_shape=tuple((jax.ShapeDtypeStruct(s, d) for s,...  20.2 us
    ppermute x3, waiting for transfers between devices, local(): column_first = lax.ppermute(column_first, everyone, pairs(across_y, 1))  10.2 us
    ppermute x3, starting transfers between devices, local(): row_first = lax.ppermute(row_first, everyone, pairs(1, 1, True))  5.57 us
    ppermute x3, starting transfers between devices, local(): row_second = lax.ppermute(row_second, everyone, pairs(1, 0, True))  4.3 us
  transfers between devices with their start and end apart: 12, of which 3 were waited for; matrix products, arithmetic and copies ran while one was open for 0% of the time, Pallas kernels for 5%

profile of v6, /device:TPU:8, one launch (start us, length us, event | category | flops | bytes accessed | tf_op | source)
XLA Modules:
  0.0 123.8 jit_solution(512632355564864707)
XLA Ops:
  0.6 0.0 copy-start
  0.6 1.8 %route.1 = (f32[64,1,128]{2,1,0:T(1,128)S(1)}, f32[64,48]{1,0:T(8,128)S(1)}, bf16[1024,384]{1,0:T(8,128)(2,1)S(1)}, bf16[256,256]{1,0:T(8,128)(2,1)S(1)}, f32[3,8,128]{2,1,0:T(8,128)S(1)}) custom-call(s32[1,512]{1,0:T(1,128)} %bitcast.11, s32[4,512]{1,0:T(4,128)} %bitcast.10, s32[1,508]{1,0:T(1,128)} %cells_hbm.1), custom_call_target="tpu_custom_call" | custom-call | tf_op jit(solution)/shard_map/route/pallas_call | solution.py:53
  2.4 21.3 %all_to_all.20.request_ref = f32[64,1,128]{2,1,0:T(1,128)S(1)} all-to-all(f32[64,1,128]{2,1,0:T(1,128)S(1)} %get-tuple-element.61), channel_id=1, replica_groups=mesh['grid'=4,'gx'=8,'gy'=8] {'gy','gx'}, dimensions={0} | all-to-all | bytes 65536 | tf_op jit(solution)/shard_map/all_to_all | solution.py:539
  23.7 2.5 %first_answer.1 = (f32[2,96,384]{2,1,0:T(8,128)S(1)}, f32[16,96,128]{2,1,0:T(8,128)S(1)}, bf16[1024,768]{1,0:T(8,128)(2,1)S(1)}, bf16[256,2048]{1,0:T(8,128)(2,1)S(1)}, f32[64,1,1536]{2,1,0:T(1,128)S(1)}) custom-call(f32[64,1,128]{2,1,0:T(1,128)S(1)} %all_to_all.20.request_ref, f32[96,2,384]{2,1,0:T(2,128)} %bitcast.9, f32[96,16,128]{2,1,0:T(8,128)} %bitcast.8), custom_call_target="tpu_custom_call" | custom-call | tf_op jit(solution)/shard_map/first_answer/pallas_call | solution.py:53
  26.3 18.7 %all_to_all.21.got_ref = f32[64,1,1536]{2,1,0:T(1,128)S(1)} all-to-all(f32[64,1,1536]{2,1,0:T(1,128)S(1)} %get-tuple-element.62), channel_id=1, replica_groups=mesh['grid'=4,'gx'=8,'gy'=8] {'gy','gx'}, dimensions={0} | all-to-all | bytes 786432 | tf_op jit(solution)/shard_map/all_to_all | solution.py:539
  45.0 1.1 rim.3
  46.1 1.7 %collective-permute-start.2 = (f32[104,384]{1,0:T(8,128)S(1)}, f32[104,384]{1,0:T(8,128)S(1)}, u32[]{:S(2)}, u32[]{:S(2)}) collective-permute-start(f32[104,384]{1,0:T(8,128)S(1)} %get-tuple-element.74), channel_id=1, source_target_pairs={{1,2},{2,1},{3,4},{4,3},{5,6},{6,5},{7,8},{8,7},{9,10},{10,9},{11,... | collective-permute-start | bytes 479240 | tf_op jit(solution)/shard_map/ppermute | solution.py:614
  47.8 1.6 %collective-permute-start.3 = (f32[104,384]{1,0:T(8,128)S(1)}, f32[104,384]{1,0:T(8,128)S(1)}, u32[]{:S(2)}, u32[]{:S(2)}) collective-permute-start(f32[104,384]{1,0:T(8,128)S(1)} %get-tuple-element.75), channel_id=1, source_target_pairs={{0,1},{1,0},{2,3},{3,2},{4,5},{5,4},{6,7},{7,6},{8,9},{9,8},{10,11... | collective-permute-start | bytes 479240 | tf_op jit(solution)/shard_map/ppermute | solution.py:615
  49.4 0.0 collective-permute-start
  49.4 0.7 collective-permute-start.1
  50.1 0.0 copy-done
  50.1 2.9 %fill.3 = (f32[16,96,128]{2,1,0:T(8,128)S(1)}, bf16[1024,2048]{1,0:T(8,128)(2,1)S(1)}, f32[16,8,128]{2,1,0:T(8,128)S(1)}, f32[14,32,128]{2,1,0:T(8,128)S(1)}, f3...) custom-call(bf16[192,1024]{1,0:T(8,128)(2,1)S(1)} %get-tuple-element, ...), custom_call_target="tpu_custom_call" | custom-call | tf_op jit(solution)/shard_map/fill/pallas_call | solution.py:53
  53.1 2.6 %collective-permute-done.refs_2_ = f32[96,128]{1,0:T(8,128)S(1)} collective-permute-done((f32[96,128]{1,0:T(8,128)S(1)}, f32[96,128]{1,0:T(8,128)S(1)}, u32[]{:S(2)}, u32[]{:S(2)}) %collective-permute-start) | collective-permute-done | bytes 49184 | tf_op jit(solution)/shard_map/ppermute | solution.py:616
  55.6 0.0 collective-permute-done.1.refs_3_
  55.6 0.0 collective-permute-done.2.refs_4_
  55.6 0.0 collective-permute-done.3.refs_5_
  55.7 2.0 %section.3 = (f32[2,96,384]{2,1,0:T(8,128)S(1)}, f32[16,96,128]{2,1,0:T(8,128)S(1)}, f32[64,1,1536]{2,1,0:T(1,128)S(1)}) custom-call(f32[2,96,384]{2,1,0:T(8,128)S(1)} %get-tuple-element.68.deck_ref.refs_0_.base_deck, f32[16,96,128]{2,1,0:T(8,128)S(1)} %get-tuple-element.71.refs_1_.base_back.refs_14_, f32[96,128]{1,0:T(8,128)S(1)} %collective-permute-done.refs_2_, ...), custom_call_target="tpu_custom_call" | custom-call | tf_op jit(solution)/shard_map/section/pallas_call | solution.py:53
  57.7 20.4 %all_to_all.22.got_ref = f32[64,1,1536]{2,1,0:T(1,128)S(1)} all-to-all(f32[64,1,1536]{2,1,0:T(1,128)S(1)} %get-tuple-element.85), channel_id=1, replica_groups=mesh['grid'=4,'gx'=8,'gy'=8] {'gy','gx'}, dimensions={0} | all-to-all | bytes 786432 | tf_op jit(solution)/shard_map/all_to_all | solution.py:539
  78.1 1.1 rim.4
  79.2 1.8 %collective-permute-start.6 = (f32[104,384]{1,0:T(8,128)S(1)}, f32[104,384]{1,0:T(8,128)S(1)}, u32[]{:S(2)}, u32[]{:S(2)}) collective-permute-start(f32[104,384]{1,0:T(8,128)S(1)} %get-tuple-element.94), channel_id=1, source_target_pairs={{1,2},{2,1},{3,4},{4,3},{5,6},{6,5},{7,8},{8,7},{9,10},{10,9},{11,... | collective-permute-start | bytes 479240 | tf_op jit(solution)/shard_map/ppermute | solution.py:614
  81.0 1.5 %collective-permute-start.7 = (f32[104,384]{1,0:T(8,128)S(1)}, f32[104,384]{1,0:T(8,128)S(1)}, u32[]{:S(2)}, u32[]{:S(2)}) collective-permute-start(f32[104,384]{1,0:T(8,128)S(1)} %get-tuple-element.95), channel_id=1, source_target_pairs={{0,1},{1,0},{2,3},{3,2},{4,5},{5,4},{6,7},{7,6},{8,9},{9,8},{10,11... | collective-permute-start | bytes 479240 | tf_op jit(solution)/shard_map/ppermute | solution.py:615
  82.5 0.0 collective-permute-start.4
  82.5 0.6 collective-permute-start.5
  83.1 1.8 %fill.4 = (f32[16,96,128]{2,1,0:T(8,128)S(1)}, f32[14,32,128]{2,1,0:T(8,128)S(1)}, f32[14,96,128]{2,1,0:T(8,128)S(1)}, f32[14,96,128]{2,1,0:T(8,128)S(1)}, f32[2...) custom-call(bf16[192,1024]{1,0:T(8,128)(2,1)S(1)} %get-tuple-element.89.got_pieces, ...), custom_call_target="tpu_custom_call" | custom-call | tf_op jit(solution)/shard_map/fill/pallas_call | solution.py:53
  84.9 3.8 %collective-permute-done.4.refs_2_ = f32[96,128]{1,0:T(8,128)S(1)} collective-permute-done((f32[96,128]{1,0:T(8,128)S(1)}, f32[96,128]{1,0:T(8,128)S(1)}, u32[]{:S(2)}, u32[]{:S(2)}) %collective-permute-start.4) | collective-permute-done | bytes 49184 | tf_op jit(solution)/shard_map/ppermute | solution.py:616
  88.7 0.0 collective-permute-done.5.refs_3_
  88.7 0.0 collective-permute-done.6.refs_4_
  88.7 0.0 collective-permute-done.7.refs_5_
  88.7 2.0 %section.4 = (f32[2,96,384]{2,1,0:T(8,128)S(1)}, f32[16,96,128]{2,1,0:T(8,128)S(1)}, f32[64,1,1536]{2,1,0:T(1,128)S(1)}) custom-call(f32[2,96,384]{2,1,0:T(8,128)S(1)} %get-tuple-element.88.deck_ref.refs_0_, f32[16,96,128]{2,1,0:T(8,128)S(1)} %get-tuple-element.91.refs_1_, f32[96,128]{1,0:T(8,128)S(1)} %collective-permute-done.4.refs_2_, ...), custom_call_target="tpu_custom_call" | custom-call | tf_op jit(solution)/shard_map/section/pallas_call | solution.py:53
  90.7 20.1 %all_to_all.23.got_ref = f32[64,1,1536]{2,1,0:T(1,128)S(1)} all-to-all(f32[64,1,1536]{2,1,0:T(1,128)S(1)} %get-tuple-element.102), channel_id=1, replica_groups=mesh['grid'=4,'gx'=8,'gy'=8] {'gy','gx'}, dimensions={0} | all-to-all | bytes 786432 | tf_op jit(solution)/shard_map/all_to_all | solution.py:539
  110.8 1.1 rim.5
  112.0 2.1 %collective-permute-start.10 = (f32[104,384]{1,0:T(8,128)S(1)}, f32[104,384]{1,0:T(8,128)S(1)}, u32[]{:S(2)}, u32[]{:S(2)}) collective-permute-start(f32[104,384]{1,0:T(8,128)S(1)} %get-tuple-element.110), channel_id=1, source_target_pairs={{1,2},{2,1},{3,4},{4,3},{5,6},{6,5},{7,8},{8,7},{9,10},{10,9},{11,... | collective-permute-start | bytes 479240 | tf_op jit(solution)/shard_map/ppermute | solution.py:614
  114.0 1.2 %collective-permute-start.11 = (f32[104,384]{1,0:T(8,128)S(1)}, f32[104,384]{1,0:T(8,128)S(1)}, u32[]{:S(2)}, u32[]{:S(2)}) collective-permute-start(f32[104,384]{1,0:T(8,128)S(1)} %get-tuple-element.111), channel_id=1, source_target_pairs={{0,1},{1,0},{2,3},{3,2},{4,5},{5,4},{6,7},{7,6},{8,9},{9,8},{10,11... | collective-permute-start | bytes 479240 | tf_op jit(solution)/shard_map/ppermute | solution.py:615
  115.3 0.0 collective-permute-start.8
  115.3 0.6 collective-permute-start.9
  115.9 1.8 %fill.5 = (f32[16,96,128]{2,1,0:T(8,128)S(1)}, f32[14,32,128]{2,1,0:T(8,128)S(1)}, f32[14,96,128]{2,1,0:T(8,128)S(1)}, f32[14,96,128]{2,1,0:T(8,128)S(1)}, f32[2...) custom-call(bf16[192,1024]{1,0:T(8,128)(2,1)S(1)} %get-tuple-element.106.got_pieces, ...), custom_call_target="tpu_custom_call" | custom-call | tf_op jit(solution)/shard_map/fill/pallas_call | solution.py:53
  117.7 3.9 %collective-permute-done.8.refs_2_ = f32[96,128]{1,0:T(8,128)S(1)} collective-permute-done((f32[96,128]{1,0:T(8,128)S(1)}, f32[96,128]{1,0:T(8,128)S(1)}, u32[]{:S(2)}, u32[]{:S(2)}) %collective-permute-start.8) | collective-permute-done | bytes 49184 | tf_op jit(solution)/shard_map/ppermute | solution.py:616
  121.6 0.0 collective-permute-done.9.refs_3_
  121.6 0.0 collective-permute-done.10.refs_4_
  121.6 0.0 collective-permute-done.11.refs_5_
  121.6 2.0 %section.5 = (f32[96,2,384]{2,1,0:T(2,128)}, f32[96,16,128]{2,1,0:T(8,128)}) custom-call(f32[2,96,384]{2,1,0:T(8,128)S(1)} %get-tuple-element.105.deck_ref.refs_0_, f32[16,96,128]{2,1,0:T(8,128)S(1)} %get-tuple-element.107.refs_1_, f32[96,128]{1,0:T(8,128)S(1)} %collective-permute-done.8.refs_2_, f32[96,128]{1,0:T(8,128)S(1)} %collective-permute-done.9.refs_3_, ...), custom_call_target="tpu_custom_call" | custom-call | tf_op jit(solution)/shard_map/section/pallas_call | solution.py:53
Async XLA Ops:
  0.6 49.5 %copy-start = (f32[4,2,384]{2,1,0:T(2,128)S(1)}, f32[4,2,384]{2,1,0:T(2,128)}, u32[]{:S(2)}) copy-start(f32[4,2,384]{2,1,0:T(2,128)} %refs_6_.5) | copy-start | bytes 36868
  46.1 9.5 %collective-permute-start.2 = (f32[104,384]{1,0:T(8,128)S(1)}, f32[104,384]{1,0:T(8,128)S(1)}, u32[]{:S(2)}, u32[]{:S(2)}) collective-permute-start(f32[104,384]{1,0:T(8,128)S(1)} %get-tuple-element.74), channel_id=1, source_target_pairs={{1,2},{2,1},{3,4},{4,3},{5,6},{6,5},{7,8},{8,7},{9,10},{10,9},{11,... | collective-permute-start | bytes 479240 | tf_op jit(solution)/shard_map/ppermute | solution.py:614
  47.8 7.8 %collective-permute-start.3 = (f32[104,384]{1,0:T(8,128)S(1)}, f32[104,384]{1,0:T(8,128)S(1)}, u32[]{:S(2)}, u32[]{:S(2)}) collective-permute-start(f32[104,384]{1,0:T(8,128)S(1)} %get-tuple-element.75), channel_id=1, source_target_pairs={{0,1},{1,0},{2,3},{3,2},{4,5},{5,4},{6,7},{7,6},{8,9},{9,8},{10,11... | collective-permute-start | bytes 479240 | tf_op jit(solution)/shard_map/ppermute | solution.py:615
  49.4 6.2 %collective-permute-start = (f32[96,128]{1,0:T(8,128)S(1)}, f32[96,128]{1,0:T(8,128)S(1)}, u32[]{:S(2)}, u32[]{:S(2)}) collective-permute-start(f32[96,128]{1,0:T(8,128)S(1)} %get-tuple-element.72), channel_id=1, source_target_pairs={{8,16},{16,8},{9,17},{17,9},{10,18},{18,10},{11,19},{19,11},{12,20... | collective-permute-start | bytes 147464 | tf_op jit(solution)/shard_map/ppermute | solution.py:616
  49.4 6.2 %collective-permute-start.1 = (f32[96,128]{1,0:T(8,128)S(1)}, f32[96,128]{1,0:T(8,128)S(1)}, u32[]{:S(2)}, u32[]{:S(2)}) collective-permute-start(f32[96,128]{1,0:T(8,128)S(1)} %get-tuple-element.73), channel_id=1, source_target_pairs={{0,8},{8,0},{1,9},{9,1},{2,10},{10,2},{3,11},{11,3},{4,12},{12,4},... | collective-permute-start | bytes 147464 | tf_op jit(solution)/shard_map/ppermute | solution.py:617
  79.2 9.5 %collective-permute-start.6 = (f32[104,384]{1,0:T(8,128)S(1)}, f32[104,384]{1,0:T(8,128)S(1)}, u32[]{:S(2)}, u32[]{:S(2)}) collective-permute-start(f32[104,384]{1,0:T(8,128)S(1)} %get-tuple-element.94), channel_id=1, source_target_pairs={{1,2},{2,1},{3,4},{4,3},{5,6},{6,5},{7,8},{8,7},{9,10},{10,9},{11,... | collective-permute-start | bytes 479240 | tf_op jit(solution)/shard_map/ppermute | solution.py:614
  81.0 7.7 %collective-permute-start.7 = (f32[104,384]{1,0:T(8,128)S(1)}, f32[104,384]{1,0:T(8,128)S(1)}, u32[]{:S(2)}, u32[]{:S(2)}) collective-permute-start(f32[104,384]{1,0:T(8,128)S(1)} %get-tuple-element.95), channel_id=1, source_target_pairs={{0,1},{1,0},{2,3},{3,2},{4,5},{5,4},{6,7},{7,6},{8,9},{9,8},{10,11... | collective-permute-start | bytes 479240 | tf_op jit(solution)/shard_map/ppermute | solution.py:615
  82.5 6.2 %collective-permute-start.4 = (f32[96,128]{1,0:T(8,128)S(1)}, f32[96,128]{1,0:T(8,128)S(1)}, u32[]{:S(2)}, u32[]{:S(2)}) collective-permute-start(f32[96,128]{1,0:T(8,128)S(1)} %get-tuple-element.92), channel_id=1, source_target_pairs={{8,16},{16,8},{9,17},{17,9},{10,18},{18,10},{11,19},{19,11},{12,20... | collective-permute-start | bytes 147464 | tf_op jit(solution)/shard_map/ppermute | solution.py:616
  82.5 6.2 %collective-permute-start.5 = (f32[96,128]{1,0:T(8,128)S(1)}, f32[96,128]{1,0:T(8,128)S(1)}, u32[]{:S(2)}, u32[]{:S(2)}) collective-permute-start(f32[96,128]{1,0:T(8,128)S(1)} %get-tuple-element.93), channel_id=1, source_target_pairs={{0,8},{8,0},{1,9},{9,1},{2,10},{10,2},{3,11},{11,3},{4,12},{12,4},... | collective-permute-start | bytes 147464 | tf_op jit(solution)/shard_map/ppermute | solution.py:617
  112.0 9.6 %collective-permute-start.10 = (f32[104,384]{1,0:T(8,128)S(1)}, f32[104,384]{1,0:T(8,128)S(1)}, u32[]{:S(2)}, u32[]{:S(2)}) collective-permute-start(f32[104,384]{1,0:T(8,128)S(1)} %get-tuple-element.110), channel_id=1, source_target_pairs={{1,2},{2,1},{3,4},{4,3},{5,6},{6,5},{7,8},{8,7},{9,10},{10,9},{11,... | collective-permute-start | bytes 479240 | tf_op jit(solution)/shard_map/ppermute | solution.py:614
  114.0 7.6 %collective-permute-start.11 = (f32[104,384]{1,0:T(8,128)S(1)}, f32[104,384]{1,0:T(8,128)S(1)}, u32[]{:S(2)}, u32[]{:S(2)}) collective-permute-start(f32[104,384]{1,0:T(8,128)S(1)} %get-tuple-element.111), channel_id=1, source_target_pairs={{0,1},{1,0},{2,3},{3,2},{4,5},{5,4},{6,7},{7,6},{8,9},{9,8},{10,11... | collective-permute-start | bytes 479240 | tf_op jit(solution)/shard_map/ppermute | solution.py:615
  115.3 6.3 %collective-permute-start.8 = (f32[96,128]{1,0:T(8,128)S(1)}, f32[96,128]{1,0:T(8,128)S(1)}, u32[]{:S(2)}, u32[]{:S(2)}) collective-permute-start(f32[96,128]{1,0:T(8,128)S(1)} %get-tuple-element.108), channel_id=1, source_target_pairs={{8,16},{16,8},{9,17},{17,9},{10,18},{18,10},{11,19},{19,11},{12,20... | collective-permute-start | bytes 147464 | tf_op jit(solution)/shard_map/ppermute | solution.py:616
  115.3 6.3 %collective-permute-start.9 = (f32[96,128]{1,0:T(8,128)S(1)}, f32[96,128]{1,0:T(8,128)S(1)}, u32[]{:S(2)}, u32[]{:S(2)}) collective-permute-start(f32[96,128]{1,0:T(8,128)S(1)} %get-tuple-element.109), channel_id=1, source_target_pairs={{0,8},{8,0},{1,9},{9,1},{2,10},{10,2},{3,11},{11,3},{4,12},{12,4},... | collective-permute-start | bytes 147464 | tf_op jit(solution)/shard_map/ppermute | solution.py:617

commit v7 on v5

--- a/solution.py
+++ b/solution.py
@@ -303,8 +303,8 @@
     section, got_pieces, fill_ref, keep_ref, back_ref, deck_ref, metric_ref, base_deck, base_back, back_out, *inner
 ):
     fill_rows(got_pieces, fill_ref, keep_ref, back_ref, back_out)
-    inner_rows(section, back_out, keep_ref, base_back, *inner[:3])
-    deck_inner(section, deck_ref, metric_ref, base_deck, *inner[3:])
+    inner_rows(section, back_out, keep_ref, base_back, *inner[:4])
+    deck_inner(section, deck_ref, metric_ref, base_deck, *inner[4:])
 
 
 def first_fill_kernel(
@@ -325,8 +325,8 @@
     for r in range(ROWS):
         keep_ref[r] = kept(listed[r])
     fill_rows(got_pieces, fill_ref, keep_ref, back_ref, back_out)
-    inner_rows(0, back_out, keep_ref, None, *inner[:3])
-    deck_inner(0, deck_ref, metric_ref, None, *inner[3:])
+    inner_rows(0, back_out, keep_ref, None, *inner[:4])
+    deck_inner(0, deck_ref, metric_ref, None, *inner[4:])
 
 
 def deck_metric(metric_ref, r):
@@ -404,21 +404,21 @@
     return strain, lap, rest
 
 
-def outer_part(here, minus_eta, plus_eta, part, keep, section):
+def outer_part(speed, b, around, part, keep, section):
     strain, lap, rest = part
     step = (WEIGHTS[section] * TIME_STEP) * keep
-    b = [plus_eta[c] - minus_eta[c] for c in range(3)]
     strain = strain + (b[0] * b[0] + b[1] * b[1] + b[2] * b[2])
     stretched = 1.0 + 0.25 * strain
     viscosity = (SMAGORINSKY * step) * (stretched * lax.rsqrt(stretched))
-    speed_eta = (0.5 * step) * here[1]
+    speed_eta = (0.5 * step) * speed
     return [
-        rest[c] + (viscosity * (lap[c] + (plus_eta[c] + minus_eta[c])) - speed_eta * b[c])
+        rest[c] + (viscosity * (lap[c] + around[c]) - speed_eta * b[c])
         for c in range(3)
     ]
 
 
-def inner_rows(section, back_ref, keep_ref, base_ref, strain_out, lap_out, rest_out):
+def inner_rows(section, back_ref, keep_ref, base_ref, strain_out, lap_out, rest_out, b_out):
+    lane = iota((SPAN, COLS), 1)
     for r in range(1, ROWS - 1):
         strain, lap, rest = inner_part(
             fields(back_ref, (r,)),
@@ -430,7 +430,11 @@
         )
         strain_out[r - 1] = strain
         for c in range(3):
-            lap_out[r - 1, c * SPAN : (c + 1) * SPAN, :] = lap[c]
+            f = back_ref[r, c * SPAN : (c + 1) * SPAN, :]
+            plus_eta = jnp.where(lane == COLS - 1, 0.0, pltpu.roll(f, COLS - 1, 1))
+            minus_eta = jnp.where(lane == 0, 0.0, pltpu.roll(f, 1, 1))
+            b_out[r - 1, c * SPAN : (c + 1) * SPAN, :] = plus_eta - minus_eta
+            lap_out[r - 1, c * SPAN : (c + 1) * SPAN, :] = lap[c] + (plus_eta + minus_eta)
             rest_out[r - 1, c * SPAN : (c + 1) * SPAN, :] = rest[c]
 
 
@@ -441,8 +445,8 @@
 def section_kernel(section, *refs):
     refs = list(refs)
     deck_ref, back_ref, column_first, column_second, row_first, row_second, metric_ref, keep_ref = refs[:8]
-    strain_ref, lap_ref, rest_ref, deck_strain, deck_lap, deck_rest = refs[8:14]
-    del refs[:14]
+    strain_ref, lap_ref, rest_ref, b_ref, deck_strain, deck_lap, deck_rest = refs[8:15]
+    del refs[:15]
     base_back = None
     if section > 0:
         base_back = refs[0]
@@ -500,22 +504,25 @@
             stack_deck(deck_pieces, r, jnp.concatenate(new, axis=0))
     lane = iota((SPAN, COLS), 1)
     for r in range(ROWS):
-        here = fields(back_ref, (r,))
-        plus_eta, minus_eta = [], []
-        for c in range(3):
-            from_west = beside[0][spans[c], r : r + 1] * west_end
-            from_east = beside[1][spans[c], r : r + 1] * east_end
-            plus_eta.append(jnp.where(lane == COLS - 1, from_east, pltpu.roll(here[c], COLS - 1, 1)))
-            minus_eta.append(jnp.where(lane == 0, from_west, pltpu.roll(here[c], 1, 1)))
         keep = keep_ref[r, 0:1, :]
+        west = [beside[0][at, r : r + 1] * west_end for at in spans]
+        east = [beside[1][at, r : r + 1] * east_end for at in spans]
         if 0 < r < ROWS - 1:
             part = strain_ref[r - 1], fields(lap_ref, (r - 1,)), fields(rest_ref, (r - 1,))
+            inside = fields(b_ref, (r - 1,))
+            b = [inside[c] + jnp.where(lane == COLS - 1, east[c], jnp.where(lane == 0, -west[c], 0.0)) for c in range(3)]
+            around = [jnp.where(lane == COLS - 1, east[c], jnp.where(lane == 0, west[c], 0.0)) for c in range(3)]
         else:
+            here = fields(back_ref, (r,))
+            plus_eta = [jnp.where(lane == COLS - 1, east[c], pltpu.roll(here[c], COLS - 1, 1)) for c in range(3)]
+            minus_eta = [jnp.where(lane == 0, west[c], pltpu.roll(here[c], 1, 1)) for c in range(3)]
             minus = fields(back_ref, (r - 1,)) if r > 0 else [a[0] for a in along]
             plus = fields(back_ref, (r + 1,)) if r < ROWS - 1 else [a[1] for a in along]
             base = fields(base_back, (r,)) if section > 0 else None
             part = inner_part(here, minus, plus, keep, base, section)
-        new = outer_part(here, minus_eta, plus_eta, part, keep, section)
+            b = [plus_eta[c] - minus_eta[c] for c in range(3)]
+            around = [plus_eta[c] + minus_eta[c] for c in range(3)]
+        new = outer_part(back_ref[r, spans[1], :], b, around, part, keep, section)
         for c in range(3):
             back_out[r, c * SPAN : (c + 1) * SPAN, :] = new[c]
         if last:
@@ -617,6 +624,7 @@
             ((ROWS - 2, SPAN, COLS), F32),
             ((ROWS - 2, PLANES, COLS), F32),
             ((ROWS - 2, PLANES, COLS), F32),
+            ((ROWS - 2, PLANES, COLS), F32),
             ((DROWS, SPAN, DCOLS), F32),
             ((DROWS, PLANES, DCOLS), F32),
             ((DROWS, PLANES, DCOLS), F32),

time: 124 us -> 124 us (level)
  no operation moved by 1% of the time
where the time goes in v7:
time: 124 us; the launch traced here: 123 us
  blocking collectives  80.7 us (65%)
  Pallas kernels  19.7 us (16%)
  starting transfers between devices  11.9 us (10%)
  waiting for transfers between devices  10.3 us (8%)
    all_to_all x4, blocking collectives, exchange(): return lax.all_to_all(x, group, split_axis=0, concat_axis=0, tiled=True)  80.7 us
    pallas_call x11, Pallas kernels, call(): pl.pallas_call(kernel, out_shape=tuple((jax.ShapeDtypeStruct(s, d) for s,...  19.7 us
    ppermute x3, waiting for transfers between devices, local(): column_first = lax.ppermute(column_first, everyone, pairs(across_y, 1))  10.3 us
    ppermute x3, starting transfers between devices, local(): row_first = lax.ppermute(row_first, everyone, pairs(1, 1, True))  5.55 us
    ppermute x3, starting transfers between devices, local(): row_second = lax.ppermute(row_second, everyone, pairs(1, 0, True))  4.33 us
  transfers between devices with their start and end apart: 12, of which 3 were waited for; matrix products, arithmetic and copies ran while one was open for 0% of the time, Pallas kernels for 5%

profile of v7, /device:TPU:8, one launch (start us, length us, event | category | flops | bytes accessed | tf_op | source)
XLA Modules:
  0.0 123.5 jit_solution(11912784367213170958)
XLA Ops:
  0.6 0.0 copy-start
  0.6 1.8 %route.1 = (f32[64,1,128]{2,1,0:T(1,128)S(1)}, f32[64,48]{1,0:T(8,128)S(1)}, bf16[1024,384]{1,0:T(8,128)(2,1)S(1)}, bf16[256,256]{1,0:T(8,128)(2,1)S(1)}, f32[3,8,128]{2,1,0:T(8,128)S(1)}) custom-call(s32[1,512]{1,0:T(1,128)} %bitcast.11, s32[4,512]{1,0:T(4,128)} %bitcast.10, s32[1,508]{1,0:T(1,128)} %cells_hbm.1), custom_call_target="tpu_custom_call" | custom-call | tf_op jit(solution)/shard_map/route/pallas_call | solution.py:53
  2.4 21.3 %all_to_all.20.request_ref = f32[64,1,128]{2,1,0:T(1,128)S(1)} all-to-all(f32[64,1,128]{2,1,0:T(1,128)S(1)} %get-tuple-element.64), channel_id=1, replica_groups=mesh['grid'=4,'gx'=8,'gy'=8] {'gy','gx'}, dimensions={0} | all-to-all | bytes 65536 | tf_op jit(solution)/shard_map/all_to_all | solution.py:544
  23.7 2.5 %first_answer.1 = (f32[2,96,384]{2,1,0:T(8,128)S(1)}, f32[16,96,128]{2,1,0:T(8,128)S(1)}, bf16[1024,768]{1,0:T(8,128)(2,1)S(1)}, bf16[256,2048]{1,0:T(8,128)(2,1)S(1)}, f32[64,1,1536]{2,1,0:T(1,128)S(1)}) custom-call(f32[64,1,128]{2,1,0:T(1,128)S(1)} %all_to_all.20.request_ref, f32[96,2,384]{2,1,0:T(2,128)} %bitcast.9, f32[96,16,128]{2,1,0:T(8,128)} %bitcast.8), custom_call_target="tpu_custom_call" | custom-call | tf_op jit(solution)/shard_map/first_answer/pallas_call | solution.py:53
  26.3 18.7 %all_to_all.21.got_ref = f32[64,1,1536]{2,1,0:T(1,128)S(1)} all-to-all(f32[64,1,1536]{2,1,0:T(1,128)S(1)} %get-tuple-element.65), channel_id=1, replica_groups=mesh['grid'=4,'gx'=8,'gy'=8] {'gy','gx'}, dimensions={0} | all-to-all | bytes 786432 | tf_op jit(solution)/shard_map/all_to_all | solution.py:544
  45.0 1.1 rim.3
  46.1 1.7 %collective-permute-start.2 = (f32[104,384]{1,0:T(8,128)S(1)}, f32[104,384]{1,0:T(8,128)S(1)}, u32[]{:S(2)}, u32[]{:S(2)}) collective-permute-start(f32[104,384]{1,0:T(8,128)S(1)} %get-tuple-element.77), channel_id=1, source_target_pairs={{1,2},{2,1},{3,4},{4,3},{5,6},{6,5},{7,8},{8,7},{9,10},{10,9},{11,... | collective-permute-start | bytes 479240 | tf_op jit(solution)/shard_map/ppermute | solution.py:619
  47.9 1.5 %collective-permute-start.3 = (f32[104,384]{1,0:T(8,128)S(1)}, f32[104,384]{1,0:T(8,128)S(1)}, u32[]{:S(2)}, u32[]{:S(2)}) collective-permute-start(f32[104,384]{1,0:T(8,128)S(1)} %get-tuple-element.78), channel_id=1, source_target_pairs={{0,1},{1,0},{2,3},{3,2},{4,5},{5,4},{6,7},{7,6},{8,9},{9,8},{10,11... | collective-permute-start | bytes 479240 | tf_op jit(solution)/shard_map/ppermute | solution.py:620
  49.4 0.0 collective-permute-start
  49.4 0.7 collective-permute-start.1
  50.1 0.0 copy-done
  50.1 3.1 %fill.3 = (f32[16,96,128]{2,1,0:T(8,128)S(1)}, bf16[1024,2048]{1,0:T(8,128)(2,1)S(1)}, f32[16,8,128]{2,1,0:T(8,128)S(1)}, f32[14,32,128]{2,1,0:T(8,128)S(1)}, f3...) custom-call(bf16[192,1024]{1,0:T(8,128)(2,1)S(1)} %get-tuple-element, ...), custom_call_target="tpu_custom_call" | custom-call | tf_op jit(solution)/shard_map/fill/pallas_call | solution.py:53
  53.2 2.5 %collective-permute-done.refs_2_ = f32[96,128]{1,0:T(8,128)S(1)} collective-permute-done((f32[96,128]{1,0:T(8,128)S(1)}, f32[96,128]{1,0:T(8,128)S(1)}, u32[]{:S(2)}, u32[]{:S(2)}) %collective-permute-start) | collective-permute-done | bytes 49184 | tf_op jit(solution)/shard_map/ppermute | solution.py:621
  55.6 0.0 collective-permute-done.1.refs_3_
  55.6 0.0 collective-permute-done.2.refs_4_
  55.6 0.0 collective-permute-done.3.refs_5_
  55.6 1.9 %section.3 = (f32[2,96,384]{2,1,0:T(8,128)S(1)}, f32[16,96,128]{2,1,0:T(8,128)S(1)}, f32[64,1,1536]{2,1,0:T(1,128)S(1)}) custom-call(f32[2,96,384]{2,1,0:T(8,128)S(1)} %get-tuple-element.71.deck_ref.refs_0_.base_deck, f32[16,96,128]{2,1,0:T(8,128)S(1)} %get-tuple-element.74.refs_1_.base_back.refs_15_, f32[96,128]{1,0:T(8,128)S(1)} %collective-permute-done.refs_2_, ...), custom_call_target="tpu_custom_call" | custom-call | tf_op jit(solution)/shard_map/section/pallas_call | solution.py:53
  57.6 20.5 %all_to_all.22.got_ref = f32[64,1,1536]{2,1,0:T(1,128)S(1)} all-to-all(f32[64,1,1536]{2,1,0:T(1,128)S(1)} %get-tuple-element.89), channel_id=1, replica_groups=mesh['grid'=4,'gx'=8,'gy'=8] {'gy','gx'}, dimensions={0} | all-to-all | bytes 786432 | tf_op jit(solution)/shard_map/all_to_all | solution.py:544
  78.1 1.1 rim.4
  79.2 1.8 %collective-permute-start.6 = (f32[104,384]{1,0:T(8,128)S(1)}, f32[104,384]{1,0:T(8,128)S(1)}, u32[]{:S(2)}, u32[]{:S(2)}) collective-permute-start(f32[104,384]{1,0:T(8,128)S(1)} %get-tuple-element.98), channel_id=1, source_target_pairs={{1,2},{2,1},{3,4},{4,3},{5,6},{6,5},{7,8},{8,7},{9,10},{10,9},{11,... | collective-permute-start | bytes 479240 | tf_op jit(solution)/shard_map/ppermute | solution.py:619
  81.0 1.5 %collective-permute-start.7 = (f32[104,384]{1,0:T(8,128)S(1)}, f32[104,384]{1,0:T(8,128)S(1)}, u32[]{:S(2)}, u32[]{:S(2)}) collective-permute-start(f32[104,384]{1,0:T(8,128)S(1)} %get-tuple-element.99), channel_id=1, source_target_pairs={{0,1},{1,0},{2,3},{3,2},{4,5},{5,4},{6,7},{7,6},{8,9},{9,8},{10,11... | collective-permute-start | bytes 479240 | tf_op jit(solution)/shard_map/ppermute | solution.py:620
  82.5 0.0 collective-permute-start.4
  82.5 0.7 collective-permute-start.5
  83.2 1.6 %fill.4 = (f32[16,96,128]{2,1,0:T(8,128)S(1)}, f32[14,32,128]{2,1,0:T(8,128)S(1)}, f32[14,96,128]{2,1,0:T(8,128)S(1)}, f32[14,96,128]{2,1,0:T(8,128)S(1)}, f32[1...) custom-call(bf16[192,1024]{1,0:T(8,128)(2,1)S(1)} %get-tuple-element.9, ...), custom_call_target="tpu_custom_call" | custom-call | tf_op jit(solution)/shard_map/fill/pallas_call | solution.py:53
  84.8 3.9 %collective-permute-done.4.refs_2_ = f32[96,128]{1,0:T(8,128)S(1)} collective-permute-done((f32[96,128]{1,0:T(8,128)S(1)}, f32[96,128]{1,0:T(8,128)S(1)}, u32[]{:S(2)}, u32[]{:S(2)}) %collective-permute-start.4) | collective-permute-done | bytes 49184 | tf_op jit(solution)/shard_map/ppermute | solution.py:621
  88.7 0.0 collective-permute-done.5.refs_3_
  88.7 0.0 collective-permute-done.6.refs_4_
  88.7 0.0 collective-permute-done.7.refs_5_
  88.7 2.0 %section.4 = (f32[2,96,384]{2,1,0:T(8,128)S(1)}, f32[16,96,128]{2,1,0:T(8,128)S(1)}, f32[64,1,1536]{2,1,0:T(1,128)S(1)}) custom-call(f32[2,96,384]{2,1,0:T(8,128)S(1)} %get-tuple-element.92.deck_ref.refs_0_, f32[16,96,128]{2,1,0:T(8,128)S(1)} %get-tuple-element.95.refs_1_, f32[96,128]{1,0:T(8,128)S(1)} %collective-permute-done.4.refs_2_, ...), custom_call_target="tpu_custom_call" | custom-call | tf_op jit(solution)/shard_map/section/pallas_call | solution.py:53
  90.7 20.1 %all_to_all.23.got_ref = f32[64,1,1536]{2,1,0:T(1,128)S(1)} all-to-all(f32[64,1,1536]{2,1,0:T(1,128)S(1)} %get-tuple-element.107), channel_id=1, replica_groups=mesh['grid'=4,'gx'=8,'gy'=8] {'gy','gx'}, dimensions={0} | all-to-all | bytes 786432 | tf_op jit(solution)/shard_map/all_to_all | solution.py:544
  110.8 1.1 rim.5
  111.9 2.1 %collective-permute-start.10 = (f32[104,384]{1,0:T(8,128)S(1)}, f32[104,384]{1,0:T(8,128)S(1)}, u32[]{:S(2)}, u32[]{:S(2)}) collective-permute-start(f32[104,384]{1,0:T(8,128)S(1)} %get-tuple-element.115), channel_id=1, source_target_pairs={{1,2},{2,1},{3,4},{4,3},{5,6},{6,5},{7,8},{8,7},{9,10},{10,9},{11,... | collective-permute-start | bytes 479240 | tf_op jit(solution)/shard_map/ppermute | solution.py:619
  114.0 1.3 %collective-permute-start.11 = (f32[104,384]{1,0:T(8,128)S(1)}, f32[104,384]{1,0:T(8,128)S(1)}, u32[]{:S(2)}, u32[]{:S(2)}) collective-permute-start(f32[104,384]{1,0:T(8,128)S(1)} %get-tuple-element.116), channel_id=1, source_target_pairs={{0,1},{1,0},{2,3},{3,2},{4,5},{5,4},{6,7},{7,6},{8,9},{9,8},{10,11... | collective-permute-start | bytes 479240 | tf_op jit(solution)/shard_map/ppermute | solution.py:620
  115.2 0.0 collective-permute-start.8
  115.2 0.6 collective-permute-start.9
  115.9 1.7 %fill.5 = (f32[16,96,128]{2,1,0:T(8,128)S(1)}, f32[14,32,128]{2,1,0:T(8,128)S(1)}, f32[14,96,128]{2,1,0:T(8,128)S(1)}, f32[14,96,128]{2,1,0:T(8,128)S(1)}, f32[1...) custom-call(bf16[192,1024]{1,0:T(8,128)(2,1)S(1)} %get-tuple-element.1, ...), custom_call_target="tpu_custom_call" | custom-call | tf_op jit(solution)/shard_map/fill/pallas_call | solution.py:53
  117.6 3.9 %collective-permute-done.8.refs_2_ = f32[96,128]{1,0:T(8,128)S(1)} collective-permute-done((f32[96,128]{1,0:T(8,128)S(1)}, f32[96,128]{1,0:T(8,128)S(1)}, u32[]{:S(2)}, u32[]{:S(2)}) %collective-permute-start.8) | collective-permute-done | bytes 49184 | tf_op jit(solution)/shard_map/ppermute | solution.py:621
  121.5 0.0 collective-permute-done.9.refs_3_
  121.5 0.0 collective-permute-done.10.refs_4_
  121.5 0.0 collective-permute-done.11.refs_5_
  121.5 1.8 %section.5 = (f32[96,2,384]{2,1,0:T(2,128)}, f32[96,16,128]{2,1,0:T(8,128)}) custom-call(f32[2,96,384]{2,1,0:T(8,128)S(1)} %get-tuple-element.110.deck_ref.refs_0_, f32[16,96,128]{2,1,0:T(8,128)S(1)} %get-tuple-element.112.refs_1_, f32[96,128]{1,0:T(8,128)S(1)} %collective-permute-done.8.refs_2_, f32[96,128]{1,0:T(8,128)S(1)} %collective-permute-done.9.refs_3_, ...), custom_call_target="tpu_custom_call" | custom-call | tf_op jit(solution)/shard_map/section/pallas_call | solution.py:53
Async XLA Ops:
  0.6 49.5 %copy-start = (f32[4,2,384]{2,1,0:T(2,128)S(1)}, f32[4,2,384]{2,1,0:T(2,128)}, u32[]{:S(2)}) copy-start(f32[4,2,384]{2,1,0:T(2,128)} %refs_6_.5) | copy-start | bytes 36868
  46.1 9.5 %collective-permute-start.2 = (f32[104,384]{1,0:T(8,128)S(1)}, f32[104,384]{1,0:T(8,128)S(1)}, u32[]{:S(2)}, u32[]{:S(2)}) collective-permute-start(f32[104,384]{1,0:T(8,128)S(1)} %get-tuple-element.77), channel_id=1, source_target_pairs={{1,2},{2,1},{3,4},{4,3},{5,6},{6,5},{7,8},{8,7},{9,10},{10,9},{11,... | collective-permute-start | bytes 479240 | tf_op jit(solution)/shard_map/ppermute | solution.py:619
  47.9 7.8 %collective-permute-start.3 = (f32[104,384]{1,0:T(8,128)S(1)}, f32[104,384]{1,0:T(8,128)S(1)}, u32[]{:S(2)}, u32[]{:S(2)}) collective-permute-start(f32[104,384]{1,0:T(8,128)S(1)} %get-tuple-element.78), channel_id=1, source_target_pairs={{0,1},{1,0},{2,3},{3,2},{4,5},{5,4},{6,7},{7,6},{8,9},{9,8},{10,11... | collective-permute-start | bytes 479240 | tf_op jit(solution)/shard_map/ppermute | solution.py:620
  49.4 6.2 %collective-permute-start = (f32[96,128]{1,0:T(8,128)S(1)}, f32[96,128]{1,0:T(8,128)S(1)}, u32[]{:S(2)}, u32[]{:S(2)}) collective-permute-start(f32[96,128]{1,0:T(8,128)S(1)} %get-tuple-element.75), channel_id=1, source_target_pairs={{8,16},{16,8},{9,17},{17,9},{10,18},{18,10},{11,19},{19,11},{12,20... | collective-permute-start | bytes 147464 | tf_op jit(solution)/shard_map/ppermute | solution.py:621
  49.4 6.2 %collective-permute-start.1 = (f32[96,128]{1,0:T(8,128)S(1)}, f32[96,128]{1,0:T(8,128)S(1)}, u32[]{:S(2)}, u32[]{:S(2)}) collective-permute-start(f32[96,128]{1,0:T(8,128)S(1)} %get-tuple-element.76), channel_id=1, source_target_pairs={{0,8},{8,0},{1,9},{9,1},{2,10},{10,2},{3,11},{11,3},{4,12},{12,4},... | collective-permute-start | bytes 147464 | tf_op jit(solution)/shard_map/ppermute | solution.py:622
  79.2 9.5 %collective-permute-start.6 = (f32[104,384]{1,0:T(8,128)S(1)}, f32[104,384]{1,0:T(8,128)S(1)}, u32[]{:S(2)}, u32[]{:S(2)}) collective-permute-start(f32[104,384]{1,0:T(8,128)S(1)} %get-tuple-element.98), channel_id=1, source_target_pairs={{1,2},{2,1},{3,4},{4,3},{5,6},{6,5},{7,8},{8,7},{9,10},{10,9},{11,... | collective-permute-start | bytes 479240 | tf_op jit(solution)/shard_map/ppermute | solution.py:619
  81.0 7.7 %collective-permute-start.7 = (f32[104,384]{1,0:T(8,128)S(1)}, f32[104,384]{1,0:T(8,128)S(1)}, u32[]{:S(2)}, u32[]{:S(2)}) collective-permute-start(f32[104,384]{1,0:T(8,128)S(1)} %get-tuple-element.99), channel_id=1, source_target_pairs={{0,1},{1,0},{2,3},{3,2},{4,5},{5,4},{6,7},{7,6},{8,9},{9,8},{10,11... | collective-permute-start | bytes 479240 | tf_op jit(solution)/shard_map/ppermute | solution.py:620
  82.5 6.2 %collective-permute-start.4 = (f32[96,128]{1,0:T(8,128)S(1)}, f32[96,128]{1,0:T(8,128)S(1)}, u32[]{:S(2)}, u32[]{:S(2)}) collective-permute-start(f32[96,128]{1,0:T(8,128)S(1)} %get-tuple-element.96), channel_id=1, source_target_pairs={{8,16},{16,8},{9,17},{17,9},{10,18},{18,10},{11,19},{19,11},{12,20... | collective-permute-start | bytes 147464 | tf_op jit(solution)/shard_map/ppermute | solution.py:621
  82.5 6.2 %collective-permute-start.5 = (f32[96,128]{1,0:T(8,128)S(1)}, f32[96,128]{1,0:T(8,128)S(1)}, u32[]{:S(2)}, u32[]{:S(2)}) collective-permute-start(f32[96,128]{1,0:T(8,128)S(1)} %get-tuple-element.97), channel_id=1, source_target_pairs={{0,8},{8,0},{1,9},{9,1},{2,10},{10,2},{3,11},{11,3},{4,12},{12,4},... | collective-permute-start | bytes 147464 | tf_op jit(solution)/shard_map/ppermute | solution.py:622
  111.9 9.6 %collective-permute-start.10 = (f32[104,384]{1,0:T(8,128)S(1)}, f32[104,384]{1,0:T(8,128)S(1)}, u32[]{:S(2)}, u32[]{:S(2)}) collective-permute-start(f32[104,384]{1,0:T(8,128)S(1)} %get-tuple-element.115), channel_id=1, source_target_pairs={{1,2},{2,1},{3,4},{4,3},{5,6},{6,5},{7,8},{8,7},{9,10},{10,9},{11,... | collective-permute-start | bytes 479240 | tf_op jit(solution)/shard_map/ppermute | solution.py:619
  114.0 7.6 %collective-permute-start.11 = (f32[104,384]{1,0:T(8,128)S(1)}, f32[104,384]{1,0:T(8,128)S(1)}, u32[]{:S(2)}, u32[]{:S(2)}) collective-permute-start(f32[104,384]{1,0:T(8,128)S(1)} %get-tuple-element.116), channel_id=1, source_target_pairs={{0,1},{1,0},{2,3},{3,2},{4,5},{5,4},{6,7},{7,6},{8,9},{9,8},{10,11... | collective-permute-start | bytes 479240 | tf_op jit(solution)/shard_map/ppermute | solution.py:620
  115.2 6.3 %collective-permute-start.8 = (f32[96,128]{1,0:T(8,128)S(1)}, f32[96,128]{1,0:T(8,128)S(1)}, u32[]{:S(2)}, u32[]{:S(2)}) collective-permute-start(f32[96,128]{1,0:T(8,128)S(1)} %get-tuple-element.113), channel_id=1, source_target_pairs={{8,16},{16,8},{9,17},{17,9},{10,18},{18,10},{11,19},{19,11},{12,20... | collective-permute-start | bytes 147464 | tf_op jit(solution)/shard_map/ppermute | solution.py:621
  115.2 6.3 %collective-permute-start.9 = (f32[96,128]{1,0:T(8,128)S(1)}, f32[96,128]{1,0:T(8,128)S(1)}, u32[]{:S(2)}, u32[]{:S(2)}) collective-permute-start(f32[96,128]{1,0:T(8,128)S(1)} %get-tuple-element.114), channel_id=1, source_target_pairs={{0,8},{8,0},{1,9},{9,1},{2,10},{10,2},{3,11},{11,3},{4,12},{12,4},... | collective-permute-start | bytes 147464 | tf_op jit(solution)/shard_map/ppermute | solution.py:622
